TPU v7x, 512 devices: a whole 4x4x16 slice. The times are simulated.
512 devices in a mesh: seq: 64 (over z_lo, x, core), head: 8 (over z_hi, y).
Axes of the slice: x: 4, y: 4, z: 16 (z_hi: 2, z_lo: 8; z = z_hi * 8 + z_lo), core: 2. Of those that a mesh axis runs over, the one named last changes fastest.
Arguments:
- query_nope: bfloat16 [8192, 64, 128], P('seq', 'head'), may hold values from -16 to 16
- query_rotary: bfloat16 [8192, 4096], P('seq', 'head'), may hold values from -12 to 12
- latent: bfloat16 [8192, 512], P('seq'), may hold values from -6 to 6
- rotary_keys: bfloat16 [8192, 64], P('seq'), may hold values from -6 to 6
- output_grad: bfloat16 [8192, 64, 512], P('seq', 'head'), may hold values from -0.3125 to 0.3125
- weight_codes: int32 [128, 64, 512], P('seq', 'head'), may hold values from -128 to 127
- weight_scale: float32 [128, 64], P('seq', 'head'), may hold values from 0.0005 to 0.002
- positions: int32 [8192], P('seq'), may hold values from 0 to 1023, as said below
Outputs:
- query_grad: bfloat16 [8192, 64, 128], P('seq', 'head')
- rotary_grad: bfloat16 [8192, 4096], P('seq', 'head')
- latent_grad: float32 [8192, 512], P('seq')
- keys_grad: float32 [8192, 64], P('seq')
- master_grad: float32 [128, 64, 512], P('seq', 'head')
Inputs may be any that keep to these rules, and one draw needn't show every extreme that they name: Each device's tokens form two aligned runs of 64 consecutive positions, each starting at a multiple of 64; the two run numbers (start divided by 64) of a device add up to 15; every position of a document occurs exactly once.
All inputs are finite; a program needn't handle non-finite values.
Results may differ from a plain program's by a relative error of at most 0.017.
Values may be sent and summed in bfloat16 or wider, within the bound.
No kernel may reach another device: no remote copies, remote signals or barrier semaphores. Data moves between devices by JAX's collectives and lax.ppermute only.
A program may use at most 64 MiB of HBM per device.

v0:
```python
from functools import partial
import math

import jax
import jax.numpy as jnp
from jax import lax
from jax.sharding import PartitionSpec as P

DOCS = 8


MASKED = -1e30


def from_behind(block, axis, distance):
    devices = range(lax.axis_size(axis))
    route = [((i - distance) % len(devices), i) for i in devices]
    return lax.ppermute(block, axis, route)


def dequant(codes, scales):
    four_bit = 16 * jnp.floor_divide(codes, 16) + 8
    two_bit = 64 * jnp.floor_divide(codes, 64) + 32
    levels = (codes + four_bit + two_bit).astype(jnp.float32)
    return (scales[:, :, None] * levels / 3.0).astype(jnp.bfloat16)


def unchanged(running):
    return running


def shards(
    query_nope,
    query_rotary,
    latent,
    rotary_keys,
    output_grad,
    weight_codes,
    weight_scale,
    positions,
):
    tokens, head_count, nope_width = query_nope.shape
    latent_width = latent.shape[1]
    rotary = rotary_keys.shape[1]
    half_size = tokens // 2
    row_count = half_size * head_count
    groups = lax.axis_size("seq") // DOCS
    factor = 1.0 / math.sqrt(nope_width + rotary)
    weight = lax.all_gather(dequant(weight_codes, weight_scale), "seq", axis=0, tiled=True)
    absorbed = jnp.einsum(
        "thn,nhc->thc", query_nope, weight, preferred_element_type=jnp.float32
    ).astype(jnp.bfloat16)
    absorbed_rows = absorbed.reshape(2, row_count, latent_width)
    rotary_rows = query_rotary.reshape(2, row_count, rotary)
    upstream_rows = output_grad.reshape(2, row_count, latent_width)
    query_place = positions.reshape(2, half_size)
    query_index = query_place[:, 0] // half_size
    place_rows = jnp.repeat(query_place, head_count, axis=1)
    offsets = jnp.arange(half_size, dtype=jnp.int32)

    def scores_of(query_half, key_part, rot_part, key_index):
        direct = jnp.einsum(
            "kc,rc->kr", key_part, absorbed_rows[query_half], preferred_element_type=jnp.float32
        )
        turned = jnp.einsum(
            "kd,rd->kr", rot_part, rotary_rows[query_half], preferred_element_type=jnp.float32
        )
        scores = factor * (direct + turned)
        key_place = key_index * half_size + offsets
        visible = key_place[:, None] <= place_rows[query_half][None, :]
        return jnp.where(visible, scores, MASKED)

    def stats_update(query_half, key_part, rot_part, key_index, running):
        maxima, totals, weighted = running
        scores = scores_of(query_half, key_part, rot_part, key_index)
        slopes = jnp.einsum(
            "kc,rc->kr", key_part, upstream_rows[query_half], preferred_element_type=jnp.float32
        )
        new_max = jnp.maximum(maxima, jnp.max(scores, axis=0))
        rescale = jnp.exp(maxima - new_max)
        softmax = jnp.exp(scores - new_max[None, :])
        return (
            new_max,
            totals * rescale + jnp.sum(softmax, axis=0),
            weighted * rescale + jnp.sum(softmax * slopes, axis=0),
        )

    def stats_step(moving, statistics):
        key_latent, key_rotary, key_block = moving
        key_index = key_block.astype(jnp.int32)
        result = []
        for query_half in range(2):
            current = tuple((member[query_half] for member in statistics))
            for key_half in range(2):
                key_part = key_latent[key_half * half_size : (key_half + 1) * half_size]
                rot_part = key_rotary[key_half * half_size : (key_half + 1) * half_size]
                update = partial(stats_update, query_half, key_part, rot_part, key_index[key_half])
                current = lax.cond(
                    key_index[key_half] <= query_index[query_half], update, unchanged, current
                )
            result.append(current)
        return tuple((jnp.stack([result[0][member], result[1][member]]) for member in range(3)))

    def keep_block(buffers, moving, turn_index):
        return tuple(
            (
                lax.dynamic_update_index_in_dim(buffer, member, turn_index, 0)
                for buffer, member in zip(buffers, moving)
            )
        )

    moving = (latent, rotary_keys, query_index.astype(jnp.bfloat16))
    statistics = (
        jnp.full((2, row_count), MASKED, jnp.float32),
        jnp.zeros((2, row_count), jnp.float32),
        jnp.zeros((2, row_count), jnp.float32),
    )
    buffers = tuple((jnp.zeros((groups,) + member.shape, member.dtype) for member in moving))

    def first_turn(turn_index, running):
        moving, statistics, buffers = running
        statistics = stats_step(moving, statistics)
        buffers = keep_block(buffers, moving, turn_index)
        moving = from_behind((moving[0], moving[1], moving[2]), "seq", DOCS)
        return (moving, statistics, buffers)

    moving, statistics, buffers = lax.fori_loop(
        0, groups - 1, first_turn, (moving, statistics, buffers)
    )
    statistics = stats_step(moving, statistics)
    buffers = keep_block(buffers, moving, groups - 1)
    log_total = statistics[0] + jnp.log(statistics[1])
    inner_sum = statistics[2] / statistics[1]

    def grads_update(query_half, key_part, rot_part, key_index, running):
        query_sum, rotary_sum, key_sum, keyrot_sum = running
        scores = scores_of(query_half, key_part, rot_part, key_index)
        softmax = jnp.exp(scores - log_total[query_half][None, :])
        slopes = jnp.einsum(
            "kc,rc->kr", key_part, upstream_rows[query_half], preferred_element_type=jnp.float32
        )
        score_grad = (softmax * (slopes - inner_sum[query_half][None, :]) * factor).astype(
            jnp.bfloat16
        )
        softmax_low = softmax.astype(jnp.bfloat16)
        query_sum = query_sum + jnp.einsum(
            "kr,kc->rc", score_grad, key_part, preferred_element_type=jnp.float32
        )
        rotary_sum = rotary_sum + jnp.einsum(
            "kr,kd->rd", score_grad, rot_part, preferred_element_type=jnp.float32
        )
        key_sum = key_sum + jnp.einsum(
            "kr,rc->kc", score_grad, absorbed_rows[query_half], preferred_element_type=jnp.float32
        )
        key_sum = key_sum + jnp.einsum(
            "kr,rc->kc", softmax_low, upstream_rows[query_half], preferred_element_type=jnp.float32
        )
        keyrot_sum = keyrot_sum + jnp.einsum(
            "kr,rd->kd", score_grad, rotary_rows[query_half], preferred_element_type=jnp.float32
        )
        return (query_sum, rotary_sum, key_sum, keyrot_sum)

    def grads_step(turn_index, running):
        query_sums, rotary_sums, carried, carried_rot = running
        key_latent = lax.dynamic_index_in_dim(buffers[0], turn_index, 0, keepdims=False)
        key_rotary = lax.dynamic_index_in_dim(buffers[1], turn_index, 0, keepdims=False)
        key_index = lax.dynamic_index_in_dim(buffers[2], turn_index, 0, keepdims=False).astype(
            jnp.int32
        )
        key_sums = [jnp.zeros((half_size, latent_width), jnp.float32) for member in range(2)]
        keyrot_sums = [jnp.zeros((half_size, rotary), jnp.float32) for member in range(2)]
        new_query = []
        new_rotary = []
        for query_half in range(2):
            current = (query_sums[query_half], rotary_sums[query_half])
            for key_half in range(2):
                key_part = key_latent[key_half * half_size : (key_half + 1) * half_size]
                rot_part = key_rotary[key_half * half_size : (key_half + 1) * half_size]
                update = partial(grads_update, query_half, key_part, rot_part, key_index[key_half])
                outcome = lax.cond(
                    key_index[key_half] <= query_index[query_half],
                    update,
                    unchanged,
                    current + (key_sums[key_half], keyrot_sums[key_half]),
                )
                current = outcome[:2]
                key_sums[key_half] = outcome[2]
                keyrot_sums[key_half] = outcome[3]
            new_query.append(current[0])
            new_rotary.append(current[1])
        pieces = (jnp.concatenate(key_sums, axis=0), jnp.concatenate(keyrot_sums, axis=0))
        carried, carried_rot = from_behind(
            (carried + pieces[0], carried_rot + pieces[1]), "seq", DOCS
        )
        return (jnp.stack(new_query), jnp.stack(new_rotary), carried, carried_rot)

    initial = (
        jnp.zeros((2, row_count, latent_width), jnp.float32),
        jnp.zeros((2, row_count, rotary), jnp.float32),
        jnp.zeros((tokens, latent_width), jnp.float32),
        jnp.zeros((tokens, rotary), jnp.float32),
    )
    query_sums, rotary_sums, carried, carried_rot = lax.fori_loop(0, groups, grads_step, initial)
    latent_grad, keys_grad = (
        lax.psum(carried.astype(jnp.bfloat16), "head").astype(jnp.float32),
        lax.psum(carried_rot.astype(jnp.bfloat16), "head").astype(jnp.float32),
    )
    dq_latent = query_sums.reshape(tokens, head_count, latent_width).astype(jnp.bfloat16)
    rotary_grad = rotary_sums.reshape(tokens, head_count * rotary).astype(jnp.bfloat16)
    query_grad = jnp.einsum(
        "thc,nhc->thn", dq_latent, weight, preferred_element_type=jnp.float32
    ).astype(jnp.bfloat16)
    master_grad = lax.psum_scatter(
        jnp.einsum("thn,thc->nhc", query_nope, dq_latent, preferred_element_type=jnp.float32),
        "seq",
        scatter_dimension=0,
        tiled=True,
    )
    return (query_grad, rotary_grad, latent_grad, keys_grad, master_grad)


def solution(mesh):
    in_specs = (
        P("seq", "head", None),
        P("seq", "head"),
        P("seq", None),
        P("seq", None),
        P("seq", "head", None),
        P("seq", "head", None),
        P("seq", "head"),
        P("seq"),
    )
    out_specs = (
        P("seq", "head", None),
        P("seq", "head"),
        P("seq", None),
        P("seq", None),
        P("seq", "head", None),
    )
    return jax.shard_map(shards, mesh=mesh, in_specs=in_specs, out_specs=out_specs, check_vma=False)
```

profile of v0, /device:TPU:8, one launch (start us, length us, event | category | flops | bytes accessed | tf_op | source)
XLA Modules:
  0.0 1467.1 jit_solution(14792197099869719092)
XLA Ops:
  15.6 118.8 %all-gather.2.cloned.1.call-done = bf16[128,8,512]{2,1,0:T(8,128)(2,1)} async-done(((bf16[2,8,512]{2,1,0:T(8,128)(2,1)}), bf16[128,8,512]{2,1,0:T(8,128)(2,1)}) %all-gather.2.cloned.1.call-update) | async-done | bytes 1048592 | tf_op jit(solution)/shard_map/all_gather | solution.py:49
  139.5 223.3 %while.52 = (s32[]{:T(128)}, bf16[128,512]{1,0:T(8,128)(2,1)S(1)}, bf16[128,64]{1,0:T(8,128)(2,1)S(1)}, bf16[2]{0:T(256)(128)(2,1)S(1)}, f32[2,512]{1,0:T(2,128)...) while((s32[]{:T(128)}, bf16[128,512]{1,0:T(8,128)(2,1)S(1)}, ...), condition=%wide.region_21.22_spmd.clone.clone, body=%wide.region_0.21_spmd.clone.clone.sunk | while | flops 286532864 | bytes 9660149 | solution.py:127
  300.5 6.0 collective-permute-start.1
  385.0 487.0 %while.53 = (s32[]{:T(128)}, f32[2,512,512]{2,1,0:T(8,128)}, f32[2,512,64]{1,2,0:T(8,128)S(1)}, f32[128,512]{1,0:T(8,128)}, f32[128,64]{1,0:T(8,128)}, /*index=5...) while((s32[]{:T(128)}, f32[2,512,512]{2,1,0:T(8,128)}, ...), condition=%wide.region_51.52_spmd.clone.clone, body=%wide.region_42.51_spmd.clone.clone.sunk | while | flops 724852992 | bytes 38610920 | solution.py:203
  400.9 12.7 conditional.44
  413.6 10.6 conditional.46
  425.5 9.9 conditional.47
  472.8 10.6 conditional.46
  484.8 9.9 conditional.47
  532.1 10.6 conditional.46
  544.0 9.9 conditional.47
  591.3 10.6 conditional.46
  603.2 9.9 conditional.47
  649.3 12.7 conditional.44
  662.0 10.6 conditional.46
  711.4 10.6 conditional.46
  723.3 9.9 conditional.47
  770.6 10.6 conditional.46
  782.5 9.9 conditional.47
  829.9 10.6 conditional.46
  841.8 9.9 conditional.47
  882.2 61.5 %psum.15 = bf16[128,64]{0,1:T(8,128)(2,1)S(1)} all-reduce(bf16[128,64]{0,1:T(8,128)(2,1)S(1)} %copy.57), channel_id=1, replica_groups=mesh['seq'=64,'head'=8] {'head'}, use_global_device_ids=true, to_apply=%region_53.54 | all-reduce | flops 8192 | bytes 32768 | tf_op jit(solution)/shard_map/psum | solution.py:206
  947.0 70.0 %all-reduce.2.cloned.1.call-done = bf16[128,512]{1,0:T(8,128)(2,1)} async-done(((bf16[128,512]{1,0:T(8,128)(2,1)}), bf16[128,512]{1,0:T(8,128)(2,1)}) %all-reduce.2.cloned.1.call-update) | async-done | bytes 131088 | tf_op jit(solution)/shard_map/psum | solution.py:205
  1018.6 442.0 %reduce-scatter.2.cloned.1.call-done = f32[2,8,512]{2,1,0:T(8,128)} async-done(((f32[128,8,512]{2,1,0:T(8,128)}), f32[2,8,512]{2,1,0:T(8,128)}) %reduce-scatter.2.cloned.1.call-update) | async-done | bytes 32784 | tf_op jit(solution)/shard_map/reduce_scatter | solution.py:213
  (885 shorter events, 731.4 us)
Async XLA Ops:
  7.2 127.2 %all-gather.2.cloned.1.call-start = ((), (), s32[]{:S(2)}) async-start(), calls=%async_computation.1 | async-start | bytes 1064960 | tf_op jit(solution)/shard_map/all_gather | solution.py:49
  8.7 1008.3 %all-reduce.2.cloned.1.call-start = ((), (), s32[]{:S(2)}) async-start(), calls=%async_computation.2 | async-start | bytes 262144 | tf_op jit(solution)/shard_map/psum | solution.py:205
  139.5 34.3 %collective-permute-start.2 = (bf16[2]{0:T(256)(128)(2,1)S(1)}, bf16[2]{0:T(256)(128)(2,1)S(1)}, u32[]{:S(2)}, u32[]{:S(2)}) collective-permute-start(bf16[2]{0:T(256)(128)(2,1)S(1)} %copy.146), channel_id=1, source_target_pairs={{448,0},{456,8},{464,16},{472,24},{480,32},{488,40},{496,48},{504,... | collective-permute-start | bytes 20 | tf_op jit(solution)/shard_map/while/body/eval_jaxpr/ppermute | solution.py:18
  142.9 30.9 %collective-permute-start.1 = (bf16[128,64]{1,0:T(8,128)(2,1)S(1)}, bf16[128,64]{1,0:T(8,128)(2,1)S(1)}, u32[]{:S(2)}, u32[]{:S(2)}) collective-permute-start(bf16[128,64]{1,0:T(8,128)(2,1)S(1)} %copy.145), channel_id=1, source_target_pairs={{448,0},{456,8},{464,16},{472,24},{480,32},{488,40},{496,48},{504,... | collective-permute-start | bytes 49160 | tf_op jit(solution)/shard_map/while/body/eval_jaxpr/ppermute | solution.py:18
  146.3 27.5 %collective-permute-start = (bf16[128,512]{1,0:T(8,128)(2,1)S(1)}, bf16[128,512]{1,0:T(8,128)(2,1)S(1)}, u32[]{:S(2)}, u32[]{:S(2)}) collective-permute-start(bf16[128,512]{1,0:T(8,128)(2,1)S(1)} %copy.144), channel_id=1, source_target_pairs={{448,0},{456,8},{464,16},{472,24},{480,32},{488,40},{496,48},{504,... | collective-permute-start | bytes 393224 | tf_op jit(solution)/shard_map/while/body/eval_jaxpr/ppermute | solution.py:18
  173.8 29.9 %collective-permute-start.2 = (bf16[2]{0:T(256)(128)(2,1)S(1)}, bf16[2]{0:T(256)(128)(2,1)S(1)}, u32[]{:S(2)}, u32[]{:S(2)}) collective-permute-start(bf16[2]{0:T(256)(128)(2,1)S(1)} %copy.146), channel_id=1, source_target_pairs={{448,0},{456,8},{464,16},{472,24},{480,32},{488,40},{496,48},{504,... | collective-permute-start | bytes 20 | tf_op jit(solution)/shard_map/while/body/eval_jaxpr/ppermute | solution.py:18
  177.7 26.0 %collective-permute-start.1 = (bf16[128,64]{1,0:T(8,128)(2,1)S(1)}, bf16[128,64]{1,0:T(8,128)(2,1)S(1)}, u32[]{:S(2)}, u32[]{:S(2)}) collective-permute-start(bf16[128,64]{1,0:T(8,128)(2,1)S(1)} %copy.145), channel_id=1, source_target_pairs={{448,0},{456,8},{464,16},{472,24},{480,32},{488,40},{496,48},{504,... | collective-permute-start | bytes 49160 | tf_op jit(solution)/shard_map/while/body/eval_jaxpr/ppermute | solution.py:18
  180.9 22.9 %collective-permute-start = (bf16[128,512]{1,0:T(8,128)(2,1)S(1)}, bf16[128,512]{1,0:T(8,128)(2,1)S(1)}, u32[]{:S(2)}, u32[]{:S(2)}) collective-permute-start(bf16[128,512]{1,0:T(8,128)(2,1)S(1)} %copy.144), channel_id=1, source_target_pairs={{448,0},{456,8},{464,16},{472,24},{480,32},{488,40},{496,48},{504,... | collective-permute-start | bytes 393224 | tf_op jit(solution)/shard_map/while/body/eval_jaxpr/ppermute | solution.py:18
  203.7 33.4 %collective-permute-start.2 = (bf16[2]{0:T(256)(128)(2,1)S(1)}, bf16[2]{0:T(256)(128)(2,1)S(1)}, u32[]{:S(2)}, u32[]{:S(2)}) collective-permute-start(bf16[2]{0:T(256)(128)(2,1)S(1)} %copy.146), channel_id=1, source_target_pairs={{448,0},{456,8},{464,16},{472,24},{480,32},{488,40},{496,48},{504,... | collective-permute-start | bytes 20 | tf_op jit(solution)/shard_map/while/body/eval_jaxpr/ppermute | solution.py:18
  205.7 31.5 %collective-permute-start.1 = (bf16[128,64]{1,0:T(8,128)(2,1)S(1)}, bf16[128,64]{1,0:T(8,128)(2,1)S(1)}, u32[]{:S(2)}, u32[]{:S(2)}) collective-permute-start(bf16[128,64]{1,0:T(8,128)(2,1)S(1)} %copy.145), channel_id=1, source_target_pairs={{448,0},{456,8},{464,16},{472,24},{480,32},{488,40},{496,48},{504,... | collective-permute-start | bytes 49160 | tf_op jit(solution)/shard_map/while/body/eval_jaxpr/ppermute | solution.py:18
  211.6 25.6 %collective-permute-start = (bf16[128,512]{1,0:T(8,128)(2,1)S(1)}, bf16[128,512]{1,0:T(8,128)(2,1)S(1)}, u32[]{:S(2)}, u32[]{:S(2)}) collective-permute-start(bf16[128,512]{1,0:T(8,128)(2,1)S(1)} %copy.144), channel_id=1, source_target_pairs={{448,0},{456,8},{464,16},{472,24},{480,32},{488,40},{496,48},{504,... | collective-permute-start | bytes 393224 | tf_op jit(solution)/shard_map/while/body/eval_jaxpr/ppermute | solution.py:18
  237.2 30.1 %collective-permute-start.2 = (bf16[2]{0:T(256)(128)(2,1)S(1)}, bf16[2]{0:T(256)(128)(2,1)S(1)}, u32[]{:S(2)}, u32[]{:S(2)}) collective-permute-start(bf16[2]{0:T(256)(128)(2,1)S(1)} %copy.146), channel_id=1, source_target_pairs={{448,0},{456,8},{464,16},{472,24},{480,32},{488,40},{496,48},{504,... | collective-permute-start | bytes 20 | tf_op jit(solution)/shard_map/while/body/eval_jaxpr/ppermute | solution.py:18
  240.0 27.3 %collective-permute-start.1 = (bf16[128,64]{1,0:T(8,128)(2,1)S(1)}, bf16[128,64]{1,0:T(8,128)(2,1)S(1)}, u32[]{:S(2)}, u32[]{:S(2)}) collective-permute-start(bf16[128,64]{1,0:T(8,128)(2,1)S(1)} %copy.145), channel_id=1, source_target_pairs={{448,0},{456,8},{464,16},{472,24},{480,32},{488,40},{496,48},{504,... | collective-permute-start | bytes 49160 | tf_op jit(solution)/shard_map/while/body/eval_jaxpr/ppermute | solution.py:18
  241.9 25.4 %collective-permute-start = (bf16[128,512]{1,0:T(8,128)(2,1)S(1)}, bf16[128,512]{1,0:T(8,128)(2,1)S(1)}, u32[]{:S(2)}, u32[]{:S(2)}) collective-permute-start(bf16[128,512]{1,0:T(8,128)(2,1)S(1)} %copy.144), channel_id=1, source_target_pairs={{448,0},{456,8},{464,16},{472,24},{480,32},{488,40},{496,48},{504,... | collective-permute-start | bytes 393224 | tf_op jit(solution)/shard_map/while/body/eval_jaxpr/ppermute | solution.py:18
  267.3 28.6 %collective-permute-start.2 = (bf16[2]{0:T(256)(128)(2,1)S(1)}, bf16[2]{0:T(256)(128)(2,1)S(1)}, u32[]{:S(2)}, u32[]{:S(2)}) collective-permute-start(bf16[2]{0:T(256)(128)(2,1)S(1)} %copy.146), channel_id=1, source_target_pairs={{448,0},{456,8},{464,16},{472,24},{480,32},{488,40},{496,48},{504,... | collective-permute-start | bytes 20 | tf_op jit(solution)/shard_map/while/body/eval_jaxpr/ppermute | solution.py:18
  271.8 24.1 %collective-permute-start.1 = (bf16[128,64]{1,0:T(8,128)(2,1)S(1)}, bf16[128,64]{1,0:T(8,128)(2,1)S(1)}, u32[]{:S(2)}, u32[]{:S(2)}) collective-permute-start(bf16[128,64]{1,0:T(8,128)(2,1)S(1)} %copy.145), channel_id=1, source_target_pairs={{448,0},{456,8},{464,16},{472,24},{480,32},{488,40},{496,48},{504,... | collective-permute-start | bytes 49160 | tf_op jit(solution)/shard_map/while/body/eval_jaxpr/ppermute | solution.py:18
  273.8 22.2 %collective-permute-start = (bf16[128,512]{1,0:T(8,128)(2,1)S(1)}, bf16[128,512]{1,0:T(8,128)(2,1)S(1)}, u32[]{:S(2)}, u32[]{:S(2)}) collective-permute-start(bf16[128,512]{1,0:T(8,128)(2,1)S(1)} %copy.144), channel_id=1, source_target_pairs={{448,0},{456,8},{464,16},{472,24},{480,32},{488,40},{496,48},{504,... | collective-permute-start | bytes 393224 | tf_op jit(solution)/shard_map/while/body/eval_jaxpr/ppermute | solution.py:18
  296.0 33.6 %collective-permute-start.2 = (bf16[2]{0:T(256)(128)(2,1)S(1)}, bf16[2]{0:T(256)(128)(2,1)S(1)}, u32[]{:S(2)}, u32[]{:S(2)}) collective-permute-start(bf16[2]{0:T(256)(128)(2,1)S(1)} %copy.146), channel_id=1, source_target_pairs={{448,0},{456,8},{464,16},{472,24},{480,32},{488,40},{496,48},{504,... | collective-permute-start | bytes 20 | tf_op jit(solution)/shard_map/while/body/eval_jaxpr/ppermute | solution.py:18
  300.5 29.0 %collective-permute-start.1 = (bf16[128,64]{1,0:T(8,128)(2,1)S(1)}, bf16[128,64]{1,0:T(8,128)(2,1)S(1)}, u32[]{:S(2)}, u32[]{:S(2)}) collective-permute-start(bf16[128,64]{1,0:T(8,128)(2,1)S(1)} %copy.145), channel_id=1, source_target_pairs={{448,0},{456,8},{464,16},{472,24},{480,32},{488,40},{496,48},{504,... | collective-permute-start | bytes 49160 | tf_op jit(solution)/shard_map/while/body/eval_jaxpr/ppermute | solution.py:18
  306.6 23.0 %collective-permute-start = (bf16[128,512]{1,0:T(8,128)(2,1)S(1)}, bf16[128,512]{1,0:T(8,128)(2,1)S(1)}, u32[]{:S(2)}, u32[]{:S(2)}) collective-permute-start(bf16[128,512]{1,0:T(8,128)(2,1)S(1)} %copy.144), channel_id=1, source_target_pairs={{448,0},{456,8},{464,16},{472,24},{480,32},{488,40},{496,48},{504,... | collective-permute-start | bytes 393224 | tf_op jit(solution)/shard_map/while/body/eval_jaxpr/ppermute | solution.py:18
  329.6 33.2 %collective-permute-start.2 = (bf16[2]{0:T(256)(128)(2,1)S(1)}, bf16[2]{0:T(256)(128)(2,1)S(1)}, u32[]{:S(2)}, u32[]{:S(2)}) collective-permute-start(bf16[2]{0:T(256)(128)(2,1)S(1)} %copy.146), channel_id=1, source_target_pairs={{448,0},{456,8},{464,16},{472,24},{480,32},{488,40},{496,48},{504,... | collective-permute-start | bytes 20 | tf_op jit(solution)/shard_map/while/body/eval_jaxpr/ppermute | solution.py:18
  331.5 31.3 %collective-permute-start.1 = (bf16[128,64]{1,0:T(8,128)(2,1)S(1)}, bf16[128,64]{1,0:T(8,128)(2,1)S(1)}, u32[]{:S(2)}, u32[]{:S(2)}) collective-permute-start(bf16[128,64]{1,0:T(8,128)(2,1)S(1)} %copy.145), channel_id=1, source_target_pairs={{448,0},{456,8},{464,16},{472,24},{480,32},{488,40},{496,48},{504,... | collective-permute-start | bytes 49160 | tf_op jit(solution)/shard_map/while/body/eval_jaxpr/ppermute | solution.py:18
  336.0 26.8 %collective-permute-start = (bf16[128,512]{1,0:T(8,128)(2,1)S(1)}, bf16[128,512]{1,0:T(8,128)(2,1)S(1)}, u32[]{:S(2)}, u32[]{:S(2)}) collective-permute-start(bf16[128,512]{1,0:T(8,128)(2,1)S(1)} %copy.144), channel_id=1, source_target_pairs={{448,0},{456,8},{464,16},{472,24},{480,32},{488,40},{496,48},{504,... | collective-permute-start | bytes 393224 | tf_op jit(solution)/shard_map/while/body/eval_jaxpr/ppermute | solution.py:18
  873.6 587.0 %reduce-scatter.2.cloned.1.call-start = ((), (), s32[]{:S(2)}) async-start(), calls=%async_computation.3 | async-start | bytes 2129920 | tf_op jit(solution)/shard_map/reduce_scatter | solution.py:213
  (48 other events, 555.5 us)
Sparse Core Ops, SparseCore 0:
  10.7 123.6 all-gather.1
  873.8 143.1 all-reduce.1
  1020.6 439.9 reduce-scatter.1
where the time goes:
time: 1480 us; the launch traced here: 1470 us
  waiting for transfers between devices  708 us (48%)
  local copies, waits for them, and re-layouts  215 us (15%)
  matrix products  144 us (10%)
  other arithmetic  115 us (8%)
  starting transfers between devices  104 us (7%)
  loops' own time  100 us (7%)
  blocking collectives  61.5 us (4%)
  between operations  19 us (1%)
    reduce_scatter x1, waiting for transfers between devices, shards(): lax.psum_scatter(jnp.einsum('thn,thc->nhc', query_nope, dq_latent, prefer...  442 us
    all_gather x1, waiting for transfers between devices, shards(): lax.all_gather(dequant(weight_codes, weight_scale), 'seq', axis=0, tiled=...  119 us
    ppermute x37, starting transfers between devices, from_behind(): return lax.ppermute(block, axis, route)  104 us
    ppermute x37, waiting for transfers between devices, from_behind(): return lax.ppermute(block, axis, route)  76.9 us
    psum x1, waiting for transfers between devices, shards(): lax.psum(carried.astype(jnp.bfloat16), 'head').astype(jnp.float32)  70 us
    psum x1, blocking collectives, shards(): lax.psum(carried_rot.astype(jnp.bfloat16), 'head').astype(jnp.float32)  61.5 us
    another operation x1, loops' own time, shards(): lax.fori_loop(0, groups, grads_step, initial)  40.4 us
    another operation x1, loops' own time, shards(): lax.fori_loop(0, groups - 1, first_turn, (moving, statistics, buffers))  36.9 us
  transfers between devices with their start and end apart: 40, of which 19 were waited for; matrix products, arithmetic and copies ran while one was open for 11% of the time, Pallas kernels for 0%

commit v1 on v0

v1 whole, which is shorter than its diff:
```python
import math

import jax
import jax.numpy as jnp
from jax import lax
from jax.experimental import pallas as pl
from jax.experimental.pallas import tpu as pltpu
from jax.sharding import Mesh, PartitionSpec as P

RANKS = 8
HEADS = 8
HALF = 64
TOK = 128
DN = 128
DC = 512
DR = 64
WIDE = 640
BLOCK = 256
ROWS = HALF * HEADS
QUARTER = 32
WROWS = 16
FACTOR = 1.0 / math.sqrt(DN + DR)
LOG2E = 1.0 / math.log(2.0)
MASKED = -1e30
VMEM_LIMIT = 56 * 1024 * 1024

bf16 = jnp.bfloat16
f32 = jnp.float32

AXES = ("zl", "x", "c", "zh", "y")
SEQ = ("zl", "x", "c")
HEAD = ("zh", "y")


def nn(a, b):
    return lax.dot_general(a, b, (((1,), (0,)), ((), ())), preferred_element_type=f32)


def nt(a, b):
    return lax.dot_general(a, b, (((1,), (1,)), ((), ())), preferred_element_type=f32)


def tn(a, b):
    return lax.dot_general(a, b, (((0,), (0,)), ((), ())), preferred_element_type=f32)


def iota(shape, axis):
    return lax.broadcasted_iota(jnp.int32, shape, axis)


def chosen(condition):
    return jnp.where(condition, 1.0, 0.0).astype(bf16)


def head_major():
    out, inp = iota((128, 128), 0), iota((128, 128), 1)
    return chosen(inp == (out % 16) * 8 + out // 16)


def token_major():
    out, inp = iota((128, 128), 0), iota((128, 128), 1)
    return chosen(inp == (out % 8) * 16 + out // 8)


def weight_order(row, x, c):
    other, step, rest = row // 64, (row // 16) % 4, row % 16
    return (rest // 2) * 16 + ((x + step) % 4) * 4 + ((c + other) % 2) * 2 + rest % 2


def call(body, outs, ins, scratch=(), flops=0, smem=(), name=None):
    nbytes = sum(math.prod(s.shape) * s.dtype.itemsize for s in list(outs) + list(ins))
    specs = [
        pl.BlockSpec(memory_space=pltpu.SMEM if i in smem else pltpu.VMEM) for i in range(len(ins))
    ]
    return pl.pallas_call(
        body,
        out_shape=outs,
        in_specs=specs,
        out_specs=[pl.BlockSpec(memory_space=pltpu.VMEM) for _ in outs],
        scratch_shapes=list(scratch),
        compiler_params=pltpu.CompilerParams(vmem_limit_bytes=VMEM_LIMIT),
        cost_estimate=pl.CostEstimate(flops=flops, bytes_accessed=nbytes, transcendentals=0),
        name=name,
    )(*ins)


def shape(*dims, dtype=bf16):
    return jax.ShapeDtypeStruct(dims, dtype)


def prepare_kernel(lat_ref, rot_ref, codes_ref, scale_ref, pos_ref, out_ref):
    y = lax.axis_index("y")
    rows = pl.ds(pl.multiple_of(y * QUARTER, QUARTER), QUARTER)
    codes = codes_ref[...]
    levels = codes + (16 * (codes >> 4) + 8) + (64 * (codes >> 6) + 32)
    row = iota((WROWS, DC), 0)
    scale = jnp.zeros((WROWS, DC), f32)
    for i in range(WROWS):
        scale = jnp.where(row == i, scale_ref[i // HEADS, i % HEADS], scale)
    weight = (scale * levels.astype(f32) / 3.0).astype(bf16)
    widen = chosen(iota((DR, 128), 0) == iota((DR, 128), 1))
    lane = iota((QUARTER, 128), 1)
    run = [(pos_ref[half * HALF] >> 6).astype(f32) for half in range(2)]
    rest = nn(rot_ref[rows, :], widen)
    rest = jnp.where(lane == DR, run[0], jnp.where(lane == DR + 1, run[1], rest)).astype(bf16)
    lat = lat_ref[rows, :]
    blank = jnp.zeros((WROWS, 128), bf16)
    for r in range(RANKS):
        out_ref[r, 0:QUARTER, 0:DC] = lat
        out_ref[r, 0:QUARTER, DC:WIDE] = rest
        out_ref[r, QUARTER : QUARTER + WROWS, 0:DC] = weight
        out_ref[r, QUARTER : QUARTER + WROWS, DC:WIDE] = blank


def split_kernel(in_ref, lat_ref, weight_ref):
    for r in range(RANKS):
        lat_ref[r * QUARTER : (r + 1) * QUARTER, :] = in_ref[r, 0:QUARTER, :]
    rows = jnp.concatenate(
        [in_ref[r, QUARTER : QUARTER + WROWS, 0:DC] for r in range(RANKS)], axis=0
    )
    out, inp = iota((128, 128), 0), iota((128, 128), 1)
    head, rank, n = out // 16, (out % 16) // 2, out % 2
    weight_ref[...] = nn(chosen(inp == rank * 16 + n * 8 + head), rows).astype(bf16)


def queries_kernel(nope_ref, rot_ref, up_ref, nope_out, rot_out, up_out):
    x, c = lax.axis_index("x"), lax.axis_index("c")
    by_head = head_major()
    inp, out = iota((DN, DN), 0), iota((DN, DN), 1)
    reorder = chosen(inp == weight_order(out, x, c))
    for g in range(TOK // 16):
        half, start = g // 4, (g % 4) * 16
        rows = slice(g * 128, (g + 1) * 128)
        nope = nn(nn(by_head, nope_ref[rows, :]).astype(bf16), reorder).astype(bf16)
        up = nn(by_head, up_ref[rows, :]).astype(bf16)
        for h in range(HEADS):
            place = (half * HEADS + h) * HALF + start
            nope_out[place : place + 16, :] = nope[h * 16 : (h + 1) * 16, :]
            up_out[place : place + 16, :] = up[h * 16 : (h + 1) * 16, :]
    inp, out = iota((128, 128), 0), iota((128, 128), 1)
    for h in range(HEADS):
        pick = chosen((inp == out + DR * (h % 2)) & (out < DR))
        turned = nn(rot_ref[:, (h // 2) * 128 : (h // 2 + 1) * 128], pick).astype(bf16)
        for half in range(2):
            place = (half * HEADS + h) * HALF
            rot_out[place : place + HALF, :] = turned[half * HALF : (half + 1) * HALF, :]


def attention_kernel(
    runs_ref,
    pos_ref,
    l0,
    l1,
    l2,
    l3,
    w0,
    w1,
    w2,
    w3,
    wo,
    nope_ref,
    rot_ref,
    up_ref,
    k0,
    k1,
    k2,
    k3,
    own_ref,
    other_ref,
    dq_ref,
    weight_ref,
    keys,
    query,
    score,
    slope,
    dkey,
    dquery,
):
    y = lax.axis_index("y")

    def place_of(step, rank):
        quarter = (y + step) % 4
        run = runs_ref[rank * 2 + quarter // 2]
        return pl.ds(pl.multiple_of(run * HALF + (quarter % 2) * QUARTER, QUARTER), QUARTER)

    for step, part in enumerate((l0, l1, l2, l3)):
        for r in range(RANKS):
            keys[place_of(step, r), :] = part[r * QUARTER : (r + 1) * QUARTER, :]
    for h in range(HEADS):
        for step, part in enumerate((w0, w1, w2, w3)):
            weight_ref[h * DN + step * 16 : h * DN + step * 16 + 16, :] = part[
                h * 16 : h * 16 + 16, :
            ]
            at = h * DN + 64 + step * 16
            weight_ref[at : at + 16, :] = wo[step * 128 + h * 16 : step * 128 + h * 16 + 16, :]
    for h in range(HEADS):
        pair = [nope_ref[(half * HEADS + h) * HALF : (half * HEADS + h + 1) * HALF, :] for half in range(2)]
        absorbed = nn(jnp.concatenate(pair, axis=0), weight_ref[h * DN : (h + 1) * DN, :])
        for half in range(2):
            at = (half * HEADS + h) * HALF
            query[at : at + HALF, 0:DC] = absorbed[half * HALF : (half + 1) * HALF, :].astype(bf16)
    query[:, DC:WIDE] = rot_ref[...]
    dkey[...] = jnp.zeros_like(dkey)

    for half in range(2):
        rows = slice(half * ROWS, (half + 1) * ROWS)
        run = pos_ref[half * HALF] >> 6
        place = run * HALF + iota((1, ROWS), 1) % HALF
        count = run // 4 + 1

        def scores(j, top):
            at = pl.ds(pl.multiple_of(j * BLOCK, BLOCK), BLOCK)
            part = keys[at, :]
            s = nt(part, query[rows, :]) * (FACTOR * LOG2E)
            s = jnp.where(j * BLOCK + iota((BLOCK, ROWS), 0) <= place, s, MASKED)
            score[j] = s
            slope[j] = nt(part[:, 0:DC], up_ref[rows, :])
            return jnp.maximum(top, jnp.max(s, axis=0, keepdims=True))

        top = lax.fori_loop(0, count, scores, jnp.full((1, ROWS), MASKED, f32))

        def totals(j, running):
            total, weighted = running
            e = jnp.exp2(score[j] - top)
            score[j] = e
            return (
                total + jnp.sum(e, axis=0, keepdims=True),
                weighted + jnp.sum(e * slope[j], axis=0, keepdims=True),
            )

        zero = jnp.zeros((1, ROWS), f32)
        total, weighted = lax.fori_loop(0, count, totals, (zero, zero))
        inverse = 1.0 / total
        inner = weighted * inverse
        dquery[...] = jnp.zeros_like(dquery)

        def grads(j, carry):
            at = pl.ds(pl.multiple_of(j * BLOCK, BLOCK), BLOCK)
            prob = score[j] * inverse
            grad = (prob * (slope[j] - inner) * FACTOR).astype(bf16)
            dquery[...] += tn(grad, keys[at, :])
            dkey[at, :] += nn(grad, query[rows, :])
            dkey[at, 0:DC] += nn(prob.astype(bf16), up_ref[rows, :])
            return carry

        lax.fori_loop(0, count, grads, 0)
        dq_ref[rows, :] = dquery[...].astype(bf16)

    for step, part in enumerate((k0, k1, k2, k3)):
        for r in range(RANKS):
            part[r * QUARTER : (r + 1) * QUARTER, :] = dkey[place_of(step, r), :].astype(bf16)
    for h in range(HEADS):
        places = [slice((half * HEADS + h) * HALF, (half * HEADS + h + 1) * HALF) for half in range(2)]
        nope = jnp.concatenate([nope_ref[p, :] for p in places], axis=0)
        dq = jnp.concatenate([dq_ref[p, 0:DC] for p in places], axis=0)
        master = tn(nope, dq).astype(bf16)
        for step in range(4):
            at = slice(step * 128 + h * 16, step * 128 + h * 16 + 16)
            own_ref[at, :] = master[step * 16 : step * 16 + 16, :]
            other_ref[at, :] = master[64 + step * 16 : 64 + step * 16 + 16, :]


def query_grads_kernel(dq_ref, weight_ref, nope_out, rot_out, scratch):
    x, c = lax.axis_index("x"), lax.axis_index("c")
    out, inp = iota((DN, DN), 1), iota((DN, DN), 0)
    reorder = chosen(out == weight_order(inp, x, c))
    i, j = iota((128, 128), 0), iota((128, 128), 1)
    left = chosen((i == j) & (j < DR))
    right = chosen((i == j - DR) & (i < DR))
    for h in range(HEADS):
        places = [slice((half * HEADS + h) * HALF, (half * HEADS + h + 1) * HALF) for half in range(2)]
        dq = jnp.concatenate([dq_ref[p, 0:DC] for p in places], axis=0)
        grad = nt(dq, weight_ref[h * DN : (h + 1) * DN, :]).astype(bf16)
        scratch[h * TOK : (h + 1) * TOK, :] = nn(grad, reorder).astype(bf16)
    by_token = token_major()
    for g in range(TOK // 16):
        rows = [scratch[h * TOK + g * 16 : h * TOK + g * 16 + 16, :] for h in range(HEADS)]
        nope_out[g * 128 : (g + 1) * 128, :] = nn(by_token, jnp.concatenate(rows, axis=0)).astype(bf16)
    for p in range(HEADS // 2):
        sides = []
        for h in (2 * p, 2 * p + 1):
            places = [slice((half * HEADS + h) * HALF, (half * HEADS + h + 1) * HALF) for half in range(2)]
            sides.append(jnp.concatenate([dq_ref[q, DC:WIDE] for q in places], axis=0))
        rot_out[:, p * 128 : (p + 1) * 128] = (nn(sides[0], left) + nn(sides[1], right)).astype(bf16)


def core_sum_kernel(own_ref, got_ref, m0, m1, m2, m3):
    for step, part in enumerate((m0, m1, m2, m3)):
        rows = slice(step * 128, (step + 1) * 128)
        part[...] = (own_ref[rows, :].astype(f32) + got_ref[rows, :].astype(f32)).astype(bf16)


def plane_sum_kernel(m0, m1, m2, m3, k0, k1, k2, k3, out_ref):
    master = m0[...].astype(f32) + m1[...].astype(f32) + m2[...].astype(f32) + m3[...].astype(f32)
    out, inp = iota((128, 128), 0), iota((128, 128), 1)
    rank, n, head = out // 16, (out % 16) // 8, out % 8
    master = nn(chosen(inp == head * 16 + rank * 2 + n), master.astype(bf16)).astype(bf16)
    blank = jnp.zeros((WROWS, 128), bf16)
    for r in range(RANKS):
        rows = slice(r * QUARTER, (r + 1) * QUARTER)
        part = k0[rows, :].astype(f32) + k1[rows, :].astype(f32)
        part = part + k2[rows, :].astype(f32) + k3[rows, :].astype(f32)
        out_ref[r, 0:QUARTER, :] = part.astype(bf16)
        out_ref[r, QUARTER : QUARTER + WROWS, 0:DC] = master[r * 16 : r * 16 + 16, :]
        out_ref[r, QUARTER : QUARTER + WROWS, DC:WIDE] = blank


def rank_sum_kernel(in_ref, keys_ref, master_ref):
    keys = in_ref[0, 0:QUARTER, :].astype(f32)
    master = in_ref[0, QUARTER : QUARTER + WROWS, 0:DC].astype(f32)
    for r in range(1, RANKS):
        keys = keys + in_ref[r, 0:QUARTER, :].astype(f32)
        master = master + in_ref[r, QUARTER : QUARTER + WROWS, 0:DC].astype(f32)
    master_ref[...] = master
    keys = keys.astype(bf16)
    for r in range(8):
        keys_ref[r] = keys


def head_sum_kernel(in_ref, latent_ref, rotary_ref):
    for y in range(4):
        rows = slice(y * QUARTER, (y + 1) * QUARTER)
        total = in_ref[y].astype(f32) + in_ref[4 + y].astype(f32)
        latent_ref[rows, :] = total[:, 0:DC]
        rotary_ref[rows, :] = total[:, DC : DC + DR]


def shift(block, axis, step):
    n = lax.axis_size(axis)
    return lax.ppermute(block, axis, [(i, (i + step) % n) for i in range(n)])


def swap(block, axis):
    return lax.ppermute(block, axis, [(0, 1), (1, 0)])


def everyone(blocks, axes):
    return lax.all_to_all(blocks, axes, 0, 0, tiled=True)


def shards(nope, rotary, latent, keys, upstream, codes, scale, positions):
    blocks = (shape(RANKS, QUARTER + WROWS, WIDE),)
    (send,) = call(
        prepare_kernel,
        blocks,
        (latent, keys, codes.reshape(WROWS, DC), scale, positions),
        smem=(3, 4),
        name="prepare",
    )
    got = everyone(send, "zl")
    l0, w0 = call(split_kernel, (shape(256, WIDE), shape(128, DC)), (got,), name="split")
    runs = got[:, 0, DC + DR : DC + DR + 2].astype(jnp.int32).reshape(16)
    w = [w0] + [shift(w0, "x", -step) for step in (1, 3, 2)]
    w = [w[0], w[1], w[3], w[2]]
    lat = [l0] + [shift(l0, "y", -step) for step in (1, 3, 2)]
    lat = [lat[0], lat[1], lat[3], lat[2]]
    wo = swap(jnp.concatenate(w, axis=0), "c")
    nope_rows, rot_rows, up_rows = call(
        queries_kernel,
        (shape(1024, DN), shape(1024, 128), shape(1024, DC)),
        (nope.reshape(1024, DN), rotary, upstream.reshape(1024, DC)),
        flops=2 * 1024 * 128 * 1024,
        name="queries",
    )
    k0, k1, k2, k3, own, other, dq, weight = call(
        attention_kernel,
        (shape(256, WIDE),) * 4 + (shape(512, DC),) * 2 + (shape(1024, WIDE), shape(1024, DC)),
        (runs, positions, *lat, *w, wo, nope_rows, rot_rows, up_rows),
        scratch=(
            pltpu.VMEM((1024, WIDE), bf16),
            pltpu.VMEM((1024, WIDE), bf16),
            pltpu.VMEM((4, BLOCK, ROWS), f32),
            pltpu.VMEM((4, BLOCK, ROWS), f32),
            pltpu.VMEM((1024, WIDE), f32),
            pltpu.VMEM((ROWS, WIDE), f32),
        ),
        smem=(0, 1),
        flops=2 * 512 * 1280 * 2944,
        name="attention",
    )
    got_other = swap(other, "c")
    k = [k0, shift(k1, "y", 1), shift(k3, "y", 3), shift(k2, "y", 2)]
    m0, m1, m2, m3 = call(core_sum_kernel, (shape(128, DC),) * 4, (own, got_other), name="core_sum")
    m = [m0, shift(m1, "x", 1), shift(m3, "x", 3), shift(m2, "x", 2)]
    nope_grad, rot_grad = call(
        query_grads_kernel,
        (shape(1024, DN), shape(TOK, HEADS * DR)),
        (dq, weight),
        scratch=(pltpu.VMEM((1024, DN), bf16),),
        flops=2 * 1024 * 128 * 768,
        name="query_grads",
    )
    (send,) = call(plane_sum_kernel, blocks, (*m, *k), name="plane_sum")
    got = everyone(send, "zl")
    summed, master = call(
        rank_sum_kernel, (shape(8, QUARTER, WIDE), shape(WROWS, DC, dtype=f32)), (got,), name="rank_sum"
    )
    got = everyone(summed, HEAD)
    latent_grad, keys_grad = call(
        head_sum_kernel, (shape(TOK, DC, dtype=f32), shape(TOK, DR, dtype=f32)), (got,), name="head_sum"
    )
    return (
        nope_grad.reshape(TOK, HEADS, DN),
        rot_grad,
        latent_grad,
        keys_grad,
        master.reshape(2, HEADS, DC),
    )


def solution(mesh):
    fine = Mesh(mesh.devices.reshape(8, 4, 2, 2, 4), AXES)
    in_specs = (
        P(SEQ, HEAD, None),
        P(SEQ, HEAD),
        P(SEQ, None),
        P(SEQ, None),
        P(SEQ, HEAD, None),
        P(SEQ, HEAD, None),
        P(SEQ, HEAD),
        P(SEQ),
    )
    out_specs = (
        P(SEQ, HEAD, None),
        P(SEQ, HEAD),
        P(SEQ, None),
        P(SEQ, None),
        P(SEQ, HEAD, None),
    )
    return jax.shard_map(shards, mesh=fine, in_specs=in_specs, out_specs=out_specs, check_vma=False)
```

time: 1480 us -> 203 us (0.14)
  the two profiles are of different devices: /device:TPU:8 before, /device:TPU:32 now
where the time goes in v1:
time: 203 us; the launch traced here: 202 us
  blocking collectives  68.1 us (34%)
  starting transfers between devices  56.5 us (28%)
  waiting for transfers between devices  36.4 us (18%)
  Pallas kernels  31.8 us (16%)
  local copies, waits for them, and re-layouts  6.62 us (3%)
    all_to_all x2, blocking collectives, everyone(): return lax.all_to_all(blocks, axes, 0, 0, tiled=True)  68.1 us
    ppermute x12, starting transfers between devices, shift(): return lax.ppermute(block, axis, [(i, (i + step) % n) for i in range(n)])  43.6 us
    pallas_call x9, Pallas kernels, call(): pl.pallas_call(body, out_shape=outs, in_specs=specs, out_specs=[pl.BlockS...  31.8 us
    all_to_all x1, waiting for transfers between devices, everyone(): return lax.all_to_all(blocks, axes, 0, 0, tiled=True)  20.1 us
    ppermute x12, waiting for transfers between devices, shift(): return lax.ppermute(block, axis, [(i, (i + step) % n) for i in range(n)])  16.4 us
    all_to_all x1, starting transfers between devices, everyone(): return lax.all_to_all(blocks, axes, 0, 0, tiled=True)  9.05 us
    unnamed x32, local copies, waits for them, and re-layouts  6.03 us
  transfers between devices with their start and end apart: 15, of which 6 were waited for; matrix products, arithmetic and copies ran while one was open for 1% of the time, Pallas kernels for 4%

profile of v1, /device:TPU:32, one launch (start us, length us, event | category | flops | bytes accessed | tf_op | source)
XLA Modules:
  0.0 202.2 jit_solution(13916480160802693146)
XLA Ops:
  4.0 38.3 %all_to_all.15.in_ref = bf16[8,48,640]{2,1,0:T(8,128)(2,1)} all-to-all(bf16[8,48,640]{2,1,0:T(8,128)(2,1)} %prepare.1), channel_id=1, replica_groups=mesh['zl'=8,'x'=4,'c'=2,'zh'=2,'y'=4] {'zl'}, dimensions={0} | all-to-all | bytes 983040 | tf_op jit(solution)/shard_map/all_to_all | solution.py:338
  44.1 3.4 %collective-permute-start.5 = (bf16[128,512]{1,0:T(8,128)(2,1)}, bf16[128,512]{1,0:T(8,128)(2,1)S(1)}, u32[]{:S(2)}, u32[]{:S(2)}) collective-permute-start(bf16[128,512]{1,0:T(8,128)(2,1)} %get-tuple-element.29.w0), channel_id=1, source_target_pairs={{0,16},{16,32},{32,48},{48,0},{1,17},{17,33},{33,49},{49,1},{2,18}... | collective-permute-start | bytes 393224 | tf_op jit(solution)/shard_map/ppermute | solution.py:330
  47.5 4.6 %collective-permute-start.4 = (bf16[128,512]{1,0:T(8,128)(2,1)}, bf16[128,512]{1,0:T(8,128)(2,1)S(1)}, u32[]{:S(2)}, u32[]{:S(2)}) collective-permute-start(bf16[128,512]{1,0:T(8,128)(2,1)} %get-tuple-element.29.w0), channel_id=1, source_target_pairs={{0,32},{16,48},{32,0},{48,16},{1,33},{17,49},{33,1},{49,17},{2,34}... | collective-permute-start | bytes 393224 | tf_op jit(solution)/shard_map/ppermute | solution.py:330
  52.2 3.3 %collective-permute-start.3 = (bf16[128,512]{1,0:T(8,128)(2,1)}, bf16[128,512]{1,0:T(8,128)(2,1)S(1)}, u32[]{:S(2)}, u32[]{:S(2)}) collective-permute-start(bf16[128,512]{1,0:T(8,128)(2,1)} %get-tuple-element.29.w0), channel_id=1, source_target_pairs={{0,48},{16,0},{32,16},{48,32},{1,49},{17,1},{33,17},{49,33},{2,50}... | collective-permute-start | bytes 393224 | tf_op jit(solution)/shard_map/ppermute | solution.py:330
  56.1 3.1 %collective-permute-done.3.w1 = bf16[128,512]{1,0:T(8,128)(2,1)S(1)} collective-permute-done((bf16[128,512]{1,0:T(8,128)(2,1)}, bf16[128,512]{1,0:T(8,128)(2,1)S(1)}, u32[]{:S(2)}, u32[]{:S(2)}) %collective-permute-start.3) | collective-permute-done | bytes 131104 | tf_op jit(solution)/shard_map/ppermute | solution.py:330
  62.2 3.5 %collective-permute-start.2 = (bf16[256,640]{1,0:T(8,128)(2,1)}, bf16[256,640]{1,0:T(8,128)(2,1)S(1)}, u32[]{:S(2)}, u32[]{:S(2)}) collective-permute-start(bf16[256,640]{1,0:T(8,128)(2,1)} %get-tuple-element.28.l0), channel_id=1, source_target_pairs={{0,1},{1,2},{2,3},{3,0},{4,5},{5,6},{6,7},{7,4},{8,9},{9,10},{10,1... | collective-permute-start | bytes 983048 | tf_op jit(solution)/shard_map/ppermute | solution.py:330
  65.7 4.8 %collective-permute-start.1 = (bf16[256,640]{1,0:T(8,128)(2,1)}, bf16[256,640]{1,0:T(8,128)(2,1)S(1)}, u32[]{:S(2)}, u32[]{:S(2)}) collective-permute-start(bf16[256,640]{1,0:T(8,128)(2,1)} %get-tuple-element.28.l0), channel_id=1, source_target_pairs={{0,2},{1,3},{2,0},{3,1},{4,6},{5,7},{6,4},{7,5},{8,10},{9,11},{10,... | collective-permute-start | bytes 983048 | tf_op jit(solution)/shard_map/ppermute | solution.py:330
  70.5 3.3 %collective-permute-start = (bf16[256,640]{1,0:T(8,128)(2,1)}, bf16[256,640]{1,0:T(8,128)(2,1)S(1)}, u32[]{:S(2)}, u32[]{:S(2)}) collective-permute-start(bf16[256,640]{1,0:T(8,128)(2,1)} %get-tuple-element.28.l0), channel_id=1, source_target_pairs={{0,3},{1,0},{2,1},{3,2},{4,7},{5,4},{6,5},{7,6},{8,11},{9,8},{10,9... | collective-permute-start | bytes 983048 | tf_op jit(solution)/shard_map/ppermute | solution.py:330
  73.7 3.2 %queries.1 = (bf16[1024,128]{1,0:T(8,128)(2,1)}, bf16[1024,128]{1,0:T(8,128)(2,1)}, bf16[1024,512]{1,0:T(8,128)(2,1)}) custom-call(bf16[1024,128]{1,0:T(8,128)(2,1)} %bitcast.6, bf16[128,512]{1,0:T(8,128)(2,1)} %rot_ref.2, bf16[1024,512]{1,0:T(8,128)(2,1)} %bitcast.5), custom_call_target="tpu_custom_call" | custom-call | flops 268435456 | bytes 3014656 | tf_op jit(solution)/shard_map/queries/pallas_call | solution.py:75
  78.3 5.5 %collective-permute-done.1.l2 = bf16[256,640]{1,0:T(8,128)(2,1)S(1)} collective-permute-done((bf16[256,640]{1,0:T(8,128)(2,1)}, bf16[256,640]{1,0:T(8,128)(2,1)S(1)}, u32[]{:S(2)}, u32[]{:S(2)}) %collective-permute-start.1) | collective-permute-done | bytes 327712 | tf_op jit(solution)/shard_map/ppermute | solution.py:330
  86.2 12.9 %attention.1 = (bf16[256,640]{1,0:T(8,128)(2,1)}, bf16[256,640]{1,0:T(8,128)(2,1)}, bf16[256,640]{1,0:T(8,128)(2,1)}, bf16[256,640]{1,0:T(8,128)(2,1)}, bf16[512...) custom-call(s32[16]{0:T(128)} %reshape.34.runs_ref, ...), custom_call_target="tpu_custom_call" | custom-call | flops 3858759680 | bytes 8651328 | tf_op jit(solution)/shard_map/attention/pallas_call | solution.py:75
  101.0 4.4 %collective-permute-start.11 = (bf16[256,640]{1,0:T(8,128)(2,1)}, bf16[256,640]{1,0:T(8,128)(2,1)S(1)}, u32[]{:S(2)}, u32[]{:S(2)}) collective-permute-start(bf16[256,640]{1,0:T(8,128)(2,1)} %get-tuple-element.44), channel_id=1, source_target_pairs={{0,1},{1,2},{2,3},{3,0},{4,5},{5,6},{6,7},{7,4},{8,9},{9,10},{10,1... | collective-permute-start | bytes 983048 | tf_op jit(solution)/shard_map/ppermute | solution.py:330
  105.4 2.6 %collective-permute-start.12 = (bf16[256,640]{1,0:T(8,128)(2,1)}, bf16[256,640]{1,0:T(8,128)(2,1)S(1)}, u32[]{:S(2)}, u32[]{:S(2)}) collective-permute-start(bf16[256,640]{1,0:T(8,128)(2,1)} %get-tuple-element.45), channel_id=1, source_target_pairs={{0,3},{1,0},{2,1},{3,2},{4,7},{5,4},{6,5},{7,6},{8,11},{9,8},{10,9... | collective-permute-start | bytes 983048 | tf_op jit(solution)/shard_map/ppermute | solution.py:330
  108.0 3.9 %collective-permute-start.13 = (bf16[256,640]{1,0:T(8,128)(2,1)}, bf16[256,640]{1,0:T(8,128)(2,1)S(1)}, u32[]{:S(2)}, u32[]{:S(2)}) collective-permute-start(bf16[256,640]{1,0:T(8,128)(2,1)} %get-tuple-element.46), channel_id=1, source_target_pairs={{0,2},{1,3},{2,0},{3,1},{4,6},{5,7},{6,4},{7,5},{8,10},{9,11},{10,... | collective-permute-start | bytes 983048 | tf_op jit(solution)/shard_map/ppermute | solution.py:330
  112.7 2.0 core_sum.1
  114.7 2.1 %collective-permute-start.8 = (bf16[128,512]{1,0:T(8,128)(2,1)}, bf16[128,512]{1,0:T(8,128)(2,1)S(1)}, u32[]{:S(2)}, u32[]{:S(2)}) collective-permute-start(bf16[128,512]{1,0:T(8,128)(2,1)} %get-tuple-element.40), channel_id=1, source_target_pairs={{0,16},{16,32},{32,48},{48,0},{1,17},{17,33},{33,49},{49,1},{2,18}... | collective-permute-start | bytes 393224 | tf_op jit(solution)/shard_map/ppermute | solution.py:330
  116.8 5.0 %collective-permute-start.9 = (bf16[128,512]{1,0:T(8,128)(2,1)}, bf16[128,512]{1,0:T(8,128)(2,1)S(1)}, u32[]{:S(2)}, u32[]{:S(2)}) collective-permute-start(bf16[128,512]{1,0:T(8,128)(2,1)} %get-tuple-element.41), channel_id=1, source_target_pairs={{0,48},{16,0},{32,16},{48,32},{1,49},{17,1},{33,17},{49,33},{2,50}... | collective-permute-start | bytes 393224 | tf_op jit(solution)/shard_map/ppermute | solution.py:330
  121.8 2.7 %collective-permute-start.10 = (bf16[128,512]{1,0:T(8,128)(2,1)}, bf16[128,512]{1,0:T(8,128)(2,1)S(1)}, u32[]{:S(2)}, u32[]{:S(2)}) collective-permute-start(bf16[128,512]{1,0:T(8,128)(2,1)} %get-tuple-element.42), channel_id=1, source_target_pairs={{0,32},{16,48},{32,0},{48,16},{1,33},{17,49},{33,1},{49,17},{2,34}... | collective-permute-start | bytes 393224 | tf_op jit(solution)/shard_map/ppermute | solution.py:330
  124.6 5.8 %collective-permute-done.10.m3 = bf16[128,512]{1,0:T(8,128)(2,1)S(1)} collective-permute-done((bf16[128,512]{1,0:T(8,128)(2,1)}, bf16[128,512]{1,0:T(8,128)(2,1)S(1)}, u32[]{:S(2)}, u32[]{:S(2)}) %collective-permute-start.10) | collective-permute-done | bytes 131104 | tf_op jit(solution)/shard_map/ppermute | solution.py:330
  131.1 2.6 %plane_sum.1 = bf16[8,48,640]{2,1,0:T(8,128)(2,1)} custom-call(bf16[128,512]{1,0:T(8,128)(2,1)} %get-tuple-element.39.m0, bf16[128,512]{1,0:T(8,128)(2,1)} %copy-done.5, bf16[128,512]{1,0:T(8,128)(2,1)} %copy-done.6, bf16[128,512]{1,0:T(8,128)(2,1)} %copy-done.7, bf16[256,640]{1,0:T(8,128)(2,1)} %get-tuple-element.43.k0, bf16[256,640]{1,0:T(8,128)(2,1)} %copy-done.2, ...), custom_call_target="tpu_custom_call" | custom-call | bytes 2326528 | tf_op jit(solution)/shard_map/plane_sum/pallas_call | solution.py:75
  133.7 29.8 %all_to_all.16.in_ref = bf16[8,48,640]{2,1,0:T(8,128)(2,1)} all-to-all(bf16[8,48,640]{2,1,0:T(8,128)(2,1)} %plane_sum.1), channel_id=1, replica_groups=mesh['zl'=8,'x'=4,'c'=2,'zh'=2,'y'=4] {'zl'}, dimensions={0} | all-to-all | bytes 983040 | tf_op jit(solution)/shard_map/all_to_all | solution.py:338
  165.3 9.0 %all-to-all-start.2 = ((bf16[8,32,640]{2,1,0:T(8,128)(2,1)}), bf16[8,32,640]{2,1,0:T(8,128)(2,1)S(1)}, u32[]{:S(2)}, u32[]{:S(2)}) async-start(bf16[8,32,640]{2,1,0:T(8,128)(2,1)} %get-tuple-element.47), calls=%async_computation.2 | async-start | bytes 655360 | tf_op jit(solution)/shard_map/all_to_all | solution.py:338
  174.3 3.8 %query_grads.1 = (bf16[1024,128]{1,0:T(8,128)(2,1)}, bf16[128,512]{1,0:T(8,128)(2,1)}) custom-call(bf16[1024,640]{1,0:T(8,128)(2,1)} %get-tuple-element.33.dq_ref, bf16[1024,512]{1,0:T(8,128)(2,1)} %get-tuple-element.34.weight_ref), custom_call_target="tpu_custom_call" | custom-call | flops 201326592 | bytes 2752512 | tf_op jit(solution)/shard_map/query_grads/pallas_call | solution.py:75
  178.2 20.1 %all-to-all-done.2.in_ref = bf16[8,32,640]{2,1,0:T(8,128)(2,1)S(1)} async-done(((bf16[8,32,640]{2,1,0:T(8,128)(2,1)}), bf16[8,32,640]{2,1,0:T(8,128)(2,1)S(1)}, u32[]{:S(2)}, u32[]{:S(2)}) %all-to-all-start.2) | async-done | bytes 327712 | tf_op jit(solution)/shard_map/all_to_all | solution.py:338
  (52 shorter events, 21.5 us)
Async XLA Ops:
  44.1 11.4 %collective-permute-start.5 = (bf16[128,512]{1,0:T(8,128)(2,1)}, bf16[128,512]{1,0:T(8,128)(2,1)S(1)}, u32[]{:S(2)}, u32[]{:S(2)}) collective-permute-start(bf16[128,512]{1,0:T(8,128)(2,1)} %get-tuple-element.29.w0), channel_id=1, source_target_pairs={{0,16},{16,32},{32,48},{48,0},{1,17},{17,33},{33,49},{49,1},{2,18}... | collective-permute-start | bytes 393224 | tf_op jit(solution)/shard_map/ppermute | solution.py:330
  47.5 8.6 %collective-permute-start.4 = (bf16[128,512]{1,0:T(8,128)(2,1)}, bf16[128,512]{1,0:T(8,128)(2,1)S(1)}, u32[]{:S(2)}, u32[]{:S(2)}) collective-permute-start(bf16[128,512]{1,0:T(8,128)(2,1)} %get-tuple-element.29.w0), channel_id=1, source_target_pairs={{0,32},{16,48},{32,0},{48,16},{1,33},{17,49},{33,1},{49,17},{2,34}... | collective-permute-start | bytes 393224 | tf_op jit(solution)/shard_map/ppermute | solution.py:330
  52.2 7.1 %collective-permute-start.3 = (bf16[128,512]{1,0:T(8,128)(2,1)}, bf16[128,512]{1,0:T(8,128)(2,1)S(1)}, u32[]{:S(2)}, u32[]{:S(2)}) collective-permute-start(bf16[128,512]{1,0:T(8,128)(2,1)} %get-tuple-element.29.w0), channel_id=1, source_target_pairs={{0,48},{16,0},{32,16},{48,32},{1,49},{17,1},{33,17},{49,33},{2,50}... | collective-permute-start | bytes 393224 | tf_op jit(solution)/shard_map/ppermute | solution.py:330
  55.5 29.7 %copy-start.8 = (bf16[128,512]{1,0:T(8,128)(2,1)}, bf16[128,512]{1,0:T(8,128)(2,1)S(1)}, u32[]{:S(2)}) copy-start(bf16[128,512]{1,0:T(8,128)(2,1)S(1)} %collective-permute-done.5.w3) | copy-start | bytes 393220
  56.1 29.1 %copy-start.9 = (bf16[128,512]{1,0:T(8,128)(2,1)}, bf16[128,512]{1,0:T(8,128)(2,1)S(1)}, u32[]{:S(2)}) copy-start(bf16[128,512]{1,0:T(8,128)(2,1)S(1)} %collective-permute-done.4.w2) | copy-start | bytes 393220
  59.2 26.0 %copy-start.10 = (bf16[128,512]{1,0:T(8,128)(2,1)}, bf16[128,512]{1,0:T(8,128)(2,1)S(1)}, u32[]{:S(2)}) copy-start(bf16[128,512]{1,0:T(8,128)(2,1)S(1)} %collective-permute-done.3.w1) | copy-start | bytes 393220
  60.2 25.0 %collective-permute-start.6 = (bf16[512,512]{1,0:T(8,128)(2,1)S(1)}, bf16[512,512]{1,0:T(8,128)(2,1)S(1)}, u32[]{:S(2)}, u32[]{:S(2)}) collective-permute-start(bf16[512,512]{1,0:T(8,128)(2,1)S(1)} %pad_maximum_fusion), channel_id=1, source_target_pairs={{0,8},{8,0},{1,9},{9,1},{2,10},{10,2},{3,11},{11,3},{4,12},{12,4},... | collective-permute-start | bytes 1572872 | tf_op jit(solution)/shard_map/ppermute | solution.py:334
  62.2 16.1 %collective-permute-start.2 = (bf16[256,640]{1,0:T(8,128)(2,1)}, bf16[256,640]{1,0:T(8,128)(2,1)S(1)}, u32[]{:S(2)}, u32[]{:S(2)}) collective-permute-start(bf16[256,640]{1,0:T(8,128)(2,1)} %get-tuple-element.28.l0), channel_id=1, source_target_pairs={{0,1},{1,2},{2,3},{3,0},{4,5},{5,6},{6,7},{7,4},{8,9},{9,10},{10,1... | collective-permute-start | bytes 983048 | tf_op jit(solution)/shard_map/ppermute | solution.py:330
  65.7 18.2 %collective-permute-start.1 = (bf16[256,640]{1,0:T(8,128)(2,1)}, bf16[256,640]{1,0:T(8,128)(2,1)S(1)}, u32[]{:S(2)}, u32[]{:S(2)}) collective-permute-start(bf16[256,640]{1,0:T(8,128)(2,1)} %get-tuple-element.28.l0), channel_id=1, source_target_pairs={{0,2},{1,3},{2,0},{3,1},{4,6},{5,7},{6,4},{7,5},{8,10},{9,11},{10,... | collective-permute-start | bytes 983048 | tf_op jit(solution)/shard_map/ppermute | solution.py:330
  70.5 14.7 %collective-permute-start = (bf16[256,640]{1,0:T(8,128)(2,1)}, bf16[256,640]{1,0:T(8,128)(2,1)S(1)}, u32[]{:S(2)}, u32[]{:S(2)}) collective-permute-start(bf16[256,640]{1,0:T(8,128)(2,1)} %get-tuple-element.28.l0), channel_id=1, source_target_pairs={{0,3},{1,0},{2,1},{3,2},{4,7},{5,4},{6,5},{7,6},{8,11},{9,8},{10,9... | collective-permute-start | bytes 983048 | tf_op jit(solution)/shard_map/ppermute | solution.py:330
  78.3 7.0 %copy-start.12 = (bf16[256,640]{1,0:T(8,128)(2,1)}, bf16[256,640]{1,0:T(8,128)(2,1)S(1)}, u32[]{:S(2)}) copy-start(bf16[256,640]{1,0:T(8,128)(2,1)S(1)} %collective-permute-done.2.l3) | copy-start | bytes 983044
  99.0 12.9 %collective-permute-start.7 = (bf16[512,512]{1,0:T(8,128)(2,1)}, bf16[512,512]{1,0:T(8,128)(2,1)S(1)}, u32[]{:S(2)}, u32[]{:S(2)}) collective-permute-start(bf16[512,512]{1,0:T(8,128)(2,1)} %get-tuple-element.38), channel_id=1, source_target_pairs={{0,8},{8,0},{1,9},{9,1},{2,10},{10,2},{3,11},{11,3},{4,12},{12,4},... | collective-permute-start | bytes 1572872 | tf_op jit(solution)/shard_map/ppermute | solution.py:334
  101.0 20.8 %collective-permute-start.11 = (bf16[256,640]{1,0:T(8,128)(2,1)}, bf16[256,640]{1,0:T(8,128)(2,1)S(1)}, u32[]{:S(2)}, u32[]{:S(2)}) collective-permute-start(bf16[256,640]{1,0:T(8,128)(2,1)} %get-tuple-element.44), channel_id=1, source_target_pairs={{0,1},{1,2},{2,3},{3,0},{4,5},{5,6},{6,7},{7,4},{8,9},{9,10},{10,1... | collective-permute-start | bytes 983048 | tf_op jit(solution)/shard_map/ppermute | solution.py:330
  105.4 19.2 %collective-permute-start.12 = (bf16[256,640]{1,0:T(8,128)(2,1)}, bf16[256,640]{1,0:T(8,128)(2,1)S(1)}, u32[]{:S(2)}, u32[]{:S(2)}) collective-permute-start(bf16[256,640]{1,0:T(8,128)(2,1)} %get-tuple-element.45), channel_id=1, source_target_pairs={{0,3},{1,0},{2,1},{3,2},{4,7},{5,4},{6,5},{7,6},{8,11},{9,8},{10,9... | collective-permute-start | bytes 983048 | tf_op jit(solution)/shard_map/ppermute | solution.py:330
  108.0 16.5 %collective-permute-start.13 = (bf16[256,640]{1,0:T(8,128)(2,1)}, bf16[256,640]{1,0:T(8,128)(2,1)S(1)}, u32[]{:S(2)}, u32[]{:S(2)}) collective-permute-start(bf16[256,640]{1,0:T(8,128)(2,1)} %get-tuple-element.46), channel_id=1, source_target_pairs={{0,2},{1,3},{2,0},{3,1},{4,6},{5,7},{6,4},{7,5},{8,10},{9,11},{10,... | collective-permute-start | bytes 983048 | tf_op jit(solution)/shard_map/ppermute | solution.py:330
  114.7 9.9 %collective-permute-start.8 = (bf16[128,512]{1,0:T(8,128)(2,1)}, bf16[128,512]{1,0:T(8,128)(2,1)S(1)}, u32[]{:S(2)}, u32[]{:S(2)}) collective-permute-start(bf16[128,512]{1,0:T(8,128)(2,1)} %get-tuple-element.40), channel_id=1, source_target_pairs={{0,16},{16,32},{32,48},{48,0},{1,17},{17,33},{33,49},{49,1},{2,18}... | collective-permute-start | bytes 393224 | tf_op jit(solution)/shard_map/ppermute | solution.py:330
  116.8 7.8 %collective-permute-start.9 = (bf16[128,512]{1,0:T(8,128)(2,1)}, bf16[128,512]{1,0:T(8,128)(2,1)S(1)}, u32[]{:S(2)}, u32[]{:S(2)}) collective-permute-start(bf16[128,512]{1,0:T(8,128)(2,1)} %get-tuple-element.41), channel_id=1, source_target_pairs={{0,48},{16,0},{32,16},{48,32},{1,49},{17,1},{33,17},{49,33},{2,50}... | collective-permute-start | bytes 393224 | tf_op jit(solution)/shard_map/ppermute | solution.py:330
  121.8 8.6 %copy-start.2 = (bf16[256,640]{1,0:T(8,128)(2,1)}, bf16[256,640]{1,0:T(8,128)(2,1)S(1)}, u32[]{:S(2)}) copy-start(bf16[256,640]{1,0:T(8,128)(2,1)S(1)} %collective-permute-done.11.k1) | copy-start | bytes 983044
  121.8 8.6 %collective-permute-start.10 = (bf16[128,512]{1,0:T(8,128)(2,1)}, bf16[128,512]{1,0:T(8,128)(2,1)S(1)}, u32[]{:S(2)}, u32[]{:S(2)}) collective-permute-start(bf16[128,512]{1,0:T(8,128)(2,1)} %get-tuple-element.42), channel_id=1, source_target_pairs={{0,32},{16,48},{32,0},{48,16},{1,33},{17,49},{33,1},{49,17},{2,34}... | collective-permute-start | bytes 393224 | tf_op jit(solution)/shard_map/ppermute | solution.py:330
  124.6 5.8 %copy-start.3 = (bf16[256,640]{1,0:T(8,128)(2,1)}, bf16[256,640]{1,0:T(8,128)(2,1)S(1)}, u32[]{:S(2)}) copy-start(bf16[256,640]{1,0:T(8,128)(2,1)S(1)} %collective-permute-done.12.k2) | copy-start | bytes 983044
  124.6 5.8 %copy-start.4 = (bf16[256,640]{1,0:T(8,128)(2,1)}, bf16[256,640]{1,0:T(8,128)(2,1)S(1)}, u32[]{:S(2)}) copy-start(bf16[256,640]{1,0:T(8,128)(2,1)S(1)} %collective-permute-done.13.k3) | copy-start | bytes 983044
  124.6 5.8 %copy-start.5 = (bf16[128,512]{1,0:T(8,128)(2,1)}, bf16[128,512]{1,0:T(8,128)(2,1)S(1)}, u32[]{:S(2)}) copy-start(bf16[128,512]{1,0:T(8,128)(2,1)S(1)} %collective-permute-done.8.m1) | copy-start | bytes 393220
  124.6 5.8 %copy-start.6 = (bf16[128,512]{1,0:T(8,128)(2,1)}, bf16[128,512]{1,0:T(8,128)(2,1)S(1)}, u32[]{:S(2)}) copy-start(bf16[128,512]{1,0:T(8,128)(2,1)S(1)} %collective-permute-done.9.m2) | copy-start | bytes 393220
  165.3 33.0 %all-to-all-start.2 = ((bf16[8,32,640]{2,1,0:T(8,128)(2,1)}), bf16[8,32,640]{2,1,0:T(8,128)(2,1)S(1)}, u32[]{:S(2)}, u32[]{:S(2)}) async-start(bf16[8,32,640]{2,1,0:T(8,128)(2,1)} %get-tuple-element.47), calls=%async_computation.2 | async-start | bytes 655360 | tf_op jit(solution)/shard_map/all_to_all | solution.py:338
  (6 other events, 5.2 us)

commit v2 on v1

v2 whole, which is shorter than its diff:
```python
import math

import jax
import jax.numpy as jnp
from jax import lax
from jax.experimental import pallas as pl
from jax.experimental.pallas import tpu as pltpu
from jax.sharding import Mesh, PartitionSpec as P

RANKS = 8
HEADS = 8
HALF = 64
TOK = 128
DN = 128
DC = 512
DR = 64
WIDE = 640
BLOCK = 256
ROWS = HALF * HEADS
QUARTER = 32
WROWS = 16
FACTOR = 1.0 / math.sqrt(DN + DR)
LOG2E = 1.0 / math.log(2.0)
MASKED = -1e30
MIB = 1024 * 1024

bf16 = jnp.bfloat16
f32 = jnp.float32

AXES = ("zl", "x", "c", "zh", "y")
SEQ = ("zl", "x", "c")
HEAD = ("zh", "y")


def nn(a, b):
    return lax.dot_general(a, b, (((1,), (0,)), ((), ())), preferred_element_type=f32)


def nt(a, b):
    return lax.dot_general(a, b, (((1,), (1,)), ((), ())), preferred_element_type=f32)


def tn(a, b):
    return lax.dot_general(a, b, (((0,), (0,)), ((), ())), preferred_element_type=f32)


def iota(shape, axis):
    return lax.broadcasted_iota(jnp.int32, shape, axis)


def chosen(condition):
    return jnp.where(condition, 1.0, 0.0).astype(bf16)


def head_major():
    out, inp = iota((128, 128), 0), iota((128, 128), 1)
    return chosen(inp == (out % 16) * 8 + out // 16)


def token_major():
    out, inp = iota((128, 128), 0), iota((128, 128), 1)
    return chosen(inp == (out % 8) * 16 + out // 8)


def weight_order(row):
    x, c, rank, n = row // 32, (row // 16) % 2, (row % 16) // 2, row % 2
    return rank * 16 + x * 4 + c * 2 + n


FETCH = (((1, -3), (-1, 3), (2, -2), (4, None)), ((-1, 3), (1, -3), (2, -2), (-4, None)))


FOLD_X = (0, 3, 1, 2)
FOLD = (0, 4, 2, 6, 1, 5, 3, 7)


def call(body, outs, ins, scratch=(), flops=0, smem=(), hbm=(), name=None, vmem=6):
    nbytes = sum(math.prod(s.shape) * s.dtype.itemsize for s in list(outs) + list(ins))
    spaces = [
        pltpu.SMEM if i in smem else pltpu.HBM if i in hbm else pltpu.VMEM for i in range(len(ins))
    ]
    specs = [pl.BlockSpec(memory_space=space) for space in spaces]
    return pl.pallas_call(
        body,
        out_shape=outs,
        in_specs=specs,
        out_specs=[pl.BlockSpec(memory_space=pltpu.VMEM) for _ in outs],
        scratch_shapes=list(scratch),
        compiler_params=pltpu.CompilerParams(vmem_limit_bytes=vmem * MIB),
        cost_estimate=pl.CostEstimate(flops=flops, bytes_accessed=nbytes, transcendentals=0),
        name=name,
    )(*ins)


def shape(*dims, dtype=bf16):
    return jax.ShapeDtypeStruct(dims, dtype)


def prepare_kernel(
    lat_hbm,
    rot_hbm,
    codes_hbm,
    scale_hbm,
    pos_hbm,
    weight_out,
    pack_out,
    rot_ref,
    codes_ref,
    scale_ref,
    pos_ref,
    sems,
):
    pairs = (
        (codes_hbm, codes_ref),
        (scale_hbm, scale_ref),
        (pos_hbm, pos_ref),
        (rot_hbm, rot_ref),
        (lat_hbm, pack_out.at[:, 0:DC]),
    )
    copies = [pltpu.make_async_copy(src, dst, sems.at[i]) for i, (src, dst) in enumerate(pairs)]
    for copy in copies:
        copy.start()
    for copy in copies:
        copy.wait()
    codes = codes_ref[...]
    levels = codes + (16 * (codes >> 4) + 8) + (64 * (codes >> 6) + 32)
    row = iota((WROWS, DC), 0)
    scale = jnp.zeros((WROWS, DC), f32)
    for i in range(WROWS):
        scale = jnp.where(row == i, scale_ref[i // HEADS, i % HEADS], scale)
    weight = (scale * levels.astype(f32) / 3.0).astype(bf16)
    lane = iota((WROWS, 128), 1)
    run = [(pos_ref[half * HALF] >> 6).astype(f32) for half in range(2)]
    rest = jnp.where(lane == 0, run[0], jnp.where(lane == 1, run[1], 0.0)).astype(bf16)
    for r in range(RANKS):
        weight_out[r, :, 0:DC] = weight
        weight_out[r, :, DC:WIDE] = rest
    widen = chosen(iota((DR, 128), 0) == iota((DR, 128), 1))
    pack_out[:, DC:WIDE] = tn(rot_ref[...], widen).astype(bf16)


def spread_weight_kernel(in_ref, out_ref):
    out, inp = iota((128, 128), 0), iota((128, 128), 1)
    head, rank, n = out // 16, (out % 16) // 2, out % 2
    weight = nn(chosen(inp == rank * 16 + n * 8 + head), in_ref[:, 0:DC]).astype(bf16)
    for i in range(8):
        out_ref[i] = weight


def join_kernel(first, second, out_ref):
    out_ref[0:TOK, :] = first[...]
    out_ref[TOK : 2 * TOK, :] = second[...]


def order_queries(nope_ref, rot_ref, up_ref, nope_out, query, up_out):
    by_head = head_major()
    inp, out = iota((DN, DN), 0), iota((DN, DN), 1)
    reorder = chosen(inp == weight_order(out))
    for g in range(TOK // 16):
        half, start = g // 4, (g % 4) * 16
        rows = slice(g * 128, (g + 1) * 128)
        nope = nn(nn(by_head, nope_ref[rows, :]).astype(bf16), reorder).astype(bf16)
        up = nn(by_head, up_ref[rows, :]).astype(bf16)
        for h in range(HEADS):
            place = (half * HEADS + h) * HALF + start
            nope_out[place : place + 16, :] = nope[h * 16 : (h + 1) * 16, :]
            up_out[place : place + 16, :] = up[h * 16 : (h + 1) * 16, :]
    for h in range(HEADS):
        pick = chosen((inp == out + DR * (h % 2)) & (out < DR))
        turned = nn(rot_ref[:, (h // 2) * 128 : (h // 2 + 1) * 128], pick).astype(bf16)
        for half in range(2):
            place = (half * HEADS + h) * HALF
            query[place : place + HALF, DC:WIDE] = turned[half * HALF : (half + 1) * HALF, :]


def attention_kernel(
    runs_ref,
    pos_ref,
    pack_ref,
    l0,
    l1,
    l2,
    l3,
    w_ref,
    nope_in,
    rot_in,
    up_in,
    k0,
    k1,
    k2,
    k3,
    own_out,
    other_out,
    dq_ref,
    weight_ref,
    keys,
    query,
    score,
    slope,
    dkey,
    dquery,
    nope_ref,
    up_ref,
    staged,
):
    order_queries(nope_in, rot_in, up_in, nope_ref, query, up_ref)
    zl, c, y = lax.axis_index("zl"), lax.axis_index("c"), lax.axis_index("y")
    x = lax.axis_index("x")

    def place_of(run, start, size):
        return pl.ds(pl.multiple_of(run * HALF + start, size), size)

    for half in range(2):
        run = pos_ref[half * HALF] >> 6
        keys[place_of(run, 0, HALF), :] = pack_ref[half * HALF : (half + 1) * HALF, :]
    for step, part in enumerate((l0, l1, l2, l3)):
        source = (y + step) % 4
        for slot in range(2):
            away = jnp.int32(0)
            for core in range(2):
                for owner in range(4):
                    here = (c == core) & (source == owner)
                    away = jnp.where(here, FETCH[core][owner][slot] or 0, away)

            @pl.when(away != 0)
            def _():
                rank = (zl + RANKS + away) % RANKS
                for half in range(2):
                    run = runs_ref[rank * 2 + half]
                    start = slot * TOK + half * HALF
                    keys[place_of(run, 0, HALF), :] = part[start : start + HALF, :]

    for h in range(HEADS):
        for i in range(8):
            weight_ref[h * DN + i * 16 : h * DN + i * 16 + 16, :] = w_ref[i, h * 16 : h * 16 + 16, :]
    for h in range(HEADS):
        pair = [nope_ref[(half * HEADS + h) * HALF : (half * HEADS + h + 1) * HALF, :] for half in range(2)]
        absorbed = nn(jnp.concatenate(pair, axis=0), weight_ref[h * DN : (h + 1) * DN, :])
        for half in range(2):
            at = (half * HEADS + h) * HALF
            query[at : at + HALF, 0:DC] = absorbed[half * HALF : (half + 1) * HALF, :].astype(bf16)
    dkey[...] = jnp.zeros_like(dkey)

    for half in range(2):
        rows = slice(half * ROWS, (half + 1) * ROWS)
        run = pos_ref[half * HALF] >> 6
        place = run * HALF + iota((1, ROWS), 1) % HALF
        count = run // 4 + 1

        def scores(j, top):
            at = pl.ds(pl.multiple_of(j * BLOCK, BLOCK), BLOCK)
            part = keys[at, :]
            s = nt(part, query[rows, :]) * (FACTOR * LOG2E)
            s = jnp.where(j * BLOCK + iota((BLOCK, ROWS), 0) <= place, s, MASKED)
            score[j] = s
            slope[j] = nt(part[:, 0:DC], up_ref[rows, :])
            return jnp.maximum(top, jnp.max(s, axis=0, keepdims=True))

        top = lax.fori_loop(0, count, scores, jnp.full((1, ROWS), MASKED, f32))

        def totals(j, running):
            total, weighted = running
            e = jnp.exp2(score[j] - top)
            score[j] = e
            return (
                total + jnp.sum(e, axis=0, keepdims=True),
                weighted + jnp.sum(e * slope[j], axis=0, keepdims=True),
            )

        zero = jnp.zeros((1, ROWS), f32)
        total, weighted = lax.fori_loop(0, count, totals, (zero, zero))
        inverse = 1.0 / total
        inner = weighted * inverse
        dquery[...] = jnp.zeros_like(dquery)

        def grads(j, carry):
            at = pl.ds(pl.multiple_of(j * BLOCK, BLOCK), BLOCK)
            prob = score[j] * inverse
            grad = (prob * (slope[j] - inner) * FACTOR).astype(bf16)
            dquery[...] += tn(grad, keys[at, :])
            dkey[at, :] += nn(grad, query[rows, :])
            dkey[at, 0:DC] += nn(prob.astype(bf16), up_ref[rows, :])
            return carry

        lax.fori_loop(0, count, grads, 0)
        dq_ref[rows, :] = dquery[...].astype(bf16)

    for step, part in enumerate((k0, k1, k2, k3)):
        quarter = (y + step) % 4
        for k in range(RANKS):
            run = runs_ref[(zl ^ FOLD[k]) * 2 + quarter // 2]
            at = place_of(run, (quarter % 2) * QUARTER, QUARTER)
            part[k * QUARTER : (k + 1) * QUARTER, :] = dkey[at, :].astype(bf16)
    for h in range(HEADS):
        places = [slice((half * HEADS + h) * HALF, (half * HEADS + h + 1) * HALF) for half in range(2)]
        nope = jnp.concatenate([nope_ref[p, :] for p in places], axis=0)
        dq = jnp.concatenate([dq_ref[p, 0:DC] for p in places], axis=0)
        master = tn(nope, dq).astype(bf16)
        staged[...] = master
        for core, part in enumerate((own_out, other_out)):
            for k, away in enumerate(FOLD_X):
                at = pl.ds(pl.multiple_of(((x ^ away) * 2 + (c + core) % 2) * 16, 16), 16)
                part[k * 128 + h * 16 : k * 128 + h * 16 + 16, :] = staged[at, :]


def query_grads_kernel(dq_ref, weight_ref, nope_out, rot_out, scratch):
    out, inp = iota((DN, DN), 1), iota((DN, DN), 0)
    reorder = chosen(out == weight_order(inp))
    i, j = iota((128, 128), 0), iota((128, 128), 1)
    left = chosen((i == j) & (j < DR))
    right = chosen((i == j - DR) & (i < DR))
    for h in range(HEADS):
        places = [slice((half * HEADS + h) * HALF, (half * HEADS + h + 1) * HALF) for half in range(2)]
        dq = jnp.concatenate([dq_ref[p, 0:DC] for p in places], axis=0)
        grad = nt(dq, weight_ref[h * DN : (h + 1) * DN, :]).astype(bf16)
        scratch[h * TOK : (h + 1) * TOK, :] = nn(grad, reorder).astype(bf16)
    by_token = token_major()
    for g in range(TOK // 16):
        rows = [scratch[h * TOK + g * 16 : h * TOK + g * 16 + 16, :] for h in range(HEADS)]
        nope_out[g * 128 : (g + 1) * 128, :] = nn(by_token, jnp.concatenate(rows, axis=0)).astype(bf16)
    for p in range(HEADS // 2):
        sides = []
        for h in (2 * p, 2 * p + 1):
            places = [slice((half * HEADS + h) * HALF, (half * HEADS + h + 1) * HALF) for half in range(2)]
            sides.append(jnp.concatenate([dq_ref[q, DC:WIDE] for q in places], axis=0))
        rot_out[:, p * 128 : (p + 1) * 128] = (nn(sides[0], left) + nn(sides[1], right)).astype(bf16)


def total_of(parts):
    total = parts[0].astype(f32)
    for part in parts[1:]:
        total = total + part.astype(f32)
    return total


def keys_plane_kernel(k0, k1, k2, k3, keep_ref, send_ref):
    total = total_of([k[...] for k in (k0, k1, k2, k3)])
    keep_ref[...] = total[0:128, :]
    send_ref[...] = total[128:256, :].astype(bf16)


def keys_pair_kernel(keep_ref, got_ref, both_out):
    both_out[...] = (keep_ref[...] + got_ref[...].astype(f32)).astype(bf16)


def keys_cross_kernel(both_ref, got_ref, keep_out, send_out):
    low, high = slice(0, QUARTER), slice(QUARTER, 2 * QUARTER)
    keep_out[...] = total_of([both_ref[low, :], got_ref[high, :]]).astype(bf16)
    send_out[...] = total_of([both_ref[high, :], got_ref[low, :]]).astype(bf16)


def keys_sum_kernel(keep_ref, got_ref, out_ref):
    keys = total_of([keep_ref[...], got_ref[...]]).astype(bf16)
    for y in range(4):
        out_ref[y] = keys


def keys_last_kernel(in_ref, latent_ref, rotary_ref):
    rest = []
    for y in range(4):
        part = in_ref[y].astype(f32)
        latent_ref[y * QUARTER : (y + 1) * QUARTER, :] = part[:, 0:DC]
        rest.append(part[:, DC:WIDE])
    rotary_ref[...] = jnp.concatenate(rest, axis=0).T[0:DR, :]


def master_plane_kernel(own_ref, got_ref, keep_ref, send_ref):
    total = own_ref[...].astype(f32) + got_ref[...].astype(f32)
    keep_ref[...] = total[0:256, :]
    send_ref[...] = total[256:512, :].astype(bf16)


def master_order_kernel(keep_ref, got_ref, keep_out, send_out):
    master = (keep_ref[...] + got_ref[...].astype(f32)).astype(bf16)
    zl = lax.axis_index("zl")
    out, inp = iota((128, 128), 0), iota((128, 128), 1)
    k, n, head = out // 16, (out % 16) // 8, out % 8
    rank = zl ^ ((k % 2) * 4 + ((k // 2) % 2) * 2 + k // 4)
    master = nn(chosen(inp == head * 16 + rank * 2 + n), master)
    keep_out[...] = master[0:64, :]
    send_out[...] = master[64:128, :].astype(bf16)


def fold_kernel(keep_ref, got_ref, keep_out, send_out):
    size = keep_out.shape[0]
    keep_out[...] = keep_ref[0:size, :] + got_ref[0:size, :].astype(f32)
    send_out[...] = (keep_ref[size:, :] + got_ref[size:, :].astype(f32)).astype(bf16)


def master_last_kernel(keep_ref, got_ref, out_ref):
    out_ref[...] = keep_ref[...] + got_ref[...].astype(f32)


def fetch(block, slot):
    axes, sizes = ("zl", "c", "zh", "y"), (8, 2, 2, 4)
    pairs = []
    for place in range(16):
        for c in range(2):
            for y in range(4):
                step = FETCH[c][y][slot]
                if step is not None:
                    ends = []
                    for z in ((place + step) % 16, place):
                        ends.append((((z % 8) * 2 + c) * 2 + z // 8) * 4 + y)
                    pairs.append(tuple(ends))
    return lax.ppermute(block, axes, pairs)


def shift(block, axis, step):
    n = lax.axis_size(axis)
    return lax.ppermute(block, axis, [(i, (i + step) % n) for i in range(n)])


def across(block, axis, step):
    n = lax.axis_size(axis)
    return lax.ppermute(block, axis, [(i, i ^ step) for i in range(n)])


def over_edge(block):
    def partner(place):
        return (place + (4 if place % 8 >= 4 else -4)) % 16

    def index(place):
        return place % 8 * 2 + place // 8

    return lax.ppermute(block, ("zl", "zh"), [(index(p), index(partner(p))) for p in range(16)])


def everyone(blocks, axes):
    return lax.all_to_all(blocks, axes, 0, 0, tiled=True)


def shards(nope, rotary, latent, keys, upstream, codes, scale, positions):
    weight_send, pack = call(
        prepare_kernel,
        (shape(RANKS, WROWS, WIDE), shape(TOK, WIDE)),
        (latent, keys.T, codes.reshape(WROWS, DC), scale, positions),
        scratch=(
            pltpu.VMEM((DR, TOK), bf16),
            pltpu.VMEM((WROWS, DC), jnp.int32),
            pltpu.SMEM((2, HEADS), f32),
            pltpu.SMEM((TOK,), jnp.int32),
            pltpu.SemaphoreType.DMA((5,)),
        ),
        hbm=(0, 1, 2, 3, 4),
        name="prepare",
        vmem=56,
    )
    weight_ranks = everyone(weight_send, "zl")
    first, second = fetch(pack, 0), fetch(pack, 1)
    weight_ranks, first, second = lax.optimization_barrier((weight_ranks, first, second))
    (weight_spread,) = call(
        spread_weight_kernel,
        (shape(8, 128, DC),),
        (weight_ranks.reshape(128, WIDE),),
        name="spread_weight",
    )
    weight_all = everyone(weight_spread, ("x", "c"))
    (joined,) = call(join_kernel, (shape(2 * TOK, WIDE),), (first, second), name="join")
    lat = [joined] + [shift(joined, "y", -step) for step in (1, 2, 3)]
    runs = weight_ranks[:, 0, DC : DC + 2].astype(jnp.int32).reshape(16)
    k0, k1, k2, k3, own, other, dq, weight = call(
        attention_kernel,
        (shape(256, WIDE),) * 4 + (shape(512, DC),) * 2 + (shape(1024, WIDE), shape(1024, DC)),
        (
            runs,
            positions,
            pack,
            *lat,
            weight_all,
            nope.reshape(1024, DN),
            rotary,
            upstream.reshape(1024, DC),
        ),
        scratch=(
            pltpu.VMEM((1024, WIDE), bf16),
            pltpu.VMEM((1024, WIDE), bf16),
            pltpu.VMEM((4, BLOCK, ROWS), f32),
            pltpu.VMEM((4, BLOCK, ROWS), f32),
            pltpu.VMEM((1024, WIDE), f32),
            pltpu.VMEM((ROWS, WIDE), f32),
            pltpu.VMEM((1024, DN), bf16),
            pltpu.VMEM((1024, DC), bf16),
            pltpu.VMEM((DN, DC), bf16),
        ),
        smem=(0, 1),
        flops=2 * 512 * 1280 * 2944,
        name="attention",
        vmem=56,
    )
    k = [k0] + [shift(part, "y", step) for step, part in ((1, k1), (2, k2), (3, k3))]
    other = across(other, "c", 1)
    nope_grad, rot_grad = call(
        query_grads_kernel,
        (shape(1024, DN), shape(TOK, HEADS * DR)),
        (dq, weight),
        scratch=(pltpu.VMEM((1024, DN), bf16),),
        flops=2 * 1024 * 128 * 768,
        name="query_grads",
    )
    def folded(body, size, width, ins, dtype=f32, name="fold"):
        return call(body, (shape(size, width, dtype=dtype), shape(size, width)), ins, name=name)

    together = lax.optimization_barrier
    mkeep, send = folded(master_plane_kernel, 256, DC, (own, other), name="master_plane")
    got = across(send, "x", 1)
    keep, send = folded(keys_plane_kernel, 128, WIDE, k, name="keys_plane")
    got, mgot = together((across(send, "zl", 1), got))
    mkeep, msend = folded(fold_kernel, 128, DC, (mkeep, mgot))
    keep, send = folded(fold_kernel, 64, WIDE, (keep, got))
    got, mgot = together((across(send, "zl", 2), across(msend, "x", 3)))
    mkeep, msend = folded(master_order_kernel, 64, DC, (mkeep, mgot), name="master_order")
    (both,) = call(keys_pair_kernel, (shape(64, WIDE),), (keep, got), name="keys_pair")
    got, mgot = together((across(both, "zl", 4), across(msend, "zl", 1)))
    mkeep, msend = folded(fold_kernel, 32, DC, (mkeep, mgot))
    keep, send = folded(keys_cross_kernel, QUARTER, WIDE, (both, got), dtype=bf16, name="keys_cross")
    got, mgot = together((over_edge(send), across(msend, "zl", 2)))
    mkeep, msend = folded(fold_kernel, 16, DC, (mkeep, mgot))
    (dkey_sum,) = call(keys_sum_kernel, (shape(4, QUARTER, WIDE),), (keep, got), name="keys_sum")
    dkey_all, mgot = together((everyone(dkey_sum, "y"), across(msend, "zl", 4)))
    (master_grad,) = call(
        master_last_kernel, (shape(WROWS, DC, dtype=f32),), (mkeep, mgot), name="master_last"
    )
    latent_grad, keys_grad = call(
        keys_last_kernel,
        (shape(TOK, DC, dtype=f32), shape(DR, TOK, dtype=f32)),
        (dkey_all,),
        name="keys_last",
    )
    return (
        nope_grad.reshape(TOK, HEADS, DN),
        rot_grad,
        latent_grad,
        keys_grad.T,
        master_grad.reshape(2, HEADS, DC),
    )


def solution(mesh):
    fine = Mesh(mesh.devices.reshape(8, 4, 2, 2, 4), AXES)
    in_specs = (
        P(SEQ, HEAD, None),
        P(SEQ, HEAD),
        P(SEQ, None),
        P(SEQ, None),
        P(SEQ, HEAD, None),
        P(SEQ, HEAD, None),
        P(SEQ, HEAD),
        P(SEQ),
    )
    out_specs = (
        P(SEQ, HEAD, None),
        P(SEQ, HEAD),
        P(SEQ, None),
        P(SEQ, None),
        P(SEQ, HEAD, None),
    )
    return jax.shard_map(shards, mesh=fine, in_specs=in_specs, out_specs=out_specs, check_vma=False)
```

time: 203 us -> 168 us (0.83)
  the two profiles are of different devices: /device:TPU:32 before, /device:TPU:40 now
where the time goes in v2:
time: 168 us; the launch traced here: 167 us
  starting transfers between devices  94.2 us (56%)
  waiting for transfers between devices  46 us (27%)
  Pallas kernels  21.8 us (13%)
  local copies, waits for them, and re-layouts  3.69 us (2%)
    ppermute x9, starting transfers between devices, across(): return lax.ppermute(block, axis, [(i, i ^ step) for i in range(n)])  29.8 us
    ppermute x6, starting transfers between devices, shift(): return lax.ppermute(block, axis, [(i, (i + step) % n) for i in range(n)])  23.9 us
    all_to_all x3, starting transfers between devices, everyone(): return lax.all_to_all(blocks, axes, 0, 0, tiled=True)  22.8 us
    ppermute x9, waiting for transfers between devices, across(): return lax.ppermute(block, axis, [(i, i ^ step) for i in range(n)])  22.1 us
    pallas_call x17, Pallas kernels, call(): pl.pallas_call(body, out_shape=outs, in_specs=specs, out_specs=[pl.BlockS...  21.8 us
    ppermute x6, waiting for transfers between devices, shift(): return lax.ppermute(block, axis, [(i, (i + step) % n) for i in range(n)])  19.7 us
    ppermute x2, starting transfers between devices, fetch(): return lax.ppermute(block, axes, pairs)  11.6 us
    ppermute x1, starting transfers between devices, over_edge(): lax.ppermute(block, ('zl', 'zh'), [(index(p), index(partner(p))) for p in...  6.15 us
  transfers between devices with their start and end apart: 21, of which 12 were waited for; matrix products, arithmetic and copies ran while one was open for 0% of the time, Pallas kernels for 2%

profile of v2, /device:TPU:40, one launch (start us, length us, event | category | flops | bytes accessed | tf_op | source)
XLA Modules:
  0.0 166.6 jit_solution(8257081059948799417)
XLA Ops:
  2.5 12.6 %all-to-all-start = ((bf16[8,16,640]{2,1,0:T(8,128)(2,1)}), bf16[8,16,640]{2,1,0:T(8,128)(2,1)S(1)}, u32[]{:S(2)}, u32[]{:S(2)}) async-start(bf16[8,16,640]{2,1,0:T(8,128)(2,1)} %get-tuple-element.48), calls=%async_computation | async-start | bytes 327680 | tf_op jit(solution)/shard_map/all_to_all | solution.py:430
  15.1 8.2 %collective-permute-start.1 = (bf16[128,640]{1,0:T(8,128)(2,1)}, bf16[128,640]{1,0:T(8,128)(2,1)S(1)}, u32[]{:S(2)}, u32[]{:S(2)}) collective-permute-start(bf16[128,640]{1,0:T(8,128)(2,1)} %get-tuple-element.49.pack_ref), channel_id=1, source_target_pairs={{324,0},{193,1},{390,2},{200,8},{333,9},{398,10},{388,64},{257,65}... | collective-permute-start | bytes 491528 | tf_op jit(solution)/shard_map/ppermute | solution.py:406
  23.3 3.4 %collective-permute-start = (bf16[128,640]{1,0:T(8,128)(2,1)}, bf16[128,640]{1,0:T(8,128)(2,1)S(1)}, u32[]{:S(2)}, u32[]{:S(2)}) collective-permute-start(bf16[128,640]{1,0:T(8,128)(2,1)} %get-tuple-element.49.pack_ref), channel_id=1, source_target_pairs={{64,0},{453,1},{130,2},{259,3},{460,8},{73,9},{138,10},{271,11},{1... | collective-permute-start | bytes 491528 | tf_op jit(solution)/shard_map/ppermute | solution.py:406
  32.2 4.7 %all-to-all-start.1 = ((bf16[8,128,512]{2,1,0:T(8,128)(2,1)}), bf16[8,128,512]{2,1,0:T(8,128)(2,1)S(1)}, u32[]{:S(2)}, u32[]{:S(2)}) async-start(bf16[8,128,512]{2,1,0:T(8,128)(2,1)} %spread_weight.1), calls=%async_computation.1 | async-start | bytes 2097152 | tf_op jit(solution)/shard_map/all_to_all | solution.py:430
  37.0 5.7 %collective-permute-start.4 = (bf16[256,640]{1,0:T(8,128)(2,1)S(1)}, bf16[256,640]{1,0:T(8,128)(2,1)S(1)}, u32[]{:S(2)}, u32[]{:S(2)}) collective-permute-start(bf16[256,640]{1,0:T(8,128)(2,1)S(1)} %join.1.l0), channel_id=1, source_target_pairs={{0,1},{1,2},{2,3},{3,0},{4,5},{5,6},{6,7},{7,4},{8,9},{9,10},{10,1... | collective-permute-start | bytes 983048 | tf_op jit(solution)/shard_map/ppermute | solution.py:411
  42.7 3.4 %collective-permute-start.3 = (bf16[256,640]{1,0:T(8,128)(2,1)S(1)}, bf16[256,640]{1,0:T(8,128)(2,1)S(1)}, u32[]{:S(2)}, u32[]{:S(2)}) collective-permute-start(bf16[256,640]{1,0:T(8,128)(2,1)S(1)} %join.1.l0), channel_id=1, source_target_pairs={{0,2},{1,3},{2,0},{3,1},{4,6},{5,7},{6,4},{7,5},{8,10},{9,11},{10,... | collective-permute-start | bytes 983048 | tf_op jit(solution)/shard_map/ppermute | solution.py:411
  46.1 4.5 %collective-permute-start.2 = (bf16[256,640]{1,0:T(8,128)(2,1)S(1)}, bf16[256,640]{1,0:T(8,128)(2,1)S(1)}, u32[]{:S(2)}, u32[]{:S(2)}) collective-permute-start(bf16[256,640]{1,0:T(8,128)(2,1)S(1)} %join.1.l0), channel_id=1, source_target_pairs={{0,3},{1,0},{2,1},{3,2},{4,7},{5,4},{6,5},{7,6},{8,11},{9,8},{10,9... | collective-permute-start | bytes 983048 | tf_op jit(solution)/shard_map/ppermute | solution.py:411
  51.3 6.1 %collective-permute-done.4.l3 = bf16[256,640]{1,0:T(8,128)(2,1)S(1)} collective-permute-done((bf16[256,640]{1,0:T(8,128)(2,1)S(1)}, bf16[256,640]{1,0:T(8,128)(2,1)S(1)}, u32[]{:S(2)}, u32[]{:S(2)}) %collective-permute-start.4) | collective-permute-done | bytes 327712 | tf_op jit(solution)/shard_map/ppermute | solution.py:411
  57.4 5.6 %collective-permute-done.2.l1 = bf16[256,640]{1,0:T(8,128)(2,1)S(1)} collective-permute-done((bf16[256,640]{1,0:T(8,128)(2,1)S(1)}, bf16[256,640]{1,0:T(8,128)(2,1)S(1)}, u32[]{:S(2)}, u32[]{:S(2)}) %collective-permute-start.2) | collective-permute-done | bytes 327712 | tf_op jit(solution)/shard_map/ppermute | solution.py:411
  64.1 13.8 %attention.1 = (bf16[256,640]{1,0:T(8,128)(2,1)}, bf16[256,640]{1,0:T(8,128)(2,1)}, bf16[256,640]{1,0:T(8,128)(2,1)}, bf16[256,640]{1,0:T(8,128)(2,1)}, bf16[512...) custom-call(s32[16]{0:T(128)} %reshape.38.runs_ref, ...), custom_call_target="tpu_custom_call" | custom-call | flops 3858759680 | bytes 8684096 | tf_op jit(solution)/shard_map/attention/pallas_call | solution.py:83
  82.3 3.7 %collective-permute-start.6 = (bf16[256,640]{1,0:T(8,128)(2,1)}, bf16[256,640]{1,0:T(8,128)(2,1)S(1)}, u32[]{:S(2)}, u32[]{:S(2)}) collective-permute-start(bf16[256,640]{1,0:T(8,128)(2,1)} %get-tuple-element.59), channel_id=1, source_target_pairs={{0,2},{1,3},{2,0},{3,1},{4,6},{5,7},{6,4},{7,5},{8,10},{9,11},{10,... | collective-permute-start | bytes 983048 | tf_op jit(solution)/shard_map/ppermute | solution.py:411
  86.0 4.0 %collective-permute-start.7 = (bf16[256,640]{1,0:T(8,128)(2,1)}, bf16[256,640]{1,0:T(8,128)(2,1)S(1)}, u32[]{:S(2)}, u32[]{:S(2)}) collective-permute-start(bf16[256,640]{1,0:T(8,128)(2,1)} %get-tuple-element.60), channel_id=1, source_target_pairs={{0,3},{1,0},{2,1},{3,2},{4,7},{5,4},{6,5},{7,6},{8,11},{9,8},{10,9... | collective-permute-start | bytes 983048 | tf_op jit(solution)/shard_map/ppermute | solution.py:411
  91.1 3.6 %collective-permute-start.10 = (bf16[256,512]{1,0:T(8,128)(2,1)S(1)}, bf16[256,512]{1,0:T(8,128)(2,1)S(1)}, u32[]{:S(2)}, u32[]{:S(2)}) collective-permute-start(bf16[256,512]{1,0:T(8,128)(2,1)S(1)} %get-tuple-element.65), channel_id=1, source_target_pairs={{0,16},{16,0},{32,48},{48,32},{1,17},{17,1},{33,49},{49,33},{2,18}... | collective-permute-start | bytes 786440 | tf_op jit(solution)/shard_map/ppermute | solution.py:416
  96.5 6.3 %collective-permute-done.7.k3 = bf16[256,640]{1,0:T(8,128)(2,1)S(1)} collective-permute-done((bf16[256,640]{1,0:T(8,128)(2,1)}, bf16[256,640]{1,0:T(8,128)(2,1)S(1)}, u32[]{:S(2)}, u32[]{:S(2)}) %collective-permute-start.7) | collective-permute-done | bytes 327712 | tf_op jit(solution)/shard_map/ppermute | solution.py:411
  105.8 6.1 %collective-permute-done.8.got_ref = bf16[128,640]{1,0:T(8,128)(2,1)S(1)} collective-permute-done((bf16[128,640]{1,0:T(8,128)(2,1)S(1)}, bf16[128,640]{1,0:T(8,128)(2,1)S(1)}, u32[]{:S(2)}, u32[]{:S(2)}) %collective-permute-start.8) | collective-permute-done | bytes 163872 | tf_op jit(solution)/shard_map/ppermute | solution.py:416
  112.0 4.9 %collective-permute-start.12 = (bf16[128,512]{1,0:T(8,128)(2,1)S(1)}, bf16[128,512]{1,0:T(8,128)(2,1)S(1)}, u32[]{:S(2)}, u32[]{:S(2)}) collective-permute-start(bf16[128,512]{1,0:T(8,128)(2,1)S(1)} %get-tuple-element.71), channel_id=1, source_target_pairs={{0,48},{16,32},{32,16},{48,0},{1,49},{17,33},{33,17},{49,1},{2,50}... | collective-permute-start | bytes 393224 | tf_op jit(solution)/shard_map/ppermute | solution.py:416
  116.9 3.7 %collective-permute-start.11 = (bf16[64,640]{1,0:T(8,128)(2,1)S(1)}, bf16[64,640]{1,0:T(8,128)(2,1)S(1)}, u32[]{:S(2)}, u32[]{:S(2)}) collective-permute-start(bf16[64,640]{1,0:T(8,128)(2,1)S(1)} %get-tuple-element.68), channel_id=1, source_target_pairs={{0,128},{64,192},{128,0},{192,64},{256,384},{320,448},{384,256},{4... | collective-permute-start | bytes 245768 | tf_op jit(solution)/shard_map/ppermute | solution.py:416
  120.7 3.5 %collective-permute-done.11.got_ref = bf16[64,640]{1,0:T(8,128)(2,1)S(1)} collective-permute-done((bf16[64,640]{1,0:T(8,128)(2,1)S(1)}, bf16[64,640]{1,0:T(8,128)(2,1)S(1)}, u32[]{:S(2)}, u32[]{:S(2)}) %collective-permute-start.11) | collective-permute-done | bytes 81952 | tf_op jit(solution)/shard_map/ppermute | solution.py:416
  124.2 4.6 %collective-permute-start.13 = (bf16[64,640]{1,0:T(8,128)(2,1)S(1)}, bf16[64,640]{1,0:T(8,128)(2,1)S(1)}, u32[]{:S(2)}, u32[]{:S(2)}) collective-permute-start(bf16[64,640]{1,0:T(8,128)(2,1)S(1)} %keys_pair.1.both_ref), channel_id=1, source_target_pairs={{0,256},{64,320},{128,384},{192,448},{256,0},{320,64},{384,128},{4... | collective-permute-start | bytes 245768 | tf_op jit(solution)/shard_map/ppermute | solution.py:416
  131.2 4.0 %collective-permute-done.14.got_ref = bf16[64,512]{1,0:T(8,128)(2,1)S(1)} collective-permute-done((bf16[64,512]{1,0:T(8,128)(2,1)S(1)}, bf16[64,512]{1,0:T(8,128)(2,1)S(1)}, u32[]{:S(2)}, u32[]{:S(2)}) %collective-permute-start.14) | collective-permute-done | bytes 65568 | tf_op jit(solution)/shard_map/ppermute | solution.py:416
  136.7 6.1 %collective-permute-start.15 = (bf16[32,640]{1,0:T(8,128)(2,1)S(1)}, bf16[32,640]{1,0:T(8,128)(2,1)S(1)}, u32[]{:S(2)}, u32[]{:S(2)}) collective-permute-start(bf16[32,640]{1,0:T(8,128)(2,1)S(1)} %get-tuple-element.78), channel_id=1, source_target_pairs={{0,260},{64,324},{128,388},{192,452},{256,4},{320,68},{384,132},{4... | collective-permute-start | bytes 122888 | tf_op jit(solution)/shard_map/ppermute | solution.py:426
  142.9 4.2 %collective-permute-start.16 = (bf16[32,512]{1,0:T(8,128)(2,1)S(1)}, bf16[32,512]{1,0:T(8,128)(2,1)S(1)}, u32[]{:S(2)}, u32[]{:S(2)}) collective-permute-start(bf16[32,512]{1,0:T(8,128)(2,1)S(1)} %get-tuple-element.81), channel_id=1, source_target_pairs={{0,128},{64,192},{128,0},{192,64},{256,384},{320,448},{384,256},{4... | collective-permute-start | bytes 98312 | tf_op jit(solution)/shard_map/ppermute | solution.py:416
  150.3 5.4 %all-to-all-start.2 = ((bf16[4,32,640]{2,1,0:T(8,128)(2,1)}), bf16[4,32,640]{2,1,0:T(8,128)(2,1)S(1)}, u32[]{:S(2)}, u32[]{:S(2)}) async-start(bf16[4,32,640]{2,1,0:T(8,128)(2,1)} %keys_sum.1), calls=%async_computation.2 | async-start | bytes 327680 | tf_op jit(solution)/shard_map/all_to_all | solution.py:430
  160.7 4.5 %collective-permute-done.17.got_ref = bf16[16,512]{1,0:T(8,128)(2,1)S(1)} collective-permute-done((bf16[16,512]{1,0:T(8,128)(2,1)S(1)}, bf16[16,512]{1,0:T(8,128)(2,1)S(1)}, u32[]{:S(2)}, u32[]{:S(2)}) %collective-permute-start.17) | collective-permute-done | bytes 16416 | tf_op jit(solution)/shard_map/ppermute | solution.py:416
  (55 shorter events, 33.0 us)
Async XLA Ops:
  2.5 28.5 %all-to-all-start = ((bf16[8,16,640]{2,1,0:T(8,128)(2,1)}), bf16[8,16,640]{2,1,0:T(8,128)(2,1)S(1)}, u32[]{:S(2)}, u32[]{:S(2)}) async-start(bf16[8,16,640]{2,1,0:T(8,128)(2,1)} %get-tuple-element.48), calls=%async_computation | async-start | bytes 327680 | tf_op jit(solution)/shard_map/all_to_all | solution.py:430
  15.1 14.4 %collective-permute-start.1 = (bf16[128,640]{1,0:T(8,128)(2,1)}, bf16[128,640]{1,0:T(8,128)(2,1)S(1)}, u32[]{:S(2)}, u32[]{:S(2)}) collective-permute-start(bf16[128,640]{1,0:T(8,128)(2,1)} %get-tuple-element.49.pack_ref), channel_id=1, source_target_pairs={{324,0},{193,1},{390,2},{200,8},{333,9},{398,10},{388,64},{257,65}... | collective-permute-start | bytes 491528 | tf_op jit(solution)/shard_map/ppermute | solution.py:406
  23.3 7.6 %collective-permute-start = (bf16[128,640]{1,0:T(8,128)(2,1)}, bf16[128,640]{1,0:T(8,128)(2,1)S(1)}, u32[]{:S(2)}, u32[]{:S(2)}) collective-permute-start(bf16[128,640]{1,0:T(8,128)(2,1)} %get-tuple-element.49.pack_ref), channel_id=1, source_target_pairs={{64,0},{453,1},{130,2},{259,3},{460,8},{73,9},{138,10},{271,11},{1... | collective-permute-start | bytes 491528 | tf_op jit(solution)/shard_map/ppermute | solution.py:406
  32.2 30.8 %all-to-all-start.1 = ((bf16[8,128,512]{2,1,0:T(8,128)(2,1)}), bf16[8,128,512]{2,1,0:T(8,128)(2,1)S(1)}, u32[]{:S(2)}, u32[]{:S(2)}) async-start(bf16[8,128,512]{2,1,0:T(8,128)(2,1)} %spread_weight.1), calls=%async_computation.1 | async-start | bytes 2097152 | tf_op jit(solution)/shard_map/all_to_all | solution.py:430
  37.0 26.0 %copy-start.4 = (bf16[256,640]{1,0:T(8,128)(2,1)}, bf16[256,640]{1,0:T(8,128)(2,1)S(1)}, u32[]{:S(2)}) copy-start(bf16[256,640]{1,0:T(8,128)(2,1)S(1)} %join.1.l0) | copy-start | bytes 983044
  37.0 20.4 %collective-permute-start.4 = (bf16[256,640]{1,0:T(8,128)(2,1)S(1)}, bf16[256,640]{1,0:T(8,128)(2,1)S(1)}, u32[]{:S(2)}, u32[]{:S(2)}) collective-permute-start(bf16[256,640]{1,0:T(8,128)(2,1)S(1)} %join.1.l0), channel_id=1, source_target_pairs={{0,1},{1,2},{2,3},{3,0},{4,5},{5,6},{6,7},{7,4},{8,9},{9,10},{10,1... | collective-permute-start | bytes 983048 | tf_op jit(solution)/shard_map/ppermute | solution.py:411
  42.7 14.6 %collective-permute-start.3 = (bf16[256,640]{1,0:T(8,128)(2,1)S(1)}, bf16[256,640]{1,0:T(8,128)(2,1)S(1)}, u32[]{:S(2)}, u32[]{:S(2)}) collective-permute-start(bf16[256,640]{1,0:T(8,128)(2,1)S(1)} %join.1.l0), channel_id=1, source_target_pairs={{0,2},{1,3},{2,0},{3,1},{4,6},{5,7},{6,4},{7,5},{8,10},{9,11},{10,... | collective-permute-start | bytes 983048 | tf_op jit(solution)/shard_map/ppermute | solution.py:411
  46.1 16.8 %collective-permute-start.2 = (bf16[256,640]{1,0:T(8,128)(2,1)S(1)}, bf16[256,640]{1,0:T(8,128)(2,1)S(1)}, u32[]{:S(2)}, u32[]{:S(2)}) collective-permute-start(bf16[256,640]{1,0:T(8,128)(2,1)S(1)} %join.1.l0), channel_id=1, source_target_pairs={{0,3},{1,0},{2,1},{3,2},{4,7},{5,4},{6,5},{7,6},{8,11},{9,8},{10,9... | collective-permute-start | bytes 983048 | tf_op jit(solution)/shard_map/ppermute | solution.py:411
  77.9 12.1 %collective-permute-start.9 = (bf16[512,512]{1,0:T(8,128)(2,1)}, bf16[512,512]{1,0:T(8,128)(2,1)S(1)}, u32[]{:S(2)}, u32[]{:S(2)}) collective-permute-start(bf16[512,512]{1,0:T(8,128)(2,1)} %get-tuple-element.64), channel_id=1, source_target_pairs={{0,8},{8,0},{1,9},{9,1},{2,10},{10,2},{3,11},{11,3},{4,12},{12,4},... | collective-permute-start | bytes 1572872 | tf_op jit(solution)/shard_map/ppermute | solution.py:416
  79.8 14.9 %collective-permute-start.5 = (bf16[256,640]{1,0:T(8,128)(2,1)}, bf16[256,640]{1,0:T(8,128)(2,1)S(1)}, u32[]{:S(2)}, u32[]{:S(2)}) collective-permute-start(bf16[256,640]{1,0:T(8,128)(2,1)} %get-tuple-element.58), channel_id=1, source_target_pairs={{0,1},{1,2},{2,3},{3,0},{4,5},{5,6},{6,7},{7,4},{8,9},{9,10},{10,1... | collective-permute-start | bytes 983048 | tf_op jit(solution)/shard_map/ppermute | solution.py:411
  82.3 14.2 %collective-permute-start.6 = (bf16[256,640]{1,0:T(8,128)(2,1)}, bf16[256,640]{1,0:T(8,128)(2,1)S(1)}, u32[]{:S(2)}, u32[]{:S(2)}) collective-permute-start(bf16[256,640]{1,0:T(8,128)(2,1)} %get-tuple-element.59), channel_id=1, source_target_pairs={{0,2},{1,3},{2,0},{3,1},{4,6},{5,7},{6,4},{7,5},{8,10},{9,11},{10,... | collective-permute-start | bytes 983048 | tf_op jit(solution)/shard_map/ppermute | solution.py:411
  86.0 16.7 %collective-permute-start.7 = (bf16[256,640]{1,0:T(8,128)(2,1)}, bf16[256,640]{1,0:T(8,128)(2,1)S(1)}, u32[]{:S(2)}, u32[]{:S(2)}) collective-permute-start(bf16[256,640]{1,0:T(8,128)(2,1)} %get-tuple-element.60), channel_id=1, source_target_pairs={{0,3},{1,0},{2,1},{3,2},{4,7},{5,4},{6,5},{7,6},{8,11},{9,8},{10,9... | collective-permute-start | bytes 983048 | tf_op jit(solution)/shard_map/ppermute | solution.py:411
  91.1 20.7 %collective-permute-start.10 = (bf16[256,512]{1,0:T(8,128)(2,1)S(1)}, bf16[256,512]{1,0:T(8,128)(2,1)S(1)}, u32[]{:S(2)}, u32[]{:S(2)}) collective-permute-start(bf16[256,512]{1,0:T(8,128)(2,1)S(1)} %get-tuple-element.65), channel_id=1, source_target_pairs={{0,16},{16,0},{32,48},{48,32},{1,17},{17,1},{33,49},{49,33},{2,18}... | collective-permute-start | bytes 786440 | tf_op jit(solution)/shard_map/ppermute | solution.py:416
  103.9 8.0 %collective-permute-start.8 = (bf16[128,640]{1,0:T(8,128)(2,1)S(1)}, bf16[128,640]{1,0:T(8,128)(2,1)S(1)}, u32[]{:S(2)}, u32[]{:S(2)}) collective-permute-start(bf16[128,640]{1,0:T(8,128)(2,1)S(1)} %get-tuple-element.62), channel_id=1, source_target_pairs={{0,64},{64,0},{128,192},{192,128},{256,320},{320,256},{384,448},{4... | collective-permute-start | bytes 491528 | tf_op jit(solution)/shard_map/ppermute | solution.py:416
  111.9 46.6 %copy-start.1 = (bf16[1024,512]{1,0:T(8,128)(2,1)S(1)}, bf16[1024,512]{1,0:T(8,128)(2,1)}, u32[]{:S(2)}) copy-start(bf16[1024,512]{1,0:T(8,128)(2,1)} %get-tuple-element.54.weight_ref) | copy-start | bytes 3145732
  111.9 46.5 %copy-start = (bf16[1024,640]{1,0:T(8,128)(2,1)S(1)}, bf16[1024,640]{1,0:T(8,128)(2,1)}, u32[]{:S(2)}) copy-start(bf16[1024,640]{1,0:T(8,128)(2,1)} %get-tuple-element.53.dq_ref) | copy-start | bytes 3932164
  112.0 12.2 %collective-permute-start.12 = (bf16[128,512]{1,0:T(8,128)(2,1)S(1)}, bf16[128,512]{1,0:T(8,128)(2,1)S(1)}, u32[]{:S(2)}, u32[]{:S(2)}) collective-permute-start(bf16[128,512]{1,0:T(8,128)(2,1)S(1)} %get-tuple-element.71), channel_id=1, source_target_pairs={{0,48},{16,32},{32,16},{48,0},{1,49},{17,33},{33,17},{49,1},{2,50}... | collective-permute-start | bytes 393224 | tf_op jit(solution)/shard_map/ppermute | solution.py:416
  116.9 7.2 %collective-permute-start.11 = (bf16[64,640]{1,0:T(8,128)(2,1)S(1)}, bf16[64,640]{1,0:T(8,128)(2,1)S(1)}, u32[]{:S(2)}, u32[]{:S(2)}) collective-permute-start(bf16[64,640]{1,0:T(8,128)(2,1)S(1)} %get-tuple-element.68), channel_id=1, source_target_pairs={{0,128},{64,192},{128,0},{192,64},{256,384},{320,448},{384,256},{4... | collective-permute-start | bytes 245768 | tf_op jit(solution)/shard_map/ppermute | solution.py:416
  124.2 12.5 %collective-permute-start.13 = (bf16[64,640]{1,0:T(8,128)(2,1)S(1)}, bf16[64,640]{1,0:T(8,128)(2,1)S(1)}, u32[]{:S(2)}, u32[]{:S(2)}) collective-permute-start(bf16[64,640]{1,0:T(8,128)(2,1)S(1)} %keys_pair.1.both_ref), channel_id=1, source_target_pairs={{0,256},{64,320},{128,384},{192,448},{256,0},{320,64},{384,128},{4... | collective-permute-start | bytes 245768 | tf_op jit(solution)/shard_map/ppermute | solution.py:416
  129.0 6.2 %collective-permute-start.14 = (bf16[64,512]{1,0:T(8,128)(2,1)S(1)}, bf16[64,512]{1,0:T(8,128)(2,1)S(1)}, u32[]{:S(2)}, u32[]{:S(2)}) collective-permute-start(bf16[64,512]{1,0:T(8,128)(2,1)S(1)} %get-tuple-element.75), channel_id=1, source_target_pairs={{0,64},{64,0},{128,192},{192,128},{256,320},{320,256},{384,448},{4... | collective-permute-start | bytes 196616 | tf_op jit(solution)/shard_map/ppermute | solution.py:416
  136.7 12.9 %collective-permute-start.15 = (bf16[32,640]{1,0:T(8,128)(2,1)S(1)}, bf16[32,640]{1,0:T(8,128)(2,1)S(1)}, u32[]{:S(2)}, u32[]{:S(2)}) collective-permute-start(bf16[32,640]{1,0:T(8,128)(2,1)S(1)} %get-tuple-element.78), channel_id=1, source_target_pairs={{0,260},{64,324},{128,388},{192,452},{256,4},{320,68},{384,132},{4... | collective-permute-start | bytes 122888 | tf_op jit(solution)/shard_map/ppermute | solution.py:426
  142.9 6.7 %collective-permute-start.16 = (bf16[32,512]{1,0:T(8,128)(2,1)S(1)}, bf16[32,512]{1,0:T(8,128)(2,1)S(1)}, u32[]{:S(2)}, u32[]{:S(2)}) collective-permute-start(bf16[32,512]{1,0:T(8,128)(2,1)S(1)} %get-tuple-element.81), channel_id=1, source_target_pairs={{0,128},{64,192},{128,0},{192,64},{256,384},{320,448},{384,256},{4... | collective-permute-start | bytes 98312 | tf_op jit(solution)/shard_map/ppermute | solution.py:416
  150.3 14.9 %all-to-all-start.2 = ((bf16[4,32,640]{2,1,0:T(8,128)(2,1)}), bf16[4,32,640]{2,1,0:T(8,128)(2,1)S(1)}, u32[]{:S(2)}, u32[]{:S(2)}) async-start(bf16[4,32,640]{2,1,0:T(8,128)(2,1)} %keys_sum.1), calls=%async_computation.2 | async-start | bytes 327680 | tf_op jit(solution)/shard_map/all_to_all | solution.py:430
  155.7 9.5 %collective-permute-start.17 = (bf16[16,512]{1,0:T(8,128)(2,1)S(1)}, bf16[16,512]{1,0:T(8,128)(2,1)S(1)}, u32[]{:S(2)}, u32[]{:S(2)}) collective-permute-start(bf16[16,512]{1,0:T(8,128)(2,1)S(1)} %get-tuple-element.85), channel_id=1, source_target_pairs={{0,256},{64,320},{128,384},{192,448},{256,0},{320,64},{384,128},{4... | collective-permute-start | bytes 49160 | tf_op jit(solution)/shard_map/ppermute | solution.py:416
  (6 other events, 15.1 us)

commit v3 on v2

--- a/solution.py
+++ b/solution.py
@@ -63,15 +63,15 @@
 
 
 def weight_order(row):
-    x, c, rank, n = row // 32, (row // 16) % 2, (row % 16) // 2, row % 2
-    return rank * 16 + x * 4 + c * 2 + n
+    x, c = lax.axis_index("x"), lax.axis_index("c")
+    core, step, rank, n = c ^ (row // 64), (row // 16) % 4, (row % 16) // 2, row % 2
+    return rank * 16 + (x ^ step ^ (step // 2)) * 4 + core * 2 + n
 
 
 FETCH = (((1, -3), (-1, 3), (2, -2), (4, None)), ((-1, 3), (1, -3), (2, -2), (-4, None)))
 
 
-FOLD_X = (0, 3, 1, 2)
-FOLD = (0, 4, 2, 6, 1, 5, 3, 7)
+FOLD_X = (0, 2, 1, 3)
 
 
 def call(body, outs, ins, scratch=(), flops=0, smem=(), hbm=(), name=None, vmem=6):
@@ -139,17 +139,22 @@
     pack_out[:, DC:WIDE] = tn(rot_ref[...], widen).astype(bf16)
 
 
-def spread_weight_kernel(in_ref, out_ref):
+def order_weight_kernel(in_ref, out_ref):
     out, inp = iota((128, 128), 0), iota((128, 128), 1)
     head, rank, n = out // 16, (out % 16) // 2, out % 2
-    weight = nn(chosen(inp == rank * 16 + n * 8 + head), in_ref[:, 0:DC]).astype(bf16)
-    for i in range(8):
-        out_ref[i] = weight
+    out_ref[...] = nn(chosen(inp == rank * 16 + n * 8 + head), in_ref[:, 0:DC]).astype(bf16)
 
 
 def join_kernel(first, second, out_ref):
-    out_ref[0:TOK, :] = first[...]
-    out_ref[TOK : 2 * TOK, :] = second[...]
+    size = first.shape[0]
+    out_ref[0:size, :] = first[...]
+    out_ref[size : 2 * size, :] = second[...]
+
+
+def spread_latent_kernel(first, second, out_ref):
+    for y in range(4):
+        out_ref[y, 0:TOK, :] = first[...]
+        out_ref[y, TOK : 2 * TOK, :] = second[...]
 
 
 def order_queries(nope_ref, rot_ref, up_ref, nope_out, query, up_out):
@@ -177,18 +182,13 @@
     runs_ref,
     pos_ref,
     pack_ref,
-    l0,
-    l1,
-    l2,
-    l3,
-    w_ref,
+    lat_ref,
+    w_own,
+    w_other,
     nope_in,
     rot_in,
     up_in,
-    k0,
-    k1,
-    k2,
-    k3,
+    dkey_out,
     own_out,
     other_out,
     dq_ref,
@@ -201,11 +201,9 @@
     dquery,
     nope_ref,
     up_ref,
-    staged,
 ):
     order_queries(nope_in, rot_in, up_in, nope_ref, query, up_ref)
-    zl, c, y = lax.axis_index("zl"), lax.axis_index("c"), lax.axis_index("y")
-    x = lax.axis_index("x")
+    zl, c = lax.axis_index("zl"), lax.axis_index("c")
 
     def place_of(run, start, size):
         return pl.ds(pl.multiple_of(run * HALF + start, size), size)
@@ -213,26 +211,22 @@
     for half in range(2):
         run = pos_ref[half * HALF] >> 6
         keys[place_of(run, 0, HALF), :] = pack_ref[half * HALF : (half + 1) * HALF, :]
-    for step, part in enumerate((l0, l1, l2, l3)):
-        source = (y + step) % 4
+    for y in range(4):
         for slot in range(2):
-            away = jnp.int32(0)
-            for core in range(2):
-                for owner in range(4):
-                    here = (c == core) & (source == owner)
-                    away = jnp.where(here, FETCH[core][owner][slot] or 0, away)
-
-            @pl.when(away != 0)
-            def _():
-                rank = (zl + RANKS + away) % RANKS
-                for half in range(2):
-                    run = runs_ref[rank * 2 + half]
-                    start = slot * TOK + half * HALF
-                    keys[place_of(run, 0, HALF), :] = part[start : start + HALF, :]
-
+            steps = [FETCH[core][y][slot] for core in range(2)]
+            if steps[0] is None:
+                continue
+            rank = (zl + RANKS + jnp.where(c == 0, steps[0], steps[1])) % RANKS
+            for half in range(2):
+                start = slot * TOK + half * HALF
+                at = place_of(runs_ref[rank * 2 + half], 0, HALF)
+                keys[at, :] = lat_ref[y, start : start + HALF, :]
     for h in range(HEADS):
-        for i in range(8):
-            weight_ref[h * DN + i * 16 : h * DN + i * 16 + 16, :] = w_ref[i, h * 16 : h * 16 + 16, :]
+        for core, part in enumerate((w_own, w_other)):
+            for step in range(4):
+                at = h * DN + core * 64 + step * 16
+                place = step * 128 + h * 16
+                weight_ref[at : at + 16, :] = part[place : place + 16, :]
     for h in range(HEADS):
         pair = [nope_ref[(half * HEADS + h) * HALF : (half * HEADS + h + 1) * HALF, :] for half in range(2)]
         absorbed = nn(jnp.concatenate(pair, axis=0), weight_ref[h * DN : (h + 1) * DN, :])
@@ -285,22 +279,20 @@
         lax.fori_loop(0, count, grads, 0)
         dq_ref[rows, :] = dquery[...].astype(bf16)
 
-    for step, part in enumerate((k0, k1, k2, k3)):
-        quarter = (y + step) % 4
+    for quarter in range(4):
         for k in range(RANKS):
-            run = runs_ref[(zl ^ FOLD[k]) * 2 + quarter // 2]
+            run = runs_ref[((zl & 4) ^ k) * 2 + quarter // 2]
             at = place_of(run, (quarter % 2) * QUARTER, QUARTER)
-            part[k * QUARTER : (k + 1) * QUARTER, :] = dkey[at, :].astype(bf16)
+            dkey_out[quarter, k * QUARTER : (k + 1) * QUARTER, :] = dkey[at, :].astype(bf16)
     for h in range(HEADS):
         places = [slice((half * HEADS + h) * HALF, (half * HEADS + h + 1) * HALF) for half in range(2)]
         nope = jnp.concatenate([nope_ref[p, :] for p in places], axis=0)
         dq = jnp.concatenate([dq_ref[p, 0:DC] for p in places], axis=0)
         master = tn(nope, dq).astype(bf16)
-        staged[...] = master
         for core, part in enumerate((own_out, other_out)):
-            for k, away in enumerate(FOLD_X):
-                at = pl.ds(pl.multiple_of(((x ^ away) * 2 + (c + core) % 2) * 16, 16), 16)
-                part[k * 128 + h * 16 : k * 128 + h * 16 + 16, :] = staged[at, :]
+            for k, step in enumerate(FOLD_X):
+                at = core * 64 + step * 16
+                part[k * 128 + h * 16 : k * 128 + h * 16 + 16, :] = master[at : at + 16, :]
 
 
 def query_grads_kernel(dq_ref, weight_ref, nope_out, rot_out, scratch):
@@ -333,20 +325,47 @@
     return total
 
 
-def keys_plane_kernel(k0, k1, k2, k3, keep_ref, send_ref):
-    total = total_of([k[...] for k in (k0, k1, k2, k3)])
-    keep_ref[...] = total[0:128, :]
-    send_ref[...] = total[128:256, :].astype(bf16)
-
-
-def keys_pair_kernel(keep_ref, got_ref, both_out):
-    both_out[...] = (keep_ref[...] + got_ref[...].astype(f32)).astype(bf16)
-
-
-def keys_cross_kernel(both_ref, got_ref, keep_out, send_out):
+def master_plane_kernel(own_ref, got_ref, keep_ref, send_ref):
+    total = own_ref[...].astype(f32) + got_ref[...].astype(f32)
+    keep_ref[...] = total[0:256, :]
+    send_ref[...] = total[256:512, :].astype(bf16)
+
+
+def fold_kernel(keep_ref, got_ref, keep_out, send_out):
+    size = keep_out.shape[0]
+    keep_out[...] = keep_ref[0:size, :] + got_ref[0:size, :].astype(f32)
+    send_out[...] = (keep_ref[size:, :] + got_ref[size:, :].astype(f32)).astype(bf16)
+
+
+def plane_kernel(dkey_ref, keep_ref, got_ref, out_ref):
+    keys = total_of([dkey_ref[y] for y in range(4)]).astype(bf16)
+    master = (keep_ref[...] + got_ref[...].astype(f32)).astype(bf16)
+    zl = lax.axis_index("zl")
+    out, inp = iota((128, 128), 0), iota((128, 128), 1)
+    rank, n, head = (out // 16) ^ (zl & 4), (out % 16) // 8, out % 8
+    master = nn(chosen(inp == head * 16 + rank * 2 + n), master).astype(bf16)
+    blank = jnp.zeros((2 * WROWS, 128), bf16)
+    for j in range(4):
+        for pair in range(2):
+            k = pair * 4 + j
+            out_ref[j, pair * QUARTER : (pair + 1) * QUARTER, :] = keys[k * QUARTER : (k + 1) * QUARTER, :]
+            at = 2 * QUARTER + pair * WROWS
+            out_ref[j, at : at + WROWS, 0:DC] = master[k * WROWS : (k + 1) * WROWS, :]
+        out_ref[j, 2 * QUARTER :, DC:WIDE] = blank
+
+
+def quad_sum_kernel(in_ref, both_out, keep_out):
+    total = total_of([in_ref[j] for j in range(4)])
+    both_out[0 : 2 * QUARTER, :] = total[0 : 2 * QUARTER, :].astype(bf16)
+    both_out[2 * QUARTER :, :] = total[2 * QUARTER + WROWS :, :].astype(bf16)
+    keep_out[...] = total[2 * QUARTER : 2 * QUARTER + WROWS, 0:DC]
+
+
+def cross_kernel(both_ref, got_ref, master_ref, keep_out, send_out, master_out):
     low, high = slice(0, QUARTER), slice(QUARTER, 2 * QUARTER)
     keep_out[...] = total_of([both_ref[low, :], got_ref[high, :]]).astype(bf16)
     send_out[...] = total_of([both_ref[high, :], got_ref[low, :]]).astype(bf16)
+    master_out[...] = master_ref[...] + got_ref[2 * QUARTER :, 0:DC].astype(f32)
 
 
 def keys_sum_kernel(keep_ref, got_ref, out_ref):
@@ -362,33 +381,6 @@
         latent_ref[y * QUARTER : (y + 1) * QUARTER, :] = part[:, 0:DC]
         rest.append(part[:, DC:WIDE])
     rotary_ref[...] = jnp.concatenate(rest, axis=0).T[0:DR, :]
-
-
-def master_plane_kernel(own_ref, got_ref, keep_ref, send_ref):
-    total = own_ref[...].astype(f32) + got_ref[...].astype(f32)
-    keep_ref[...] = total[0:256, :]
-    send_ref[...] = total[256:512, :].astype(bf16)
-
-
-def master_order_kernel(keep_ref, got_ref, keep_out, send_out):
-    master = (keep_ref[...] + got_ref[...].astype(f32)).astype(bf16)
-    zl = lax.axis_index("zl")
-    out, inp = iota((128, 128), 0), iota((128, 128), 1)
-    k, n, head = out // 16, (out % 16) // 8, out % 8
-    rank = zl ^ ((k % 2) * 4 + ((k // 2) % 2) * 2 + k // 4)
-    master = nn(chosen(inp == head * 16 + rank * 2 + n), master)
-    keep_out[...] = master[0:64, :]
-    send_out[...] = master[64:128, :].astype(bf16)
-
-
-def fold_kernel(keep_ref, got_ref, keep_out, send_out):
-    size = keep_out.shape[0]
-    keep_out[...] = keep_ref[0:size, :] + got_ref[0:size, :].astype(f32)
-    send_out[...] = (keep_ref[size:, :] + got_ref[size:, :].astype(f32)).astype(bf16)
-
-
-def master_last_kernel(keep_ref, got_ref, out_ref):
-    out_ref[...] = keep_ref[...] + got_ref[...].astype(f32)
 
 
 def fetch(block, slot):
@@ -406,11 +398,6 @@
     return lax.ppermute(block, axes, pairs)
 
 
-def shift(block, axis, step):
-    n = lax.axis_size(axis)
-    return lax.ppermute(block, axis, [(i, (i + step) % n) for i in range(n)])
-
-
 def across(block, axis, step):
     n = lax.axis_size(axis)
     return lax.ppermute(block, axis, [(i, i ^ step) for i in range(n)])
@@ -424,6 +411,11 @@
         return place % 8 * 2 + place // 8
 
     return lax.ppermute(block, ("zl", "zh"), [(index(p), index(partner(p))) for p in range(16)])
+
+
+def quads(blocks):
+    groups = [[0, 1, 2, 3], [4, 5, 6, 7]]
+    return lax.all_to_all(blocks, "zl", 0, 0, tiled=True, axis_index_groups=groups)
 
 
 def everyone(blocks, axes):
@@ -448,26 +440,36 @@
     )
     weight_ranks = everyone(weight_send, "zl")
     first, second = fetch(pack, 0), fetch(pack, 1)
-    weight_ranks, first, second = lax.optimization_barrier((weight_ranks, first, second))
-    (weight_spread,) = call(
-        spread_weight_kernel,
-        (shape(8, 128, DC),),
-        (weight_ranks.reshape(128, WIDE),),
-        name="spread_weight",
-    )
-    weight_all = everyone(weight_spread, ("x", "c"))
-    (joined,) = call(join_kernel, (shape(2 * TOK, WIDE),), (first, second), name="join")
-    lat = [joined] + [shift(joined, "y", -step) for step in (1, 2, 3)]
+    together = lax.optimization_barrier
+    weight_ranks, first, second = together((weight_ranks, first, second))
+    (latent_spread,) = call(
+        spread_latent_kernel, (shape(4, 2 * TOK, WIDE),), (first, second), name="spread_latent"
+    )
+    latent_all = everyone(latent_spread, "y")
+    (w_own,) = call(
+        order_weight_kernel, (shape(128, DC),), (weight_ranks.reshape(128, WIDE),), name="order_weight"
+    )
+    for size, step in ((256, 1), (512, 3)):
+        (w_own,) = call(join_kernel, (shape(size, DC),), (w_own, across(w_own, "x", step)), name="join")
+    w_other = across(w_own, "c", 1)
+    latent_all, w_own, w_other = together((latent_all, w_own, w_other))
     runs = weight_ranks[:, 0, DC : DC + 2].astype(jnp.int32).reshape(16)
-    k0, k1, k2, k3, own, other, dq, weight = call(
+    dkey, own, other, dq, weight = call(
         attention_kernel,
-        (shape(256, WIDE),) * 4 + (shape(512, DC),) * 2 + (shape(1024, WIDE), shape(1024, DC)),
+        (
+            shape(4, 256, WIDE),
+            shape(512, DC),
+            shape(512, DC),
+            shape(1024, WIDE),
+            shape(1024, DC),
+        ),
         (
             runs,
             positions,
             pack,
-            *lat,
-            weight_all,
+            latent_all,
+            w_own,
+            w_other,
             nope.reshape(1024, DN),
             rotary,
             upstream.reshape(1024, DC),
@@ -481,15 +483,12 @@
             pltpu.VMEM((ROWS, WIDE), f32),
             pltpu.VMEM((1024, DN), bf16),
             pltpu.VMEM((1024, DC), bf16),
-            pltpu.VMEM((DN, DC), bf16),
         ),
         smem=(0, 1),
         flops=2 * 512 * 1280 * 2944,
         name="attention",
         vmem=56,
     )
-    k = [k0] + [shift(part, "y", step) for step, part in ((1, k1), (2, k2), (3, k3))]
-    other = across(other, "c", 1)
     nope_grad, rot_grad = call(
         query_grads_kernel,
         (shape(1024, DN), shape(TOK, HEADS * DR)),
@@ -498,29 +497,27 @@
         flops=2 * 1024 * 128 * 768,
         name="query_grads",
     )
-    def folded(body, size, width, ins, dtype=f32, name="fold"):
-        return call(body, (shape(size, width, dtype=dtype), shape(size, width)), ins, name=name)
-
-    together = lax.optimization_barrier
-    mkeep, send = folded(master_plane_kernel, 256, DC, (own, other), name="master_plane")
-    got = across(send, "x", 1)
-    keep, send = folded(keys_plane_kernel, 128, WIDE, k, name="keys_plane")
-    got, mgot = together((across(send, "zl", 1), got))
-    mkeep, msend = folded(fold_kernel, 128, DC, (mkeep, mgot))
-    keep, send = folded(fold_kernel, 64, WIDE, (keep, got))
-    got, mgot = together((across(send, "zl", 2), across(msend, "x", 3)))
-    mkeep, msend = folded(master_order_kernel, 64, DC, (mkeep, mgot), name="master_order")
-    (both,) = call(keys_pair_kernel, (shape(64, WIDE),), (keep, got), name="keys_pair")
-    got, mgot = together((across(both, "zl", 4), across(msend, "zl", 1)))
-    mkeep, msend = folded(fold_kernel, 32, DC, (mkeep, mgot))
-    keep, send = folded(keys_cross_kernel, QUARTER, WIDE, (both, got), dtype=bf16, name="keys_cross")
-    got, mgot = together((over_edge(send), across(msend, "zl", 2)))
-    mkeep, msend = folded(fold_kernel, 16, DC, (mkeep, mgot))
-    (dkey_sum,) = call(keys_sum_kernel, (shape(4, QUARTER, WIDE),), (keep, got), name="keys_sum")
-    dkey_all, mgot = together((everyone(dkey_sum, "y"), across(msend, "zl", 4)))
-    (master_grad,) = call(
-        master_last_kernel, (shape(WROWS, DC, dtype=f32),), (mkeep, mgot), name="master_last"
-    )
+    def folded(body, size, ins, name):
+        return call(body, (shape(size, DC, dtype=f32), shape(size, DC)), ins, name=name)
+
+    keep, send = folded(master_plane_kernel, 256, (own, across(other, "c", 1)), "master_plane")
+    keep, send = folded(fold_kernel, 128, (keep, across(send, "x", 1)), "fold")
+    dkey_planes, got = together((everyone(dkey, "y"), across(send, "x", 3)))
+    (blocks,) = call(plane_kernel, (shape(4, 96, WIDE),), (dkey_planes, keep, got), name="plane")
+    both, keep = call(
+        quad_sum_kernel, (shape(80, WIDE), shape(WROWS, DC, dtype=f32)), (quads(blocks),), name="quad_sum"
+    )
+    got = across(both, "zl", 4)
+    keep, send, master_grad = call(
+        cross_kernel,
+        (shape(QUARTER, WIDE), shape(QUARTER, WIDE), shape(WROWS, DC, dtype=f32)),
+        (both, got, keep),
+        name="cross",
+    )
+    (dkey_sum,) = call(
+        keys_sum_kernel, (shape(4, QUARTER, WIDE),), (keep, over_edge(send)), name="keys_sum"
+    )
+    dkey_all = everyone(dkey_sum, "y")
     latent_grad, keys_grad = call(
         keys_last_kernel,
         (shape(TOK, DC, dtype=f32), shape(DR, TOK, dtype=f32)),

time: 168 us -> 157 us (0.935)
  the two profiles are of different devices: /device:TPU:40 before, /device:TPU:6 now
where the time goes in v3:
time: 157 us; the launch traced here: 156 us
  starting transfers between devices  59.5 us (38%)
  waiting for transfers between devices  55.1 us (35%)
  Pallas kernels  21.4 us (14%)
  blocking collectives  17.2 us (11%)
  local copies, waits for them, and re-layouts  1.88 us (1%)
    ppermute x7, waiting for transfers between devices, across(): return lax.ppermute(block, axis, [(i, i ^ step) for i in range(n)])  38 us
    all_to_all x4, starting transfers between devices, everyone(): return lax.all_to_all(blocks, axes, 0, 0, tiled=True)  27.3 us
    pallas_call x14, Pallas kernels, call(): pl.pallas_call(body, out_shape=outs, in_specs=specs, out_specs=[pl.BlockS...  21.4 us
    ppermute x7, starting transfers between devices, across(): return lax.ppermute(block, axis, [(i, i ^ step) for i in range(n)])  18.3 us
    all_to_all x1, blocking collectives, quads(): lax.all_to_all(blocks, 'zl', 0, 0, tiled=True, axis_index_groups=groups)  17.2 us
    ppermute x2, starting transfers between devices, fetch(): return lax.ppermute(block, axes, pairs)  10.7 us
    ppermute x1, waiting for transfers between devices, over_edge(): lax.ppermute(block, ('zl', 'zh'), [(index(p), index(partner(p))) for p in...  6.61 us
    ppermute x2, waiting for transfers between devices, fetch(): return lax.ppermute(block, axes, pairs)  5.43 us
  transfers between devices with their start and end apart: 14, of which 12 were waited for; matrix products, arithmetic and copies ran while one was open for 0% of the time, Pallas kernels for 2%

profile of v3, /device:TPU:6, one launch (start us, length us, event | category | flops | bytes accessed | tf_op | source)
XLA Modules:
  0.0 155.9 jit_solution(16969387541404650593)
XLA Ops:
  2.5 12.5 %all-to-all-start = ((bf16[8,16,640]{2,1,0:T(8,128)(2,1)}), bf16[8,16,640]{2,1,0:T(8,128)(2,1)S(1)}, u32[]{:S(2)}, u32[]{:S(2)}) async-start(bf16[8,16,640]{2,1,0:T(8,128)(2,1)} %get-tuple-element.33), calls=%async_computation | async-start | bytes 327680 | tf_op jit(solution)/shard_map/all_to_all | solution.py:422
  15.0 5.7 %collective-permute-start.1 = (bf16[128,640]{1,0:T(8,128)(2,1)}, bf16[128,640]{1,0:T(8,128)(2,1)S(1)}, u32[]{:S(2)}, u32[]{:S(2)}) collective-permute-start(bf16[128,640]{1,0:T(8,128)(2,1)} %get-tuple-element.34.pack_ref), channel_id=1, source_target_pairs={{324,0},{193,1},{390,2},{200,8},{333,9},{398,10},{388,64},{257,65}... | collective-permute-start | bytes 491528 | tf_op jit(solution)/shard_map/ppermute | solution.py:398
  20.7 5.0 %collective-permute-start = (bf16[128,640]{1,0:T(8,128)(2,1)}, bf16[128,640]{1,0:T(8,128)(2,1)S(1)}, u32[]{:S(2)}, u32[]{:S(2)}) collective-permute-start(bf16[128,640]{1,0:T(8,128)(2,1)} %get-tuple-element.34.pack_ref), channel_id=1, source_target_pairs={{64,0},{453,1},{130,2},{259,3},{460,8},{73,9},{138,10},{271,11},{1... | collective-permute-start | bytes 491528 | tf_op jit(solution)/shard_map/ppermute | solution.py:398
  25.7 5.4 %collective-permute-done.1.second = bf16[128,640]{1,0:T(8,128)(2,1)S(1)} collective-permute-done((bf16[128,640]{1,0:T(8,128)(2,1)}, bf16[128,640]{1,0:T(8,128)(2,1)S(1)}, u32[]{:S(2)}, u32[]{:S(2)}) %collective-permute-start.1) | collective-permute-done | bytes 163872 | tf_op jit(solution)/shard_map/ppermute | solution.py:398
  33.5 5.3 %all-to-all-start.1 = ((bf16[4,256,640]{2,1,0:T(8,128)(2,1)}), bf16[4,256,640]{2,1,0:T(8,128)(2,1)S(1)}, u32[]{:S(2)}, u32[]{:S(2)}) async-start(bf16[4,256,640]{2,1,0:T(8,128)(2,1)} %spread_latent.1), calls=%async_computation.1 | async-start | bytes 2621440 | tf_op jit(solution)/shard_map/all_to_all | solution.py:422
  39.0 2.7 %collective-permute-start.2 = (bf16[128,512]{1,0:T(8,128)(2,1)S(1)}, bf16[128,512]{1,0:T(8,128)(2,1)S(1)}, u32[]{:S(2)}, u32[]{:S(2)}) collective-permute-start(bf16[128,512]{1,0:T(8,128)(2,1)S(1)} %order_weight.1.first), channel_id=1, source_target_pairs={{0,16},{16,0},{32,48},{48,32},{1,17},{17,1},{33,49},{49,33},{2,18}... | collective-permute-start | bytes 393224 | tf_op jit(solution)/shard_map/ppermute | solution.py:403
  41.8 4.1 %collective-permute-done.2.second = bf16[128,512]{1,0:T(8,128)(2,1)S(1)} collective-permute-done((bf16[128,512]{1,0:T(8,128)(2,1)S(1)}, bf16[128,512]{1,0:T(8,128)(2,1)S(1)}, u32[]{:S(2)}, u32[]{:S(2)}) %collective-permute-start.2) | collective-permute-done | bytes 131104 | tf_op jit(solution)/shard_map/ppermute | solution.py:403
  45.9 2.4 %collective-permute-start.3 = (bf16[256,512]{1,0:T(8,128)(2,1)S(1)}, bf16[256,512]{1,0:T(8,128)(2,1)S(1)}, u32[]{:S(2)}, u32[]{:S(2)}) collective-permute-start(bf16[256,512]{1,0:T(8,128)(2,1)S(1)} %join.2.first), channel_id=1, source_target_pairs={{0,48},{16,32},{32,16},{48,0},{1,49},{17,33},{33,17},{49,1},{2,50}... | collective-permute-start | bytes 786440 | tf_op jit(solution)/shard_map/ppermute | solution.py:403
  48.3 7.5 %collective-permute-done.3.second = bf16[256,512]{1,0:T(8,128)(2,1)S(1)} collective-permute-done((bf16[256,512]{1,0:T(8,128)(2,1)S(1)}, bf16[256,512]{1,0:T(8,128)(2,1)S(1)}, u32[]{:S(2)}, u32[]{:S(2)}) %collective-permute-start.3) | collective-permute-done | bytes 262176 | tf_op jit(solution)/shard_map/ppermute | solution.py:403
  55.8 1.9 %collective-permute-start.4 = (bf16[512,512]{1,0:T(8,128)(2,1)S(1)}, bf16[512,512]{1,0:T(8,128)(2,1)S(1)}, u32[]{:S(2)}, u32[]{:S(2)}) collective-permute-start(bf16[512,512]{1,0:T(8,128)(2,1)S(1)} %join.3.w_own), channel_id=1, source_target_pairs={{0,8},{8,0},{1,9},{9,1},{2,10},{10,2},{3,11},{11,3},{4,12},{12,4},... | collective-permute-start | bytes 1572872 | tf_op jit(solution)/shard_map/ppermute | solution.py:403
  60.9 13.3 %attention.1 = (bf16[4,256,640]{2,1,0:T(8,128)(2,1)}, bf16[512,512]{1,0:T(8,128)(2,1)}, bf16[512,512]{1,0:T(8,128)(2,1)}, bf16[1024,640]{1,0:T(8,128)(2,1)}, bf16[1024,512]{1,0:T(8,128)(2,1)}) custom-call(s32[16]{0:T(128)} %reshape.38.runs_ref, s32[128]{0:T(128)} %pos_ref.1, bf16[128,640]{1,0:T(8,128)(2,1)} %get-tuple-element.34.pack_ref, ...), custom_call_target="tpu_custom_call" | custom-call | flops 3858759680 | bytes 8684096 | tf_op jit(solution)/shard_map/attention/pallas_call | solution.py:83
  74.3 4.7 %all-to-all-start.2 = ((bf16[4,256,640]{2,1,0:T(8,128)(2,1)}), bf16[4,256,640]{2,1,0:T(8,128)(2,1)S(1)}, u32[]{:S(2)}, u32[]{:S(2)}) async-start(bf16[4,256,640]{2,1,0:T(8,128)(2,1)} %get-tuple-element.45), calls=%async_computation.2 | async-start | bytes 2621440 | tf_op jit(solution)/shard_map/all_to_all | solution.py:422
  82.8 1.9 %collective-permute-start.6 = (bf16[256,512]{1,0:T(8,128)(2,1)S(1)}, bf16[256,512]{1,0:T(8,128)(2,1)S(1)}, u32[]{:S(2)}, u32[]{:S(2)}) collective-permute-start(bf16[256,512]{1,0:T(8,128)(2,1)S(1)} %get-tuple-element.49), channel_id=1, source_target_pairs={{0,16},{16,0},{32,48},{48,32},{1,17},{17,1},{33,49},{49,33},{2,18}... | collective-permute-start | bytes 786440 | tf_op jit(solution)/shard_map/ppermute | solution.py:403
  84.8 8.3 %collective-permute-done.6.got_ref = bf16[256,512]{1,0:T(8,128)(2,1)S(1)} collective-permute-done((bf16[256,512]{1,0:T(8,128)(2,1)S(1)}, bf16[256,512]{1,0:T(8,128)(2,1)S(1)}, u32[]{:S(2)}, u32[]{:S(2)}) %collective-permute-start.6) | collective-permute-done | bytes 262176 | tf_op jit(solution)/shard_map/ppermute | solution.py:403
  93.1 2.4 %collective-permute-start.7 = (bf16[128,512]{1,0:T(8,128)(2,1)S(1)}, bf16[128,512]{1,0:T(8,128)(2,1)S(1)}, u32[]{:S(2)}, u32[]{:S(2)}) collective-permute-start(bf16[128,512]{1,0:T(8,128)(2,1)S(1)} %get-tuple-element.50), channel_id=1, source_target_pairs={{0,48},{16,32},{32,16},{48,0},{1,49},{17,33},{33,17},{49,1},{2,50}... | collective-permute-start | bytes 393224 | tf_op jit(solution)/shard_map/ppermute | solution.py:403
  95.5 5.7 %collective-permute-done.7.got_ref = bf16[128,512]{1,0:T(8,128)(2,1)S(1)} collective-permute-done((bf16[128,512]{1,0:T(8,128)(2,1)S(1)}, bf16[128,512]{1,0:T(8,128)(2,1)S(1)}, u32[]{:S(2)}, u32[]{:S(2)}) %collective-permute-start.7) | collective-permute-done | bytes 131104 | tf_op jit(solution)/shard_map/ppermute | solution.py:403
  101.6 17.2 %all_to_all.25.in_ref = bf16[4,96,640]{2,1,0:T(8,128)(2,1)S(1)} all-to-all(bf16[4,96,640]{2,1,0:T(8,128)(2,1)S(1)} %plane.1), channel_id=1, replica_groups={{0,64,128,192},{256,320,384,448},{1,65,129,193},{257,321,385,449},{2,66..., dimensions={0} | all-to-all | bytes 983040 | tf_op jit(solution)/shard_map/all_to_all | solution.py:418
  118.8 5.0 %collective-permute-start.8 = (bf16[80,640]{1,0:T(8,128)(2,1)S(1)}, bf16[80,640]{1,0:T(8,128)(2,1)S(1)}, u32[]{:S(2)}, u32[]{:S(2)}) collective-permute-start(bf16[80,640]{1,0:T(8,128)(2,1)S(1)} %get-tuple-element.54.both_ref), channel_id=1, source_target_pairs={{0,256},{64,320},{128,384},{192,448},{256,0},{320,64},{384,128},{4... | collective-permute-start | bytes 307208 | tf_op jit(solution)/shard_map/ppermute | solution.py:403
  123.9 9.2 %collective-permute-done.8.got_ref = bf16[80,640]{1,0:T(8,128)(2,1)S(1)} collective-permute-done((bf16[80,640]{1,0:T(8,128)(2,1)S(1)}, bf16[80,640]{1,0:T(8,128)(2,1)S(1)}, u32[]{:S(2)}, u32[]{:S(2)}) %collective-permute-start.8) | collective-permute-done | bytes 102432 | tf_op jit(solution)/shard_map/ppermute | solution.py:403
  133.7 3.2 %collective-permute-start.9 = (bf16[32,640]{1,0:T(8,128)(2,1)S(1)}, bf16[32,640]{1,0:T(8,128)(2,1)S(1)}, u32[]{:S(2)}, u32[]{:S(2)}) collective-permute-start(bf16[32,640]{1,0:T(8,128)(2,1)S(1)} %get-tuple-element.57), channel_id=1, source_target_pairs={{0,260},{64,324},{128,388},{192,452},{256,4},{320,68},{384,132},{4... | collective-permute-start | bytes 122888 | tf_op jit(solution)/shard_map/ppermute | solution.py:413
  136.9 6.6 %collective-permute-done.9.got_ref = bf16[32,640]{1,0:T(8,128)(2,1)S(1)} collective-permute-done((bf16[32,640]{1,0:T(8,128)(2,1)S(1)}, bf16[32,640]{1,0:T(8,128)(2,1)S(1)}, u32[]{:S(2)}, u32[]{:S(2)}) %collective-permute-start.9) | collective-permute-done | bytes 40992 | tf_op jit(solution)/shard_map/ppermute | solution.py:413
  144.2 4.8 %all-to-all-start.4 = ((bf16[4,32,640]{2,1,0:T(8,128)(2,1)}), bf16[4,32,640]{2,1,0:T(8,128)(2,1)S(1)}, u32[]{:S(2)}, u32[]{:S(2)}) async-start(bf16[4,32,640]{2,1,0:T(8,128)(2,1)} %keys_sum.1), calls=%async_computation.4 | async-start | bytes 327680 | tf_op jit(solution)/shard_map/all_to_all | solution.py:422
  149.0 2.2 %query_grads.1 = (bf16[1024,128]{1,0:T(8,128)(2,1)}, bf16[128,512]{1,0:T(8,128)(2,1)}) custom-call(bf16[1024,640]{1,0:T(8,128)(2,1)S(1)} %copy-done, bf16[1024,512]{1,0:T(8,128)(2,1)S(1)} %copy-done.1), custom_call_target="tpu_custom_call" | custom-call | flops 201326592 | bytes 2752512 | tf_op jit(solution)/shard_map/query_grads/pallas_call | solution.py:83
  151.3 3.9 %all-to-all-done.4.in_ref = bf16[4,32,640]{2,1,0:T(8,128)(2,1)S(1)} async-done(((bf16[4,32,640]{2,1,0:T(8,128)(2,1)}), bf16[4,32,640]{2,1,0:T(8,128)(2,1)S(1)}, u32[]{:S(2)}, u32[]{:S(2)}) %all-to-all-start.4) | async-done | bytes 163872 | tf_op jit(solution)/shard_map/all_to_all | solution.py:422
  (35 shorter events, 14.0 us)
Async XLA Ops:
  2.5 29.8 %all-to-all-start = ((bf16[8,16,640]{2,1,0:T(8,128)(2,1)}), bf16[8,16,640]{2,1,0:T(8,128)(2,1)S(1)}, u32[]{:S(2)}, u32[]{:S(2)}) async-start(bf16[8,16,640]{2,1,0:T(8,128)(2,1)} %get-tuple-element.33), calls=%async_computation | async-start | bytes 327680 | tf_op jit(solution)/shard_map/all_to_all | solution.py:422
  15.0 16.1 %collective-permute-start.1 = (bf16[128,640]{1,0:T(8,128)(2,1)}, bf16[128,640]{1,0:T(8,128)(2,1)S(1)}, u32[]{:S(2)}, u32[]{:S(2)}) collective-permute-start(bf16[128,640]{1,0:T(8,128)(2,1)} %get-tuple-element.34.pack_ref), channel_id=1, source_target_pairs={{324,0},{193,1},{390,2},{200,8},{333,9},{398,10},{388,64},{257,65}... | collective-permute-start | bytes 491528 | tf_op jit(solution)/shard_map/ppermute | solution.py:398
  20.7 10.4 %collective-permute-start = (bf16[128,640]{1,0:T(8,128)(2,1)}, bf16[128,640]{1,0:T(8,128)(2,1)S(1)}, u32[]{:S(2)}, u32[]{:S(2)}) collective-permute-start(bf16[128,640]{1,0:T(8,128)(2,1)} %get-tuple-element.34.pack_ref), channel_id=1, source_target_pairs={{64,0},{453,1},{130,2},{259,3},{460,8},{73,9},{138,10},{271,11},{1... | collective-permute-start | bytes 491528 | tf_op jit(solution)/shard_map/ppermute | solution.py:398
  33.5 26.1 %all-to-all-start.1 = ((bf16[4,256,640]{2,1,0:T(8,128)(2,1)}), bf16[4,256,640]{2,1,0:T(8,128)(2,1)S(1)}, u32[]{:S(2)}, u32[]{:S(2)}) async-start(bf16[4,256,640]{2,1,0:T(8,128)(2,1)} %spread_latent.1), calls=%async_computation.1 | async-start | bytes 2621440 | tf_op jit(solution)/shard_map/all_to_all | solution.py:422
  39.0 6.9 %collective-permute-start.2 = (bf16[128,512]{1,0:T(8,128)(2,1)S(1)}, bf16[128,512]{1,0:T(8,128)(2,1)S(1)}, u32[]{:S(2)}, u32[]{:S(2)}) collective-permute-start(bf16[128,512]{1,0:T(8,128)(2,1)S(1)} %order_weight.1.first), channel_id=1, source_target_pairs={{0,16},{16,0},{32,48},{48,32},{1,17},{17,1},{33,49},{49,33},{2,18}... | collective-permute-start | bytes 393224 | tf_op jit(solution)/shard_map/ppermute | solution.py:403
  45.9 9.9 %collective-permute-start.3 = (bf16[256,512]{1,0:T(8,128)(2,1)S(1)}, bf16[256,512]{1,0:T(8,128)(2,1)S(1)}, u32[]{:S(2)}, u32[]{:S(2)}) collective-permute-start(bf16[256,512]{1,0:T(8,128)(2,1)S(1)} %join.2.first), channel_id=1, source_target_pairs={{0,48},{16,32},{32,16},{48,0},{1,49},{17,33},{33,17},{49,1},{2,50}... | collective-permute-start | bytes 786440 | tf_op jit(solution)/shard_map/ppermute | solution.py:403
  55.8 3.8 %copy-start.2 = (bf16[512,512]{1,0:T(8,128)(2,1)}, bf16[512,512]{1,0:T(8,128)(2,1)S(1)}, u32[]{:S(2)}) copy-start(bf16[512,512]{1,0:T(8,128)(2,1)S(1)} %join.3.w_own) | copy-start | bytes 1572868
  55.8 3.8 %collective-permute-start.4 = (bf16[512,512]{1,0:T(8,128)(2,1)S(1)}, bf16[512,512]{1,0:T(8,128)(2,1)S(1)}, u32[]{:S(2)}, u32[]{:S(2)}) collective-permute-start(bf16[512,512]{1,0:T(8,128)(2,1)S(1)} %join.3.w_own), channel_id=1, source_target_pairs={{0,8},{8,0},{1,9},{9,1},{2,10},{10,2},{3,11},{11,3},{4,12},{12,4},... | collective-permute-start | bytes 1572872 | tf_op jit(solution)/shard_map/ppermute | solution.py:403
  59.6 0.8 copy-start.5
  59.6 1.3 copy-start.4
  74.2 4.7 %copy-start.6 = (bf16[512,512]{1,0:T(8,128)(2,1)S(1)}, bf16[512,512]{1,0:T(8,128)(2,1)}, u32[]{:S(2)}) copy-start(bf16[512,512]{1,0:T(8,128)(2,1)} %get-tuple-element.47) | copy-start | bytes 1572868
  74.3 8.5 %copy-start.3 = (bf16[512,512]{1,0:T(8,128)(2,1)S(1)}, bf16[512,512]{1,0:T(8,128)(2,1)}, u32[]{:S(2)}) copy-start(bf16[512,512]{1,0:T(8,128)(2,1)} %get-tuple-element.46.own_ref) | copy-start | bytes 1572868
  74.3 26.9 %all-to-all-start.2 = ((bf16[4,256,640]{2,1,0:T(8,128)(2,1)}), bf16[4,256,640]{2,1,0:T(8,128)(2,1)S(1)}, u32[]{:S(2)}, u32[]{:S(2)}) async-start(bf16[4,256,640]{2,1,0:T(8,128)(2,1)} %get-tuple-element.45), calls=%async_computation.2 | async-start | bytes 2621440 | tf_op jit(solution)/shard_map/all_to_all | solution.py:422
  78.9 3.8 %collective-permute-start.5 = (bf16[512,512]{1,0:T(8,128)(2,1)S(1)}, bf16[512,512]{1,0:T(8,128)(2,1)S(1)}, u32[]{:S(2)}, u32[]{:S(2)}) collective-permute-start(bf16[512,512]{1,0:T(8,128)(2,1)S(1)} %copy-done.6), channel_id=1, source_target_pairs={{0,8},{8,0},{1,9},{9,1},{2,10},{10,2},{3,11},{11,3},{4,12},{12,4},... | collective-permute-start | bytes 1572872 | tf_op jit(solution)/shard_map/ppermute | solution.py:403
  82.8 10.2 %collective-permute-start.6 = (bf16[256,512]{1,0:T(8,128)(2,1)S(1)}, bf16[256,512]{1,0:T(8,128)(2,1)S(1)}, u32[]{:S(2)}, u32[]{:S(2)}) collective-permute-start(bf16[256,512]{1,0:T(8,128)(2,1)S(1)} %get-tuple-element.49), channel_id=1, source_target_pairs={{0,16},{16,0},{32,48},{48,32},{1,17},{17,1},{33,49},{49,33},{2,18}... | collective-permute-start | bytes 786440 | tf_op jit(solution)/shard_map/ppermute | solution.py:403
  93.1 8.1 %collective-permute-start.7 = (bf16[128,512]{1,0:T(8,128)(2,1)S(1)}, bf16[128,512]{1,0:T(8,128)(2,1)S(1)}, u32[]{:S(2)}, u32[]{:S(2)}) collective-permute-start(bf16[128,512]{1,0:T(8,128)(2,1)S(1)} %get-tuple-element.50), channel_id=1, source_target_pairs={{0,48},{16,32},{32,16},{48,0},{1,49},{17,33},{33,17},{49,1},{2,50}... | collective-permute-start | bytes 393224 | tf_op jit(solution)/shard_map/ppermute | solution.py:403
  101.2 47.8 %copy-start.1 = (bf16[1024,512]{1,0:T(8,128)(2,1)S(1)}, bf16[1024,512]{1,0:T(8,128)(2,1)}, u32[]{:S(2)}) copy-start(bf16[1024,512]{1,0:T(8,128)(2,1)} %get-tuple-element.42.weight_ref) | copy-start | bytes 3145732
  101.6 47.4 %copy-start = (bf16[1024,640]{1,0:T(8,128)(2,1)S(1)}, bf16[1024,640]{1,0:T(8,128)(2,1)}, u32[]{:S(2)}) copy-start(bf16[1024,640]{1,0:T(8,128)(2,1)} %get-tuple-element.41.dq_ref) | copy-start | bytes 3932164
  118.8 14.3 %collective-permute-start.8 = (bf16[80,640]{1,0:T(8,128)(2,1)S(1)}, bf16[80,640]{1,0:T(8,128)(2,1)S(1)}, u32[]{:S(2)}, u32[]{:S(2)}) collective-permute-start(bf16[80,640]{1,0:T(8,128)(2,1)S(1)} %get-tuple-element.54.both_ref), channel_id=1, source_target_pairs={{0,256},{64,320},{128,384},{192,448},{256,0},{320,64},{384,128},{4... | collective-permute-start | bytes 307208 | tf_op jit(solution)/shard_map/ppermute | solution.py:403
  133.7 9.8 %collective-permute-start.9 = (bf16[32,640]{1,0:T(8,128)(2,1)S(1)}, bf16[32,640]{1,0:T(8,128)(2,1)S(1)}, u32[]{:S(2)}, u32[]{:S(2)}) collective-permute-start(bf16[32,640]{1,0:T(8,128)(2,1)S(1)} %get-tuple-element.57), channel_id=1, source_target_pairs={{0,260},{64,324},{128,388},{192,452},{256,4},{320,68},{384,132},{4... | collective-permute-start | bytes 122888 | tf_op jit(solution)/shard_map/ppermute | solution.py:413
  144.2 10.9 %all-to-all-start.4 = ((bf16[4,32,640]{2,1,0:T(8,128)(2,1)}), bf16[4,32,640]{2,1,0:T(8,128)(2,1)S(1)}, u32[]{:S(2)}, u32[]{:S(2)}) async-start(bf16[4,32,640]{2,1,0:T(8,128)(2,1)} %keys_sum.1), calls=%async_computation.4 | async-start | bytes 327680 | tf_op jit(solution)/shard_map/all_to_all | solution.py:422

commit v4 on v3

--- a/solution.py
+++ b/solution.py
@@ -65,26 +65,23 @@
 def weight_order(row):
     x, c = lax.axis_index("x"), lax.axis_index("c")
     core, step, rank, n = c ^ (row // 64), (row // 16) % 4, (row % 16) // 2, row % 2
-    return rank * 16 + (x ^ step ^ (step // 2)) * 4 + core * 2 + n
+    return rank * 16 + (x ^ step) * 4 + core * 2 + n
 
 
 FETCH = (((1, -3), (-1, 3), (2, -2), (4, None)), ((-1, 3), (1, -3), (2, -2), (-4, None)))
 
 
-FOLD_X = (0, 2, 1, 3)
-
-
-def call(body, outs, ins, scratch=(), flops=0, smem=(), hbm=(), name=None, vmem=6):
+def call(body, outs, ins, scratch=(), flops=0, smem=(), hbm=(), name=None, vmem=6, out_any=False):
     nbytes = sum(math.prod(s.shape) * s.dtype.itemsize for s in list(outs) + list(ins))
     spaces = [
-        pltpu.SMEM if i in smem else pltpu.HBM if i in hbm else pltpu.VMEM for i in range(len(ins))
+        pltpu.SMEM if i in smem else pl.ANY if i in hbm else pltpu.VMEM for i in range(len(ins))
     ]
     specs = [pl.BlockSpec(memory_space=space) for space in spaces]
     return pl.pallas_call(
         body,
         out_shape=outs,
         in_specs=specs,
-        out_specs=[pl.BlockSpec(memory_space=pltpu.VMEM) for _ in outs],
+        out_specs=[pl.BlockSpec(memory_space=pl.ANY if out_any else pltpu.VMEM) for _ in outs],
         scratch_shapes=list(scratch),
         compiler_params=pltpu.CompilerParams(vmem_limit_bytes=vmem * MIB),
         cost_estimate=pl.CostEstimate(flops=flops, bytes_accessed=nbytes, transcendentals=0),
@@ -145,10 +142,10 @@
     out_ref[...] = nn(chosen(inp == rank * 16 + n * 8 + head), in_ref[:, 0:DC]).astype(bf16)
 
 
-def join_kernel(first, second, out_ref):
-    size = first.shape[0]
-    out_ref[0:size, :] = first[...]
-    out_ref[size : 2 * size, :] = second[...]
+def join_kernel(*refs):
+    size = refs[0].shape[0]
+    for i, part in enumerate(refs[:-1]):
+        refs[-1][i * size : (i + 1) * size, :] = part[...]
 
 
 def spread_latent_kernel(first, second, out_ref):
@@ -157,7 +154,7 @@
         out_ref[y, TOK : 2 * TOK, :] = second[...]
 
 
-def order_queries(nope_ref, rot_ref, up_ref, nope_out, query, up_out):
+def order_queries(nope_ref, rot_ref, nope_out, query):
     by_head = head_major()
     inp, out = iota((DN, DN), 0), iota((DN, DN), 1)
     reorder = chosen(inp == weight_order(out))
@@ -165,11 +162,9 @@
         half, start = g // 4, (g % 4) * 16
         rows = slice(g * 128, (g + 1) * 128)
         nope = nn(nn(by_head, nope_ref[rows, :]).astype(bf16), reorder).astype(bf16)
-        up = nn(by_head, up_ref[rows, :]).astype(bf16)
         for h in range(HEADS):
             place = (half * HEADS + h) * HALF + start
             nope_out[place : place + 16, :] = nope[h * 16 : (h + 1) * 16, :]
-            up_out[place : place + 16, :] = up[h * 16 : (h + 1) * 16, :]
     for h in range(HEADS):
         pick = chosen((inp == out + DR * (h % 2)) & (out < DR))
         turned = nn(rot_ref[:, (h // 2) * 128 : (h // 2 + 1) * 128], pick).astype(bf16)
@@ -178,39 +173,79 @@
             query[place : place + HALF, DC:WIDE] = turned[half * HALF : (half + 1) * HALF, :]
 
 
+def order_upstream(up_ref, up_out):
+    by_head = head_major()
+    for g in range(TOK // 16):
+        half, start = g // 4, (g % 4) * 16
+        up = nn(by_head, up_ref[g * 128 : (g + 1) * 128, :]).astype(bf16)
+        for h in range(HEADS):
+            place = (half * HEADS + h) * HALF + start
+            up_out[place : place + 16, :] = up[h * 16 : (h + 1) * 16, :]
+
+
 def attention_kernel(
     runs_ref,
-    pos_ref,
-    pack_ref,
-    lat_ref,
-    w_own,
-    w_other,
-    nope_in,
-    rot_in,
-    up_in,
-    dkey_out,
-    own_out,
-    other_out,
-    dq_ref,
-    weight_ref,
+    pack_any,
+    lat_any,
+    own_any,
+    other_any,
+    nope_any,
+    rot_any,
+    up_any,
+    dkey_any,
+    master_own_any,
+    master_other_any,
+    dq_any,
+    weight_any,
     keys,
     query,
     score,
     slope,
     dkey,
     dquery,
+    nope_in,
+    rot_in,
+    up_in,
     nope_ref,
     up_ref,
+    weight_ref,
+    dq_ref,
+    dkey_out,
+    own_out,
+    other_out,
+    query_sems,
+    key_sems,
+    weight_sems,
+    out_sems,
 ):
-    order_queries(nope_in, rot_in, up_in, nope_ref, query, up_ref)
     zl, c = lax.axis_index("zl"), lax.axis_index("c")
 
     def place_of(run, start, size):
         return pl.ds(pl.multiple_of(run * HALF + start, size), size)
 
+    def started(pairs, sems, base=0):
+        copies = [
+            pltpu.make_async_copy(src, dst, sems.at[base + i]) for i, (src, dst) in enumerate(pairs)
+        ]
+        for copy in copies:
+            copy.start()
+        return copies
+
+    def finish(copies):
+        for copy in copies:
+            copy.wait()
+
+    query_copies = started(((nope_any, nope_in), (rot_any, rot_in)), query_sems)
+    pairs = []
+    for core, part in enumerate((own_any, other_any)):
+        for step in range(4):
+            at = pl.ds(core * 64 + step * 16, 16)
+            pairs.append((part.at[step], weight_ref.at[:, at, :]))
+    weight_copies = started(pairs, weight_sems)
+    pairs = []
     for half in range(2):
-        run = pos_ref[half * HALF] >> 6
-        keys[place_of(run, 0, HALF), :] = pack_ref[half * HALF : (half + 1) * HALF, :]
+        at = place_of(runs_ref[zl * 2 + half], 0, HALF)
+        pairs.append((pack_any.at[pl.ds(half * HALF, HALF), :], keys.at[at, :]))
     for y in range(4):
         for slot in range(2):
             steps = [FETCH[core][y][slot] for core in range(2)]
@@ -218,81 +253,100 @@
                 continue
             rank = (zl + RANKS + jnp.where(c == 0, steps[0], steps[1])) % RANKS
             for half in range(2):
-                start = slot * TOK + half * HALF
                 at = place_of(runs_ref[rank * 2 + half], 0, HALF)
-                keys[at, :] = lat_ref[y, start : start + HALF, :]
-    for h in range(HEADS):
-        for core, part in enumerate((w_own, w_other)):
-            for step in range(4):
-                at = h * DN + core * 64 + step * 16
-                place = step * 128 + h * 16
-                weight_ref[at : at + 16, :] = part[place : place + 16, :]
+                rows = pl.ds(slot * TOK + half * HALF, HALF)
+                pairs.append((lat_any.at[y, rows, :], keys.at[at, :]))
+    key_copies = started(pairs, key_sems)
+    up_copies = started(((up_any, up_in),), query_sems, 2)
+    dkey[...] = jnp.zeros_like(dkey)
+    dquery[...] = jnp.zeros_like(dquery)
+    finish(query_copies)
+    order_queries(nope_in, rot_in, nope_ref, query)
+    finish(weight_copies)
+    outputs = started([(weight_ref, weight_any)], out_sems)
     for h in range(HEADS):
         pair = [nope_ref[(half * HEADS + h) * HALF : (half * HEADS + h + 1) * HALF, :] for half in range(2)]
-        absorbed = nn(jnp.concatenate(pair, axis=0), weight_ref[h * DN : (h + 1) * DN, :])
+        absorbed = nn(jnp.concatenate(pair, axis=0), weight_ref[h])
         for half in range(2):
             at = (half * HEADS + h) * HALF
             query[at : at + HALF, 0:DC] = absorbed[half * HALF : (half + 1) * HALF, :].astype(bf16)
-    dkey[...] = jnp.zeros_like(dkey)
-
+    finish(key_copies)
+
+    own_runs = [runs_ref[zl * 2 + half] for half in range(2)]
+    first_count = own_runs[0] // 4 + 1
+    steps = []
+    for t in range(5):
+        second = t >= first_count
+        j = jnp.where(second, t - first_count, t)
+        half = jnp.where(second, 1, 0)
+        steps.append(
+            (
+                second,
+                jnp.where(second, own_runs[1], own_runs[0]),
+                j,
+                pl.ds(pl.multiple_of(j * BLOCK, BLOCK), BLOCK),
+                pl.ds(pl.multiple_of(half * ROWS, ROWS), ROWS),
+            )
+        )
+
+    def per_half(values, empty, join):
+        totals = [jnp.full((1, ROWS), empty, f32) for _ in range(2)]
+        for (second, *_), value in zip(steps, values):
+            totals[0] = join(totals[0], jnp.where(second, empty, value))
+            totals[1] = join(totals[1], jnp.where(second, value, empty))
+        return totals
+
+    tops = []
+    for t, (second, run, j, at, rows) in enumerate(steps):
+        s = nt(keys[at, :], query[rows, :]) * (FACTOR * LOG2E)
+        place = run * HALF + iota((1, ROWS), 1) % HALF
+        s = jnp.where(j * BLOCK + iota((BLOCK, ROWS), 0) <= place, s, MASKED)
+        score[t] = s
+        tops.append(jnp.max(s, axis=0, keepdims=True))
+    top = per_half(tops, MASKED, jnp.maximum)
+    finish(up_copies)
+    order_upstream(up_in, up_ref)
+    sums, weighted = [], []
+    for t, (second, run, j, at, rows) in enumerate(steps):
+        d = nt(keys[at, 0:DC], up_ref[rows, :])
+        e = jnp.exp2(score[t] - jnp.where(second, top[1], top[0]))
+        slope[t] = d
+        score[t] = e
+        sums.append(jnp.sum(e, axis=0, keepdims=True))
+        weighted.append(jnp.sum(e * d, axis=0, keepdims=True))
+    inverse = [1.0 / total for total in per_half(sums, 0.0, jnp.add)]
+    inner = [w * i for w, i in zip(per_half(weighted, 0.0, jnp.add), inverse)]
+    for t, (second, run, j, at, rows) in enumerate(steps):
+        prob = score[t] * jnp.where(second, inverse[1], inverse[0])
+        grad = (prob * (slope[t] - jnp.where(second, inner[1], inner[0])) * FACTOR).astype(bf16)
+        dquery[rows, :] += tn(grad, keys[at, :])
+        dkey[at, :] += nn(grad, query[rows, :])
+        dkey[at, 0:DC] += nn(prob.astype(bf16), up_ref[rows, :])
     for half in range(2):
-        rows = slice(half * ROWS, (half + 1) * ROWS)
-        run = pos_ref[half * HALF] >> 6
-        place = run * HALF + iota((1, ROWS), 1) % HALF
-        count = run // 4 + 1
-
-        def scores(j, top):
-            at = pl.ds(pl.multiple_of(j * BLOCK, BLOCK), BLOCK)
-            part = keys[at, :]
-            s = nt(part, query[rows, :]) * (FACTOR * LOG2E)
-            s = jnp.where(j * BLOCK + iota((BLOCK, ROWS), 0) <= place, s, MASKED)
-            score[j] = s
-            slope[j] = nt(part[:, 0:DC], up_ref[rows, :])
-            return jnp.maximum(top, jnp.max(s, axis=0, keepdims=True))
-
-        top = lax.fori_loop(0, count, scores, jnp.full((1, ROWS), MASKED, f32))
-
-        def totals(j, running):
-            total, weighted = running
-            e = jnp.exp2(score[j] - top)
-            score[j] = e
-            return (
-                total + jnp.sum(e, axis=0, keepdims=True),
-                weighted + jnp.sum(e * slope[j], axis=0, keepdims=True),
-            )
-
-        zero = jnp.zeros((1, ROWS), f32)
-        total, weighted = lax.fori_loop(0, count, totals, (zero, zero))
-        inverse = 1.0 / total
-        inner = weighted * inverse
-        dquery[...] = jnp.zeros_like(dquery)
-
-        def grads(j, carry):
-            at = pl.ds(pl.multiple_of(j * BLOCK, BLOCK), BLOCK)
-            prob = score[j] * inverse
-            grad = (prob * (slope[j] - inner) * FACTOR).astype(bf16)
-            dquery[...] += tn(grad, keys[at, :])
-            dkey[at, :] += nn(grad, query[rows, :])
-            dkey[at, 0:DC] += nn(prob.astype(bf16), up_ref[rows, :])
-            return carry
-
-        lax.fori_loop(0, count, grads, 0)
-        dq_ref[rows, :] = dquery[...].astype(bf16)
+        rows = pl.ds(half * ROWS, ROWS)
+        dq_ref[rows, :] = dquery[rows, :].astype(bf16)
+        outputs += started([(dq_ref.at[rows, :], dq_any.at[rows, :])], out_sems, 1 + half)
 
     for quarter in range(4):
         for k in range(RANKS):
             run = runs_ref[((zl & 4) ^ k) * 2 + quarter // 2]
             at = place_of(run, (quarter % 2) * QUARTER, QUARTER)
             dkey_out[quarter, k * QUARTER : (k + 1) * QUARTER, :] = dkey[at, :].astype(bf16)
+        outputs += started(
+            [(dkey_out.at[quarter], dkey_any.at[quarter])], out_sems, 3 + quarter
+        )
     for h in range(HEADS):
         places = [slice((half * HEADS + h) * HALF, (half * HEADS + h + 1) * HALF) for half in range(2)]
         nope = jnp.concatenate([nope_ref[p, :] for p in places], axis=0)
         dq = jnp.concatenate([dq_ref[p, 0:DC] for p in places], axis=0)
         master = tn(nope, dq).astype(bf16)
         for core, part in enumerate((own_out, other_out)):
-            for k, step in enumerate(FOLD_X):
+            for step in range(4):
                 at = core * 64 + step * 16
-                part[k * 128 + h * 16 : k * 128 + h * 16 + 16, :] = master[at : at + 16, :]
+                part[step * 128 + h * 16 : step * 128 + h * 16 + 16, :] = master[at : at + 16, :]
+    pairs = ((own_out, master_own_any), (other_out, master_other_any))
+    outputs += started(pairs, out_sems, 7)
+    finish(outputs)
 
 
 def query_grads_kernel(dq_ref, weight_ref, nope_out, rot_out, scratch):
@@ -304,7 +358,7 @@
     for h in range(HEADS):
         places = [slice((half * HEADS + h) * HALF, (half * HEADS + h + 1) * HALF) for half in range(2)]
         dq = jnp.concatenate([dq_ref[p, 0:DC] for p in places], axis=0)
-        grad = nt(dq, weight_ref[h * DN : (h + 1) * DN, :]).astype(bf16)
+        grad = nt(dq, weight_ref[h]).astype(bf16)
         scratch[h * TOK : (h + 1) * TOK, :] = nn(grad, reorder).astype(bf16)
     by_token = token_major()
     for g in range(TOK // 16):
@@ -325,21 +379,17 @@
     return total
 
 
-def master_plane_kernel(own_ref, got_ref, keep_ref, send_ref):
+def master_plane_kernel(own_ref, got_ref, keep_ref, *sends):
     total = own_ref[...].astype(f32) + got_ref[...].astype(f32)
-    keep_ref[...] = total[0:256, :]
-    send_ref[...] = total[256:512, :].astype(bf16)
-
-
-def fold_kernel(keep_ref, got_ref, keep_out, send_out):
-    size = keep_out.shape[0]
-    keep_out[...] = keep_ref[0:size, :] + got_ref[0:size, :].astype(f32)
-    send_out[...] = (keep_ref[size:, :] + got_ref[size:, :].astype(f32)).astype(bf16)
-
-
-def plane_kernel(dkey_ref, keep_ref, got_ref, out_ref):
+    keep_ref[...] = total[0:128, :]
+    for i, send in enumerate(sends):
+        send[...] = total[(i + 1) * 128 : (i + 2) * 128, :].astype(bf16)
+
+
+def plane_kernel(dkey_ref, keep_ref, *refs):
     keys = total_of([dkey_ref[y] for y in range(4)]).astype(bf16)
-    master = (keep_ref[...] + got_ref[...].astype(f32)).astype(bf16)
+    out_ref = refs[-1]
+    master = (keep_ref[...] + total_of([part[...] for part in refs[:-1]])).astype(bf16)
     zl = lax.axis_index("zl")
     out, inp = iota((128, 128), 0), iota((128, 128), 1)
     rank, n, head = (out // 16) ^ (zl & 4), (out % 16) // 8, out % 8
@@ -361,17 +411,20 @@
     keep_out[...] = total[2 * QUARTER : 2 * QUARTER + WROWS, 0:DC]
 
 
-def cross_kernel(both_ref, got_ref, master_ref, keep_out, send_out, master_out):
+def cross_kernel(both_ref, got_ref, keep_out, send_out):
     low, high = slice(0, QUARTER), slice(QUARTER, 2 * QUARTER)
     keep_out[...] = total_of([both_ref[low, :], got_ref[high, :]]).astype(bf16)
-    send_out[...] = total_of([both_ref[high, :], got_ref[low, :]]).astype(bf16)
-    master_out[...] = master_ref[...] + got_ref[2 * QUARTER :, 0:DC].astype(f32)
-
-
-def keys_sum_kernel(keep_ref, got_ref, out_ref):
-    keys = total_of([keep_ref[...], got_ref[...]]).astype(bf16)
+    send_out[low, :] = total_of([both_ref[high, :], got_ref[low, :]]).astype(bf16)
+    send_out[QUARTER:, :] = both_ref[2 * QUARTER :, :]
+
+
+def keys_sum_kernel(keep_ref, got_ref, master_ref, first_ref, out_ref, master_out):
+    keys = total_of([keep_ref[...], got_ref[0:QUARTER, :]]).astype(bf16)
     for y in range(4):
         out_ref[y] = keys
+    inside = lax.axis_index("c") == 0
+    got = jnp.where(inside, first_ref[2 * QUARTER :, 0:DC].astype(f32), got_ref[QUARTER:, 0:DC].astype(f32))
+    master_out[...] = master_ref[...] + got
 
 
 def keys_last_kernel(in_ref, latent_ref, rotary_ref):
@@ -403,14 +456,17 @@
     return lax.ppermute(block, axis, [(i, i ^ step) for i in range(n)])
 
 
-def over_edge(block):
-    def partner(place):
-        return (place + (4 if place % 8 >= 4 else -4)) % 16
-
-    def index(place):
-        return place % 8 * 2 + place // 8
-
-    return lax.ppermute(block, ("zl", "zh"), [(index(p), index(partner(p))) for p in range(16)])
+def across_half(block, turn):
+    def partner(place, c):
+        inside = turn == c
+        up = (place % 8 < 4) == inside
+        return (place + (4 if up else -4)) % 16
+
+    def index(place, c):
+        return (place % 8 * 2 + c) * 2 + place // 8
+
+    pairs = [(index(p, c), index(partner(p, c), c)) for p in range(16) for c in range(2)]
+    return lax.ppermute(block, ("zl", "c", "zh"), pairs)
 
 
 def quads(blocks):
@@ -449,8 +505,8 @@
     (w_own,) = call(
         order_weight_kernel, (shape(128, DC),), (weight_ranks.reshape(128, WIDE),), name="order_weight"
     )
-    for size, step in ((256, 1), (512, 3)):
-        (w_own,) = call(join_kernel, (shape(size, DC),), (w_own, across(w_own, "x", step)), name="join")
+    far, left, right = [across(w_own, "x", step) for step in (2, 1, 3)]
+    (w_own,) = call(join_kernel, (shape(512, DC),), (w_own, left, far, right), name="join")
     w_other = across(w_own, "c", 1)
     latent_all, w_own, w_other = together((latent_all, w_own, w_other))
     runs = weight_ranks[:, 0, DC : DC + 2].astype(jnp.int32).reshape(16)
@@ -461,15 +517,14 @@
             shape(512, DC),
             shape(512, DC),
             shape(1024, WIDE),
-            shape(1024, DC),
+            shape(HEADS, DN, DC),
         ),
         (
             runs,
-            positions,
             pack,
             latent_all,
-            w_own,
-            w_other,
+            w_own.reshape(4, HEADS, 16, DC),
+            w_other.reshape(4, HEADS, 16, DC),
             nope.reshape(1024, DN),
             rotary,
             upstream.reshape(1024, DC),
@@ -477,18 +532,39 @@
         scratch=(
             pltpu.VMEM((1024, WIDE), bf16),
             pltpu.VMEM((1024, WIDE), bf16),
-            pltpu.VMEM((4, BLOCK, ROWS), f32),
-            pltpu.VMEM((4, BLOCK, ROWS), f32),
+            pltpu.VMEM((5, BLOCK, ROWS), f32),
+            pltpu.VMEM((5, BLOCK, ROWS), f32),
             pltpu.VMEM((1024, WIDE), f32),
-            pltpu.VMEM((ROWS, WIDE), f32),
+            pltpu.VMEM((1024, WIDE), f32),
+            pltpu.VMEM((1024, DN), bf16),
+            pltpu.VMEM((TOK, HEADS * DR), bf16),
+            pltpu.VMEM((1024, DC), bf16),
             pltpu.VMEM((1024, DN), bf16),
             pltpu.VMEM((1024, DC), bf16),
+            pltpu.VMEM((HEADS, DN, DC), bf16),
+            pltpu.VMEM((1024, WIDE), bf16),
+            pltpu.VMEM((4, 256, WIDE), bf16),
+            pltpu.VMEM((512, DC), bf16),
+            pltpu.VMEM((512, DC), bf16),
+            pltpu.SemaphoreType.DMA((3,)),
+            pltpu.SemaphoreType.DMA((16,)),
+            pltpu.SemaphoreType.DMA((8,)),
+            pltpu.SemaphoreType.DMA((9,)),
         ),
-        smem=(0, 1),
+        smem=(0,),
+        hbm=(1, 2, 3, 4, 5, 6, 7),
+        out_any=True,
         flops=2 * 512 * 1280 * 2944,
         name="attention",
         vmem=56,
     )
+    keep, left, far, right = call(
+        master_plane_kernel,
+        (shape(128, DC, dtype=f32),) + (shape(128, DC),) * 3,
+        (own, across(other, "c", 1)),
+        name="master_plane",
+    )
+    got = [across(part, "x", step) for part, step in ((far, 2), (left, 1), (right, 3))]
     nope_grad, rot_grad = call(
         query_grads_kernel,
         (shape(1024, DN), shape(TOK, HEADS * DR)),
@@ -497,25 +573,20 @@
         flops=2 * 1024 * 128 * 768,
         name="query_grads",
     )
-    def folded(body, size, ins, name):
-        return call(body, (shape(size, DC, dtype=f32), shape(size, DC)), ins, name=name)
-
-    keep, send = folded(master_plane_kernel, 256, (own, across(other, "c", 1)), "master_plane")
-    keep, send = folded(fold_kernel, 128, (keep, across(send, "x", 1)), "fold")
-    dkey_planes, got = together((everyone(dkey, "y"), across(send, "x", 3)))
-    (blocks,) = call(plane_kernel, (shape(4, 96, WIDE),), (dkey_planes, keep, got), name="plane")
+    dkey_planes, nope_grad, rot_grad, *got = together((everyone(dkey, "y"), nope_grad, rot_grad, *got))
+    (blocks,) = call(plane_kernel, (shape(4, 96, WIDE),), (dkey_planes, keep, *got), name="plane")
     both, keep = call(
         quad_sum_kernel, (shape(80, WIDE), shape(WROWS, DC, dtype=f32)), (quads(blocks),), name="quad_sum"
     )
-    got = across(both, "zl", 4)
-    keep, send, master_grad = call(
-        cross_kernel,
-        (shape(QUARTER, WIDE), shape(QUARTER, WIDE), shape(WROWS, DC, dtype=f32)),
-        (both, got, keep),
-        name="cross",
-    )
-    (dkey_sum,) = call(
-        keys_sum_kernel, (shape(4, QUARTER, WIDE),), (keep, over_edge(send)), name="keys_sum"
+    first = across_half(both, 0)
+    own, send = call(
+        cross_kernel, (shape(QUARTER, WIDE), shape(QUARTER + WROWS, WIDE)), (both, first), name="cross"
+    )
+    dkey_sum, master_grad = call(
+        keys_sum_kernel,
+        (shape(4, QUARTER, WIDE), shape(WROWS, DC, dtype=f32)),
+        (own, across_half(send, 1), keep, first),
+        name="keys_sum",
     )
     dkey_all = everyone(dkey_sum, "y")
     latent_grad, keys_grad = call(

time: 157 us -> 148 us (0.943)
  waiting for transfers between devices: 55.1 us -> 28.5 us
  blocking collectives: 17.2 us -> 27.8 us
  starting transfers between devices: 59.5 us -> 67.8 us
  Pallas kernels: 21.4 us -> 18.9 us
    ppermute x7 -> x8, waiting for transfers between devices: 38 us -> 8.9 us  [across(): return lax.ppermute(block, axis, [(i, i ^ step) for i in range(n)])]
    all_to_all x0 -> x1, blocking collectives: none -> 10.1 us  [everyone(): return lax.all_to_all(blocks, axes, 0, 0, tiled=True)]
    ppermute x1 -> x2, starting transfers between devices: 3.17 us -> 10.7 us  [across_half(): return lax.ppermute(block, ('zl', 'c', 'zh'), pairs)]
    ppermute x1 -> x2, waiting for transfers between devices: 6.61 us -> 12.8 us  [across_half(): return lax.ppermute(block, ('zl', 'c', 'zh'), pairs)]
    ppermute x7 -> x8, starting transfers between devices: 18.3 us -> 23.6 us  [across(): return lax.ppermute(block, axis, [(i, i ^ step) for i in range(n)])]
    all_to_all x4 -> x3, starting transfers between devices: 27.3 us -> 22.8 us  [everyone(): return lax.all_to_all(blocks, axes, 0, 0, tiled=True)]
    all_to_all x4 -> x3, waiting for transfers between devices: 5.06 us -> 1.33 us  [everyone(): return lax.all_to_all(blocks, axes, 0, 0, tiled=True)]
    pallas_call x14 -> x12, Pallas kernels: 21.4 us -> 18.9 us  [call(): pl.pallas_call(body, out_shape=outs, in_specs=specs, out_specs=[pl.BlockS...]
  transfers between devices with their start and end apart: 14 -> 15, of which waited for: 12 -> 12; matrix products, arithmetic and copies ran while one was open for 0% -> 0% of each run, Pallas kernels for 2% -> 2%
where the time goes in v4:
time: 148 us; the launch traced here: 146 us
  starting transfers between devices  67.8 us (46%)
  waiting for transfers between devices  28.5 us (19%)
  blocking collectives  27.8 us (19%)
  Pallas kernels  18.9 us (13%)
  local copies, waits for them, and re-layouts  1.78 us (1%)
    ppermute x8, starting transfers between devices, across(): return lax.ppermute(block, axis, [(i, i ^ step) for i in range(n)])  23.6 us
    all_to_all x3, starting transfers between devices, everyone(): return lax.all_to_all(blocks, axes, 0, 0, tiled=True)  22.8 us
    pallas_call x12, Pallas kernels, call(): pl.pallas_call(body, out_shape=outs, in_specs=specs, out_specs=[pl.BlockS...  18.9 us
    all_to_all x1, blocking collectives, quads(): lax.all_to_all(blocks, 'zl', 0, 0, tiled=True, axis_index_groups=groups)  17.6 us
    ppermute x2, waiting for transfers between devices, across_half(): return lax.ppermute(block, ('zl', 'c', 'zh'), pairs)  12.8 us
    ppermute x2, starting transfers between devices, across_half(): return lax.ppermute(block, ('zl', 'c', 'zh'), pairs)  10.7 us
    ppermute x2, starting transfers between devices, fetch(): return lax.ppermute(block, axes, pairs)  10.7 us
    all_to_all x1, blocking collectives, everyone(): return lax.all_to_all(blocks, axes, 0, 0, tiled=True)  10.1 us
  transfers between devices with their start and end apart: 15, of which 12 were waited for; matrix products, arithmetic and copies ran while one was open for 0% of the time, Pallas kernels for 2%

profile of v4, /device:TPU:6, one launch (start us, length us, event | category | flops | bytes accessed | tf_op | source)
XLA Modules:
  0.0 145.5 jit_solution(10057099104697116447)
XLA Ops:
  2.5 12.5 %all-to-all-start = ((bf16[8,16,640]{2,1,0:T(8,128)(2,1)}), bf16[8,16,640]{2,1,0:T(8,128)(2,1)S(1)}, u32[]{:S(2)}, u32[]{:S(2)}) async-start(bf16[8,16,640]{2,1,0:T(8,128)(2,1)} %get-tuple-element.38), calls=%async_computation | async-start | bytes 327680 | tf_op jit(solution)/shard_map/all_to_all | solution.py:478
  15.0 5.7 %collective-permute-start.1 = (bf16[128,640]{1,0:T(8,128)(2,1)}, bf16[128,640]{1,0:T(8,128)(2,1)S(1)}, u32[]{:S(2)}, u32[]{:S(2)}) collective-permute-start(bf16[128,640]{1,0:T(8,128)(2,1)} %get-tuple-element.39.pack_any), channel_id=1, source_target_pairs={{324,0},{193,1},{390,2},{200,8},{333,9},{398,10},{388,64},{257,65}... | collective-permute-start | bytes 491528 | tf_op jit(solution)/shard_map/ppermute | solution.py:451
  20.7 5.0 %collective-permute-start = (bf16[128,640]{1,0:T(8,128)(2,1)}, bf16[128,640]{1,0:T(8,128)(2,1)S(1)}, u32[]{:S(2)}, u32[]{:S(2)}) collective-permute-start(bf16[128,640]{1,0:T(8,128)(2,1)} %get-tuple-element.39.pack_any), channel_id=1, source_target_pairs={{64,0},{453,1},{130,2},{259,3},{460,8},{73,9},{138,10},{271,11},{1... | collective-permute-start | bytes 491528 | tf_op jit(solution)/shard_map/ppermute | solution.py:451
  25.7 5.4 %collective-permute-done.1.second = bf16[128,640]{1,0:T(8,128)(2,1)S(1)} collective-permute-done((bf16[128,640]{1,0:T(8,128)(2,1)}, bf16[128,640]{1,0:T(8,128)(2,1)S(1)}, u32[]{:S(2)}, u32[]{:S(2)}) %collective-permute-start.1) | collective-permute-done | bytes 163872 | tf_op jit(solution)/shard_map/ppermute | solution.py:451
  33.5 5.3 %all-to-all-start.1 = ((bf16[4,256,640]{2,1,0:T(8,128)(2,1)}), bf16[4,256,640]{2,1,0:T(8,128)(2,1)S(1)}, u32[]{:S(2)}, u32[]{:S(2)}) async-start(bf16[4,256,640]{2,1,0:T(8,128)(2,1)} %spread_latent.1), calls=%async_computation.1 | async-start | bytes 2621440 | tf_op jit(solution)/shard_map/all_to_all | solution.py:478
  39.0 2.4 %collective-permute-start.4 = (bf16[128,512]{1,0:T(8,128)(2,1)S(1)}, bf16[128,512]{1,0:T(8,128)(2,1)S(1)}, u32[]{:S(2)}, u32[]{:S(2)}) collective-permute-start(bf16[128,512]{1,0:T(8,128)(2,1)S(1)} %order_weight.1.refs_0_), channel_id=1, source_target_pairs={{0,48},{16,32},{32,16},{48,0},{1,49},{17,33},{33,17},{49,1},{2,50}... | collective-permute-start | bytes 393224 | tf_op jit(solution)/shard_map/ppermute | solution.py:456
  41.4 4.3 %collective-permute-start.3 = (bf16[128,512]{1,0:T(8,128)(2,1)S(1)}, bf16[128,512]{1,0:T(8,128)(2,1)S(1)}, u32[]{:S(2)}, u32[]{:S(2)}) collective-permute-start(bf16[128,512]{1,0:T(8,128)(2,1)S(1)} %order_weight.1.refs_0_), channel_id=1, source_target_pairs={{0,32},{16,48},{32,0},{48,16},{1,33},{17,49},{33,1},{49,17},{2,34}... | collective-permute-start | bytes 393224 | tf_op jit(solution)/shard_map/ppermute | solution.py:456
  45.7 3.1 %collective-permute-start.2 = (bf16[128,512]{1,0:T(8,128)(2,1)S(1)}, bf16[128,512]{1,0:T(8,128)(2,1)S(1)}, u32[]{:S(2)}, u32[]{:S(2)}) collective-permute-start(bf16[128,512]{1,0:T(8,128)(2,1)S(1)} %order_weight.1.refs_0_), channel_id=1, source_target_pairs={{0,16},{16,0},{32,48},{48,32},{1,17},{17,1},{33,49},{49,33},{2,18}... | collective-permute-start | bytes 393224 | tf_op jit(solution)/shard_map/ppermute | solution.py:456
  49.9 2.8 %collective-permute-done.2.refs_1_ = bf16[128,512]{1,0:T(8,128)(2,1)S(1)} collective-permute-done((bf16[128,512]{1,0:T(8,128)(2,1)S(1)}, bf16[128,512]{1,0:T(8,128)(2,1)S(1)}, u32[]{:S(2)}, u32[]{:S(2)}) %collective-permute-start.2) | collective-permute-done | bytes 131104 | tf_op jit(solution)/shard_map/ppermute | solution.py:456
  52.7 1.9 %collective-permute-start.5 = (bf16[512,512]{1,0:T(8,128)(2,1)S(1)}, bf16[512,512]{1,0:T(8,128)(2,1)S(1)}, u32[]{:S(2)}, u32[]{:S(2)}) collective-permute-start(bf16[512,512]{1,0:T(8,128)(2,1)S(1)} %join.1), channel_id=1, source_target_pairs={{0,8},{8,0},{1,9},{9,1},{2,10},{10,2},{3,11},{11,3},{4,12},{12,4},... | collective-permute-start | bytes 1572872 | tf_op jit(solution)/shard_map/ppermute | solution.py:456
  57.8 11.5 %attention.1 = (bf16[4,256,640]{2,1,0:T(8,128)(2,1)}, bf16[512,512]{1,0:T(8,128)(2,1)}, bf16[512,512]{1,0:T(8,128)(2,1)}, bf16[1024,640]{1,0:T(8,128)(2,1)}, bf16[8,128,512]{2,1,0:T(8,128)(2,1)}) custom-call(s32[16]{0:T(128)} %reshape.46.runs_ref, bf16[128,640]{1,0:T(8,128)(2,1)} %get-tuple-element.39.pack_any, bf16[4,256,640]{2,1,0:T(8,128)(2,1)} %copy-done.4, ...), custom_call_target="tpu_custom_call" | custom-call | flops 3858759680 | bytes 8683584 | tf_op jit(solution)/shard_map/attention/pallas_call | solution.py:80
  69.3 4.9 %all-to-all-start.2 = ((bf16[4,256,640]{2,1,0:T(8,128)(2,1)}), bf16[4,256,640]{2,1,0:T(8,128)(2,1)S(1)}, u32[]{:S(2)}, u32[]{:S(2)}) async-start(bf16[4,256,640]{2,1,0:T(8,128)(2,1)} %get-tuple-element.46), calls=%async_computation.2 | async-start | bytes 2621440 | tf_op jit(solution)/shard_map/all_to_all | solution.py:478
  74.2 2.0 %collective-permute-start.6 = (bf16[512,512]{1,0:T(8,128)(2,1)}, bf16[512,512]{1,0:T(8,128)(2,1)S(1)}, u32[]{:S(2)}, u32[]{:S(2)}) collective-permute-start(bf16[512,512]{1,0:T(8,128)(2,1)} %get-tuple-element.52), channel_id=1, source_target_pairs={{0,8},{8,0},{1,9},{9,1},{2,10},{10,2},{3,11},{11,3},{4,12},{12,4},... | collective-permute-start | bytes 1572872 | tf_op jit(solution)/shard_map/ppermute | solution.py:456
  76.2 2.1 %collective-permute-done.6.got_ref = bf16[512,512]{1,0:T(8,128)(2,1)S(1)} collective-permute-done((bf16[512,512]{1,0:T(8,128)(2,1)}, bf16[512,512]{1,0:T(8,128)(2,1)S(1)}, u32[]{:S(2)}, u32[]{:S(2)}) %collective-permute-start.6) | collective-permute-done | bytes 524320 | tf_op jit(solution)/shard_map/ppermute | solution.py:456
  78.5 3.3 %collective-permute-start.7 = (bf16[128,512]{1,0:T(8,128)(2,1)S(1)}, bf16[128,512]{1,0:T(8,128)(2,1)S(1)}, u32[]{:S(2)}, u32[]{:S(2)}) collective-permute-start(bf16[128,512]{1,0:T(8,128)(2,1)S(1)} %get-tuple-element.53), channel_id=1, source_target_pairs={{0,32},{16,48},{32,0},{48,16},{1,33},{17,49},{33,1},{49,17},{2,34}... | collective-permute-start | bytes 393224 | tf_op jit(solution)/shard_map/ppermute | solution.py:456
  81.8 2.4 %collective-permute-start.8 = (bf16[128,512]{1,0:T(8,128)(2,1)S(1)}, bf16[128,512]{1,0:T(8,128)(2,1)S(1)}, u32[]{:S(2)}, u32[]{:S(2)}) collective-permute-start(bf16[128,512]{1,0:T(8,128)(2,1)S(1)} %get-tuple-element.54), channel_id=1, source_target_pairs={{0,16},{16,0},{32,48},{48,32},{1,17},{17,1},{33,49},{49,33},{2,18}... | collective-permute-start | bytes 393224 | tf_op jit(solution)/shard_map/ppermute | solution.py:456
  84.2 4.1 %collective-permute-start.9 = (bf16[128,512]{1,0:T(8,128)(2,1)S(1)}, bf16[128,512]{1,0:T(8,128)(2,1)S(1)}, u32[]{:S(2)}, u32[]{:S(2)}) collective-permute-start(bf16[128,512]{1,0:T(8,128)(2,1)S(1)} %get-tuple-element.55), channel_id=1, source_target_pairs={{0,48},{16,32},{32,16},{48,0},{1,49},{17,33},{33,17},{49,1},{2,50}... | collective-permute-start | bytes 393224 | tf_op jit(solution)/shard_map/ppermute | solution.py:456
  88.3 2.2 %query_grads.1 = (bf16[1024,128]{1,0:T(8,128)(2,1)}, bf16[128,512]{1,0:T(8,128)(2,1)}) custom-call(bf16[1024,640]{1,0:T(8,128)(2,1)S(1)} %copy-done, bf16[8,128,512]{2,1,0:T(8,128)(2,1)S(1)} %copy-done.1), custom_call_target="tpu_custom_call" | custom-call | flops 201326592 | bytes 2752512 | tf_op jit(solution)/shard_map/query_grads/pallas_call | solution.py:80
  92.8 17.6 %all_to_all.25.in_ref = bf16[4,96,640]{2,1,0:T(8,128)(2,1)S(1)} all-to-all(bf16[4,96,640]{2,1,0:T(8,128)(2,1)S(1)} %plane.1), channel_id=1, replica_groups={{0,64,128,192},{256,320,384,448},{1,65,129,193},{257,321,385,449},{2,66..., dimensions={0} | all-to-all | bytes 983040 | tf_op jit(solution)/shard_map/all_to_all | solution.py:474
  110.5 5.3 %collective-permute-start.10 = (bf16[80,640]{1,0:T(8,128)(2,1)S(1)}, bf16[80,640]{1,0:T(8,128)(2,1)S(1)}, u32[]{:S(2)}, u32[]{:S(2)}) collective-permute-start(bf16[80,640]{1,0:T(8,128)(2,1)S(1)} %get-tuple-element.63.both_ref), channel_id=1, source_target_pairs={{0,256},{8,268},{64,320},{72,332},{128,384},{136,396},{192,448},{2... | collective-permute-start | bytes 307208 | tf_op jit(solution)/shard_map/ppermute | solution.py:469
  115.8 8.2 %collective-permute-done.10.got_ref.first_ref = bf16[80,640]{1,0:T(8,128)(2,1)S(1)} collective-permute-done((bf16[80,640]{1,0:T(8,128)(2,1)S(1)}, bf16[80,640]{1,0:T(8,128)(2,1)S(1)}, u32[]{:S(2)}, u32[]{:S(2)}) %collective-permute-start.10) | collective-permute-done | bytes 102432 | tf_op jit(solution)/shard_map/ppermute | solution.py:469
  124.0 5.4 %collective-permute-start.11 = (bf16[48,640]{1,0:T(8,128)(2,1)S(1)}, bf16[48,640]{1,0:T(8,128)(2,1)S(1)}, u32[]{:S(2)}, u32[]{:S(2)}) collective-permute-start(bf16[48,640]{1,0:T(8,128)(2,1)S(1)} %get-tuple-element.65), channel_id=1, source_target_pairs={{0,260},{8,264},{64,324},{72,328},{128,388},{136,392},{192,452},{2... | collective-permute-start | bytes 184328 | tf_op jit(solution)/shard_map/ppermute | solution.py:469
  129.5 4.6 %collective-permute-done.11.got_ref = bf16[48,640]{1,0:T(8,128)(2,1)S(1)} collective-permute-done((bf16[48,640]{1,0:T(8,128)(2,1)S(1)}, bf16[48,640]{1,0:T(8,128)(2,1)S(1)}, u32[]{:S(2)}, u32[]{:S(2)}) %collective-permute-start.11) | collective-permute-done | bytes 61472 | tf_op jit(solution)/shard_map/ppermute | solution.py:469
  134.7 10.1 %all_to_all.26.in_ref = bf16[4,32,640]{2,1,0:T(8,128)(2,1)S(1)} all-to-all(bf16[4,32,640]{2,1,0:T(8,128)(2,1)S(1)} %get-tuple-element.67), channel_id=1, replica_groups=mesh['zl'=8,'x'=4,'c'=2,'zh'=2,'y'=4] {'y'}, dimensions={0} | all-to-all | bytes 327680 | tf_op jit(solution)/shard_map/all_to_all | solution.py:478
  (34 shorter events, 12.4 us)
Async XLA Ops:
  2.5 29.8 %all-to-all-start = ((bf16[8,16,640]{2,1,0:T(8,128)(2,1)}), bf16[8,16,640]{2,1,0:T(8,128)(2,1)S(1)}, u32[]{:S(2)}, u32[]{:S(2)}) async-start(bf16[8,16,640]{2,1,0:T(8,128)(2,1)} %get-tuple-element.38), calls=%async_computation | async-start | bytes 327680 | tf_op jit(solution)/shard_map/all_to_all | solution.py:478
  15.0 16.1 %collective-permute-start.1 = (bf16[128,640]{1,0:T(8,128)(2,1)}, bf16[128,640]{1,0:T(8,128)(2,1)S(1)}, u32[]{:S(2)}, u32[]{:S(2)}) collective-permute-start(bf16[128,640]{1,0:T(8,128)(2,1)} %get-tuple-element.39.pack_any), channel_id=1, source_target_pairs={{324,0},{193,1},{390,2},{200,8},{333,9},{398,10},{388,64},{257,65}... | collective-permute-start | bytes 491528 | tf_op jit(solution)/shard_map/ppermute | solution.py:451
  20.7 10.4 %collective-permute-start = (bf16[128,640]{1,0:T(8,128)(2,1)}, bf16[128,640]{1,0:T(8,128)(2,1)S(1)}, u32[]{:S(2)}, u32[]{:S(2)}) collective-permute-start(bf16[128,640]{1,0:T(8,128)(2,1)} %get-tuple-element.39.pack_any), channel_id=1, source_target_pairs={{64,0},{453,1},{130,2},{259,3},{460,8},{73,9},{138,10},{271,11},{1... | collective-permute-start | bytes 491528 | tf_op jit(solution)/shard_map/ppermute | solution.py:451
  33.5 23.1 %all-to-all-start.1 = ((bf16[4,256,640]{2,1,0:T(8,128)(2,1)}), bf16[4,256,640]{2,1,0:T(8,128)(2,1)S(1)}, u32[]{:S(2)}, u32[]{:S(2)}) async-start(bf16[4,256,640]{2,1,0:T(8,128)(2,1)} %spread_latent.1), calls=%async_computation.1 | async-start | bytes 2621440 | tf_op jit(solution)/shard_map/all_to_all | solution.py:478
  39.0 10.9 %collective-permute-start.4 = (bf16[128,512]{1,0:T(8,128)(2,1)S(1)}, bf16[128,512]{1,0:T(8,128)(2,1)S(1)}, u32[]{:S(2)}, u32[]{:S(2)}) collective-permute-start(bf16[128,512]{1,0:T(8,128)(2,1)S(1)} %order_weight.1.refs_0_), channel_id=1, source_target_pairs={{0,48},{16,32},{32,16},{48,0},{1,49},{17,33},{33,17},{49,1},{2,50}... | collective-permute-start | bytes 393224 | tf_op jit(solution)/shard_map/ppermute | solution.py:456
  41.4 8.5 %collective-permute-start.3 = (bf16[128,512]{1,0:T(8,128)(2,1)S(1)}, bf16[128,512]{1,0:T(8,128)(2,1)S(1)}, u32[]{:S(2)}, u32[]{:S(2)}) collective-permute-start(bf16[128,512]{1,0:T(8,128)(2,1)S(1)} %order_weight.1.refs_0_), channel_id=1, source_target_pairs={{0,32},{16,48},{32,0},{48,16},{1,33},{17,49},{33,1},{49,17},{2,34}... | collective-permute-start | bytes 393224 | tf_op jit(solution)/shard_map/ppermute | solution.py:456
  45.7 6.9 %collective-permute-start.2 = (bf16[128,512]{1,0:T(8,128)(2,1)S(1)}, bf16[128,512]{1,0:T(8,128)(2,1)S(1)}, u32[]{:S(2)}, u32[]{:S(2)}) collective-permute-start(bf16[128,512]{1,0:T(8,128)(2,1)S(1)} %order_weight.1.refs_0_), channel_id=1, source_target_pairs={{0,16},{16,0},{32,48},{48,32},{1,17},{17,1},{33,49},{49,33},{2,18}... | collective-permute-start | bytes 393224 | tf_op jit(solution)/shard_map/ppermute | solution.py:456
  52.7 3.9 %copy-start.2 = (bf16[512,512]{1,0:T(8,128)(2,1)}, bf16[512,512]{1,0:T(8,128)(2,1)S(1)}, u32[]{:S(2)}) copy-start(bf16[512,512]{1,0:T(8,128)(2,1)S(1)} %join.1) | copy-start | bytes 1572868
  52.7 3.8 %collective-permute-start.5 = (bf16[512,512]{1,0:T(8,128)(2,1)S(1)}, bf16[512,512]{1,0:T(8,128)(2,1)S(1)}, u32[]{:S(2)}, u32[]{:S(2)}) collective-permute-start(bf16[512,512]{1,0:T(8,128)(2,1)S(1)} %join.1), channel_id=1, source_target_pairs={{0,8},{8,0},{1,9},{9,1},{2,10},{10,2},{3,11},{11,3},{4,12},{12,4},... | collective-permute-start | bytes 1572872 | tf_op jit(solution)/shard_map/ppermute | solution.py:456
  56.5 0.8 copy-start.5
  56.6 1.2 copy-start.4
  69.2 9.1 %copy-start.3 = (bf16[512,512]{1,0:T(8,128)(2,1)S(1)}, bf16[512,512]{1,0:T(8,128)(2,1)}, u32[]{:S(2)}) copy-start(bf16[512,512]{1,0:T(8,128)(2,1)} %get-tuple-element.51.own_ref) | copy-start | bytes 1572868
  69.2 19.1 %copy-start = (bf16[1024,640]{1,0:T(8,128)(2,1)S(1)}, bf16[1024,640]{1,0:T(8,128)(2,1)}, u32[]{:S(2)}) copy-start(bf16[1024,640]{1,0:T(8,128)(2,1)} %get-tuple-element.47.dq_ref) | copy-start | bytes 3932164
  69.3 23.2 %all-to-all-start.2 = ((bf16[4,256,640]{2,1,0:T(8,128)(2,1)}), bf16[4,256,640]{2,1,0:T(8,128)(2,1)S(1)}, u32[]{:S(2)}, u32[]{:S(2)}) async-start(bf16[4,256,640]{2,1,0:T(8,128)(2,1)} %get-tuple-element.46), calls=%async_computation.2 | async-start | bytes 2621440 | tf_op jit(solution)/shard_map/all_to_all | solution.py:478
  74.2 14.1 %copy-start.1 = (bf16[8,128,512]{2,1,0:T(8,128)(2,1)S(1)}, bf16[8,128,512]{2,1,0:T(8,128)(2,1)}, u32[]{:S(2)}) copy-start(bf16[8,128,512]{2,1,0:T(8,128)(2,1)} %get-tuple-element.48.weight_ref) | copy-start | bytes 3145732
  74.2 4.1 %collective-permute-start.6 = (bf16[512,512]{1,0:T(8,128)(2,1)}, bf16[512,512]{1,0:T(8,128)(2,1)S(1)}, u32[]{:S(2)}, u32[]{:S(2)}) collective-permute-start(bf16[512,512]{1,0:T(8,128)(2,1)} %get-tuple-element.52), channel_id=1, source_target_pairs={{0,8},{8,0},{1,9},{9,1},{2,10},{10,2},{3,11},{11,3},{4,12},{12,4},... | collective-permute-start | bytes 1572872 | tf_op jit(solution)/shard_map/ppermute | solution.py:456
  78.5 12.1 %collective-permute-start.7 = (bf16[128,512]{1,0:T(8,128)(2,1)S(1)}, bf16[128,512]{1,0:T(8,128)(2,1)S(1)}, u32[]{:S(2)}, u32[]{:S(2)}) collective-permute-start(bf16[128,512]{1,0:T(8,128)(2,1)S(1)} %get-tuple-element.53), channel_id=1, source_target_pairs={{0,32},{16,48},{32,0},{48,16},{1,33},{17,49},{33,1},{49,17},{2,34}... | collective-permute-start | bytes 393224 | tf_op jit(solution)/shard_map/ppermute | solution.py:456
  81.8 8.8 %collective-permute-start.8 = (bf16[128,512]{1,0:T(8,128)(2,1)S(1)}, bf16[128,512]{1,0:T(8,128)(2,1)S(1)}, u32[]{:S(2)}, u32[]{:S(2)}) collective-permute-start(bf16[128,512]{1,0:T(8,128)(2,1)S(1)} %get-tuple-element.54), channel_id=1, source_target_pairs={{0,16},{16,0},{32,48},{48,32},{1,17},{17,1},{33,49},{49,33},{2,18}... | collective-permute-start | bytes 393224 | tf_op jit(solution)/shard_map/ppermute | solution.py:456
  84.2 8.1 %collective-permute-start.9 = (bf16[128,512]{1,0:T(8,128)(2,1)S(1)}, bf16[128,512]{1,0:T(8,128)(2,1)S(1)}, u32[]{:S(2)}, u32[]{:S(2)}) collective-permute-start(bf16[128,512]{1,0:T(8,128)(2,1)S(1)} %get-tuple-element.55), channel_id=1, source_target_pairs={{0,48},{16,32},{32,16},{48,0},{1,49},{17,33},{33,17},{49,1},{2,50}... | collective-permute-start | bytes 393224 | tf_op jit(solution)/shard_map/ppermute | solution.py:456
  110.5 13.5 %collective-permute-start.10 = (bf16[80,640]{1,0:T(8,128)(2,1)S(1)}, bf16[80,640]{1,0:T(8,128)(2,1)S(1)}, u32[]{:S(2)}, u32[]{:S(2)}) collective-permute-start(bf16[80,640]{1,0:T(8,128)(2,1)S(1)} %get-tuple-element.63.both_ref), channel_id=1, source_target_pairs={{0,256},{8,268},{64,320},{72,332},{128,384},{136,396},{192,448},{2... | collective-permute-start | bytes 307208 | tf_op jit(solution)/shard_map/ppermute | solution.py:469
  124.0 10.0 %collective-permute-start.11 = (bf16[48,640]{1,0:T(8,128)(2,1)S(1)}, bf16[48,640]{1,0:T(8,128)(2,1)S(1)}, u32[]{:S(2)}, u32[]{:S(2)}) collective-permute-start(bf16[48,640]{1,0:T(8,128)(2,1)S(1)} %get-tuple-element.65), channel_id=1, source_target_pairs={{0,260},{8,264},{64,324},{72,328},{128,388},{136,392},{192,452},{2... | collective-permute-start | bytes 184328 | tf_op jit(solution)/shard_map/ppermute | solution.py:469

commit v5 on v4

--- a/solution.py
+++ b/solution.py
@@ -126,20 +126,20 @@
     for i in range(WROWS):
         scale = jnp.where(row == i, scale_ref[i // HEADS, i % HEADS], scale)
     weight = (scale * levels.astype(f32) / 3.0).astype(bf16)
-    lane = iota((WROWS, 128), 1)
+    for r in range(RANKS):
+        weight_out[r] = weight
+    widen = chosen(iota((DR, 128), 0) == iota((DR, 128), 1))
+    lane = iota((TOK, 128), 1)
     run = [(pos_ref[half * HALF] >> 6).astype(f32) for half in range(2)]
-    rest = jnp.where(lane == 0, run[0], jnp.where(lane == 1, run[1], 0.0)).astype(bf16)
-    for r in range(RANKS):
-        weight_out[r, :, 0:DC] = weight
-        weight_out[r, :, DC:WIDE] = rest
-    widen = chosen(iota((DR, 128), 0) == iota((DR, 128), 1))
-    pack_out[:, DC:WIDE] = tn(rot_ref[...], widen).astype(bf16)
+    rest = tn(rot_ref[...], widen)
+    rest = jnp.where(lane == DR, run[0], jnp.where(lane == DR + 1, run[1], rest))
+    pack_out[:, DC:WIDE] = rest.astype(bf16)
 
 
 def order_weight_kernel(in_ref, out_ref):
     out, inp = iota((128, 128), 0), iota((128, 128), 1)
     head, rank, n = out // 16, (out % 16) // 2, out % 2
-    out_ref[...] = nn(chosen(inp == rank * 16 + n * 8 + head), in_ref[:, 0:DC]).astype(bf16)
+    out_ref[...] = nn(chosen(inp == rank * 16 + n * 8 + head), in_ref[...]).astype(bf16)
 
 
 def join_kernel(*refs):
@@ -184,7 +184,8 @@
 
 
 def attention_kernel(
-    runs_ref,
+    runs_in,
+    pos_ref,
     pack_any,
     lat_any,
     own_any,
@@ -217,8 +218,21 @@
     key_sems,
     weight_sems,
     out_sems,
+    runs_ref,
 ):
     zl, c = lax.axis_index("zl"), lax.axis_index("c")
+
+    blocks = []
+    for y in range(4):
+        for slot in range(2):
+            steps = [FETCH[core][y][slot] for core in range(2)]
+            if steps[0] is not None:
+                rank = (zl + RANKS + jnp.where(c == 0, steps[0], steps[1])) % RANKS
+                blocks.append((y, slot, rank))
+    for half in range(2):
+        runs_ref[zl * 2 + half] = pos_ref[half * HALF] >> 6
+        for y, slot, rank in blocks:
+            runs_ref[rank * 2 + half] = runs_in[(y * 2 + slot) * 2 + half]
 
     def place_of(run, start, size):
         return pl.ds(pl.multiple_of(run * HALF + start, size), size)
@@ -246,16 +260,11 @@
     for half in range(2):
         at = place_of(runs_ref[zl * 2 + half], 0, HALF)
         pairs.append((pack_any.at[pl.ds(half * HALF, HALF), :], keys.at[at, :]))
-    for y in range(4):
-        for slot in range(2):
-            steps = [FETCH[core][y][slot] for core in range(2)]
-            if steps[0] is None:
-                continue
-            rank = (zl + RANKS + jnp.where(c == 0, steps[0], steps[1])) % RANKS
-            for half in range(2):
-                at = place_of(runs_ref[rank * 2 + half], 0, HALF)
-                rows = pl.ds(slot * TOK + half * HALF, HALF)
-                pairs.append((lat_any.at[y, rows, :], keys.at[at, :]))
+    for y, slot, rank in blocks:
+        for half in range(2):
+            at = place_of(runs_ref[rank * 2 + half], 0, HALF)
+            rows = pl.ds(slot * TOK + half * HALF, HALF)
+            pairs.append((lat_any.at[y, rows, :], keys.at[at, :]))
     key_copies = started(pairs, key_sems)
     up_copies = started(((up_any, up_in),), query_sems, 2)
     dkey[...] = jnp.zeros_like(dkey)
@@ -481,7 +490,7 @@
 def shards(nope, rotary, latent, keys, upstream, codes, scale, positions):
     weight_send, pack = call(
         prepare_kernel,
-        (shape(RANKS, WROWS, WIDE), shape(TOK, WIDE)),
+        (shape(RANKS, WROWS, DC), shape(TOK, WIDE)),
         (latent, keys.T, codes.reshape(WROWS, DC), scale, positions),
         scratch=(
             pltpu.VMEM((DR, TOK), bf16),
@@ -497,19 +506,19 @@
     weight_ranks = everyone(weight_send, "zl")
     first, second = fetch(pack, 0), fetch(pack, 1)
     together = lax.optimization_barrier
-    weight_ranks, first, second = together((weight_ranks, first, second))
     (latent_spread,) = call(
         spread_latent_kernel, (shape(4, 2 * TOK, WIDE),), (first, second), name="spread_latent"
     )
+    weight_ranks, latent_spread = together((weight_ranks, latent_spread))
     latent_all = everyone(latent_spread, "y")
     (w_own,) = call(
-        order_weight_kernel, (shape(128, DC),), (weight_ranks.reshape(128, WIDE),), name="order_weight"
+        order_weight_kernel, (shape(128, DC),), (weight_ranks.reshape(128, DC),), name="order_weight"
     )
     far, left, right = [across(w_own, "x", step) for step in (2, 1, 3)]
     (w_own,) = call(join_kernel, (shape(512, DC),), (w_own, left, far, right), name="join")
     w_other = across(w_own, "c", 1)
     latent_all, w_own, w_other = together((latent_all, w_own, w_other))
-    runs = weight_ranks[:, 0, DC : DC + 2].astype(jnp.int32).reshape(16)
+    runs = latent_all.reshape(8, TOK, WIDE)[:, 0, DC + DR : DC + DR + 2].astype(jnp.int32).reshape(16)
     dkey, own, other, dq, weight = call(
         attention_kernel,
         (
@@ -521,6 +530,7 @@
         ),
         (
             runs,
+            positions,
             pack,
             latent_all,
             w_own.reshape(4, HEADS, 16, DC),
@@ -550,9 +560,10 @@
             pltpu.SemaphoreType.DMA((16,)),
             pltpu.SemaphoreType.DMA((8,)),
             pltpu.SemaphoreType.DMA((9,)),
+            pltpu.SMEM((16,), jnp.int32),
         ),
-        smem=(0,),
-        hbm=(1, 2, 3, 4, 5, 6, 7),
+        smem=(0, 1),
+        hbm=(2, 3, 4, 5, 6, 7, 8),
         out_any=True,
         flops=2 * 512 * 1280 * 2944,
         name="attention",

time: 148 us -> 147 us (level)
  starting transfers between devices: 67.8 us -> 66 us
    ppermute x2, starting transfers between devices: 10.7 us -> 8.55 us  [across_half(): return lax.ppermute(block, ('zl', 'c', 'zh'), pairs)]
    ppermute x2, waiting for transfers between devices: 12.8 us -> 14.6 us  [across_half(): return lax.ppermute(block, ('zl', 'c', 'zh'), pairs)]
  transfers between devices with their start and end apart: 15 -> 15, of which waited for: 12 -> 10; matrix products, arithmetic and copies ran while one was open for 0% -> 0% of each run, Pallas kernels for 2% -> 3%
where the time goes in v5:
time: 147 us; the launch traced here: 146 us
  starting transfers between devices  66 us (45%)
  waiting for transfers between devices  29.7 us (20%)
  blocking collectives  28.9 us (20%)
  Pallas kernels  19 us (13%)
    ppermute x8, starting transfers between devices, across(): return lax.ppermute(block, axis, [(i, i ^ step) for i in range(n)])  23.6 us
    all_to_all x3, starting transfers between devices, everyone(): return lax.all_to_all(blocks, axes, 0, 0, tiled=True)  23.1 us
    pallas_call x12, Pallas kernels, call(): pl.pallas_call(body, out_shape=outs, in_specs=specs, out_specs=[pl.BlockS...  19 us
    all_to_all x1, blocking collectives, quads(): lax.all_to_all(blocks, 'zl', 0, 0, tiled=True, axis_index_groups=groups)  18.4 us
    ppermute x2, waiting for transfers between devices, across_half(): return lax.ppermute(block, ('zl', 'c', 'zh'), pairs)  14.6 us
    ppermute x2, starting transfers between devices, fetch(): return lax.ppermute(block, axes, pairs)  10.7 us
    all_to_all x1, blocking collectives, everyone(): return lax.all_to_all(blocks, axes, 0, 0, tiled=True)  10.4 us
    ppermute x8, waiting for transfers between devices, across(): return lax.ppermute(block, axis, [(i, i ^ step) for i in range(n)])  9.59 us
  transfers between devices with their start and end apart: 15, of which 10 were waited for; matrix products, arithmetic and copies ran while one was open for 0% of the time, Pallas kernels for 3%

profile of v5, /device:TPU:6, one launch (start us, length us, event | category | flops | bytes accessed | tf_op | source)
XLA Modules:
  0.0 145.6 jit_solution(9418938093761533417)
XLA Ops:
  2.5 12.5 %all-to-all-start = ((bf16[8,16,512]{2,1,0:T(8,128)(2,1)}), bf16[8,16,512]{2,1,0:T(8,128)(2,1)S(1)}, u32[]{:S(2)}, u32[]{:S(2)}) async-start(bf16[8,16,512]{2,1,0:T(8,128)(2,1)} %get-tuple-element.37), calls=%async_computation | async-start | bytes 262144 | tf_op jit(solution)/shard_map/all_to_all | solution.py:487
  15.0 5.7 %collective-permute-start.1 = (bf16[128,640]{1,0:T(8,128)(2,1)}, bf16[128,640]{1,0:T(8,128)(2,1)S(1)}, u32[]{:S(2)}, u32[]{:S(2)}) collective-permute-start(bf16[128,640]{1,0:T(8,128)(2,1)} %get-tuple-element.38.pack_any), channel_id=1, source_target_pairs={{324,0},{193,1},{390,2},{200,8},{333,9},{398,10},{388,64},{257,65}... | collective-permute-start | bytes 491528 | tf_op jit(solution)/shard_map/ppermute | solution.py:460
  20.7 5.0 %collective-permute-start = (bf16[128,640]{1,0:T(8,128)(2,1)}, bf16[128,640]{1,0:T(8,128)(2,1)S(1)}, u32[]{:S(2)}, u32[]{:S(2)}) collective-permute-start(bf16[128,640]{1,0:T(8,128)(2,1)} %get-tuple-element.38.pack_any), channel_id=1, source_target_pairs={{64,0},{453,1},{130,2},{259,3},{460,8},{73,9},{138,10},{271,11},{1... | collective-permute-start | bytes 491528 | tf_op jit(solution)/shard_map/ppermute | solution.py:460
  25.7 3.7 %collective-permute-done.1.second = bf16[128,640]{1,0:T(8,128)(2,1)S(1)} collective-permute-done((bf16[128,640]{1,0:T(8,128)(2,1)}, bf16[128,640]{1,0:T(8,128)(2,1)S(1)}, u32[]{:S(2)}, u32[]{:S(2)}) %collective-permute-start.1) | collective-permute-done | bytes 163872 | tf_op jit(solution)/shard_map/ppermute | solution.py:460
  32.4 5.7 %all-to-all-start.1 = ((bf16[4,256,640]{2,1,0:T(8,128)(2,1)}), bf16[4,256,640]{2,1,0:T(8,128)(2,1)S(1)}, u32[]{:S(2)}, u32[]{:S(2)}) async-start(bf16[4,256,640]{2,1,0:T(8,128)(2,1)} %spread_latent.1), calls=%async_computation.1 | async-start | bytes 2621440 | tf_op jit(solution)/shard_map/all_to_all | solution.py:487
  38.3 2.4 %collective-permute-start.4 = (bf16[128,512]{1,0:T(8,128)(2,1)S(1)}, bf16[128,512]{1,0:T(8,128)(2,1)S(1)}, u32[]{:S(2)}, u32[]{:S(2)}) collective-permute-start(bf16[128,512]{1,0:T(8,128)(2,1)S(1)} %order_weight.1.refs_0_), channel_id=1, source_target_pairs={{0,48},{16,32},{32,16},{48,0},{1,49},{17,33},{33,17},{49,1},{2,50}... | collective-permute-start | bytes 393224 | tf_op jit(solution)/shard_map/ppermute | solution.py:465
  40.7 4.3 %collective-permute-start.3 = (bf16[128,512]{1,0:T(8,128)(2,1)S(1)}, bf16[128,512]{1,0:T(8,128)(2,1)S(1)}, u32[]{:S(2)}, u32[]{:S(2)}) collective-permute-start(bf16[128,512]{1,0:T(8,128)(2,1)S(1)} %order_weight.1.refs_0_), channel_id=1, source_target_pairs={{0,32},{16,48},{32,0},{48,16},{1,33},{17,49},{33,1},{49,17},{2,34}... | collective-permute-start | bytes 393224 | tf_op jit(solution)/shard_map/ppermute | solution.py:465
  45.0 3.1 %collective-permute-start.2 = (bf16[128,512]{1,0:T(8,128)(2,1)S(1)}, bf16[128,512]{1,0:T(8,128)(2,1)S(1)}, u32[]{:S(2)}, u32[]{:S(2)}) collective-permute-start(bf16[128,512]{1,0:T(8,128)(2,1)S(1)} %order_weight.1.refs_0_), channel_id=1, source_target_pairs={{0,16},{16,0},{32,48},{48,32},{1,17},{17,1},{33,49},{49,33},{2,18}... | collective-permute-start | bytes 393224 | tf_op jit(solution)/shard_map/ppermute | solution.py:465
  49.8 2.1 %collective-permute-done.2.refs_1_ = bf16[128,512]{1,0:T(8,128)(2,1)S(1)} collective-permute-done((bf16[128,512]{1,0:T(8,128)(2,1)S(1)}, bf16[128,512]{1,0:T(8,128)(2,1)S(1)}, u32[]{:S(2)}, u32[]{:S(2)}) %collective-permute-start.2) | collective-permute-done | bytes 131104 | tf_op jit(solution)/shard_map/ppermute | solution.py:465
  52.0 1.9 %collective-permute-start.5 = (bf16[512,512]{1,0:T(8,128)(2,1)S(1)}, bf16[512,512]{1,0:T(8,128)(2,1)S(1)}, u32[]{:S(2)}, u32[]{:S(2)}) collective-permute-start(bf16[512,512]{1,0:T(8,128)(2,1)S(1)} %join.1), channel_id=1, source_target_pairs={{0,8},{8,0},{1,9},{9,1},{2,10},{10,2},{3,11},{11,3},{4,12},{12,4},... | collective-permute-start | bytes 1572872 | tf_op jit(solution)/shard_map/ppermute | solution.py:465
  57.1 11.5 %attention.1 = (bf16[4,256,640]{2,1,0:T(8,128)(2,1)}, bf16[512,512]{1,0:T(8,128)(2,1)}, bf16[512,512]{1,0:T(8,128)(2,1)}, bf16[1024,640]{1,0:T(8,128)(2,1)}, bf16[8,128,512]{2,1,0:T(8,128)(2,1)}) custom-call(s32[16]{0:T(128)} %reshape.50.runs_in, s32[128]{0:T(128)} %pos_ref.1, bf16[128,640]{1,0:T(8,128)(2,1)} %get-tuple-element.38.pack_any, ...), custom_call_target="tpu_custom_call" | custom-call | flops 3858759680 | bytes 8684096 | tf_op jit(solution)/shard_map/attention/pallas_call | solution.py:80
  68.6 4.9 %all-to-all-start.2 = ((bf16[4,256,640]{2,1,0:T(8,128)(2,1)}), bf16[4,256,640]{2,1,0:T(8,128)(2,1)S(1)}, u32[]{:S(2)}, u32[]{:S(2)}) async-start(bf16[4,256,640]{2,1,0:T(8,128)(2,1)} %get-tuple-element.44), calls=%async_computation.2 | async-start | bytes 2621440 | tf_op jit(solution)/shard_map/all_to_all | solution.py:487
  73.5 2.0 %collective-permute-start.6 = (bf16[512,512]{1,0:T(8,128)(2,1)}, bf16[512,512]{1,0:T(8,128)(2,1)S(1)}, u32[]{:S(2)}, u32[]{:S(2)}) collective-permute-start(bf16[512,512]{1,0:T(8,128)(2,1)} %get-tuple-element.50), channel_id=1, source_target_pairs={{0,8},{8,0},{1,9},{9,1},{2,10},{10,2},{3,11},{11,3},{4,12},{12,4},... | collective-permute-start | bytes 1572872 | tf_op jit(solution)/shard_map/ppermute | solution.py:465
  75.6 2.1 %collective-permute-done.6.got_ref = bf16[512,512]{1,0:T(8,128)(2,1)S(1)} collective-permute-done((bf16[512,512]{1,0:T(8,128)(2,1)}, bf16[512,512]{1,0:T(8,128)(2,1)S(1)}, u32[]{:S(2)}, u32[]{:S(2)}) %collective-permute-start.6) | collective-permute-done | bytes 524320 | tf_op jit(solution)/shard_map/ppermute | solution.py:465
  77.8 3.0 %collective-permute-start.7 = (bf16[128,512]{1,0:T(8,128)(2,1)S(1)}, bf16[128,512]{1,0:T(8,128)(2,1)S(1)}, u32[]{:S(2)}, u32[]{:S(2)}) collective-permute-start(bf16[128,512]{1,0:T(8,128)(2,1)S(1)} %get-tuple-element.51), channel_id=1, source_target_pairs={{0,32},{16,48},{32,0},{48,16},{1,33},{17,49},{33,1},{49,17},{2,34}... | collective-permute-start | bytes 393224 | tf_op jit(solution)/shard_map/ppermute | solution.py:465
  80.8 2.8 %collective-permute-start.8 = (bf16[128,512]{1,0:T(8,128)(2,1)S(1)}, bf16[128,512]{1,0:T(8,128)(2,1)S(1)}, u32[]{:S(2)}, u32[]{:S(2)}) collective-permute-start(bf16[128,512]{1,0:T(8,128)(2,1)S(1)} %get-tuple-element.52), channel_id=1, source_target_pairs={{0,16},{16,0},{32,48},{48,32},{1,17},{17,1},{33,49},{49,33},{2,18}... | collective-permute-start | bytes 393224 | tf_op jit(solution)/shard_map/ppermute | solution.py:465
  83.6 4.0 %collective-permute-start.9 = (bf16[128,512]{1,0:T(8,128)(2,1)S(1)}, bf16[128,512]{1,0:T(8,128)(2,1)S(1)}, u32[]{:S(2)}, u32[]{:S(2)}) collective-permute-start(bf16[128,512]{1,0:T(8,128)(2,1)S(1)} %get-tuple-element.53), channel_id=1, source_target_pairs={{0,48},{16,32},{32,16},{48,0},{1,49},{17,33},{33,17},{49,1},{2,50}... | collective-permute-start | bytes 393224 | tf_op jit(solution)/shard_map/ppermute | solution.py:465
  87.6 2.2 %query_grads.1 = (bf16[1024,128]{1,0:T(8,128)(2,1)}, bf16[128,512]{1,0:T(8,128)(2,1)}) custom-call(bf16[1024,640]{1,0:T(8,128)(2,1)S(1)} %copy-done, bf16[8,128,512]{2,1,0:T(8,128)(2,1)S(1)} %copy-done.1), custom_call_target="tpu_custom_call" | custom-call | flops 201326592 | bytes 2752512 | tf_op jit(solution)/shard_map/query_grads/pallas_call | solution.py:80
  92.1 18.4 %all_to_all.25.in_ref = bf16[4,96,640]{2,1,0:T(8,128)(2,1)S(1)} all-to-all(bf16[4,96,640]{2,1,0:T(8,128)(2,1)S(1)} %plane.1), channel_id=1, replica_groups={{0,64,128,192},{256,320,384,448},{1,65,129,193},{257,321,385,449},{2,66..., dimensions={0} | all-to-all | bytes 983040 | tf_op jit(solution)/shard_map/all_to_all | solution.py:483
  110.6 4.7 %collective-permute-start.10 = (bf16[80,640]{1,0:T(8,128)(2,1)S(1)}, bf16[80,640]{1,0:T(8,128)(2,1)S(1)}, u32[]{:S(2)}, u32[]{:S(2)}) collective-permute-start(bf16[80,640]{1,0:T(8,128)(2,1)S(1)} %get-tuple-element.61.both_ref), channel_id=1, source_target_pairs={{0,256},{8,268},{64,320},{72,332},{128,384},{136,396},{192,448},{2... | collective-permute-start | bytes 307208 | tf_op jit(solution)/shard_map/ppermute | solution.py:478
  115.3 8.3 %collective-permute-done.10.got_ref.first_ref = bf16[80,640]{1,0:T(8,128)(2,1)S(1)} collective-permute-done((bf16[80,640]{1,0:T(8,128)(2,1)S(1)}, bf16[80,640]{1,0:T(8,128)(2,1)S(1)}, u32[]{:S(2)}, u32[]{:S(2)}) %collective-permute-start.10) | collective-permute-done | bytes 102432 | tf_op jit(solution)/shard_map/ppermute | solution.py:478
  123.7 3.8 %collective-permute-start.11 = (bf16[48,640]{1,0:T(8,128)(2,1)S(1)}, bf16[48,640]{1,0:T(8,128)(2,1)S(1)}, u32[]{:S(2)}, u32[]{:S(2)}) collective-permute-start(bf16[48,640]{1,0:T(8,128)(2,1)S(1)} %get-tuple-element.63), channel_id=1, source_target_pairs={{0,260},{8,264},{64,324},{72,328},{128,388},{136,392},{192,452},{2... | collective-permute-start | bytes 184328 | tf_op jit(solution)/shard_map/ppermute | solution.py:478
  127.5 6.3 %collective-permute-done.11.got_ref = bf16[48,640]{1,0:T(8,128)(2,1)S(1)} collective-permute-done((bf16[48,640]{1,0:T(8,128)(2,1)S(1)}, bf16[48,640]{1,0:T(8,128)(2,1)S(1)}, u32[]{:S(2)}, u32[]{:S(2)}) %collective-permute-start.11) | collective-permute-done | bytes 61472 | tf_op jit(solution)/shard_map/ppermute | solution.py:478
  134.4 10.4 %all_to_all.26.in_ref = bf16[4,32,640]{2,1,0:T(8,128)(2,1)S(1)} all-to-all(bf16[4,32,640]{2,1,0:T(8,128)(2,1)S(1)} %get-tuple-element.65), channel_id=1, replica_groups=mesh['zl'=8,'x'=4,'c'=2,'zh'=2,'y'=4] {'y'}, dimensions={0} | all-to-all | bytes 327680 | tf_op jit(solution)/shard_map/all_to_all | solution.py:487
  (35 shorter events, 13.6 us)
Async XLA Ops:
  2.5 29.9 %all-to-all-start = ((bf16[8,16,512]{2,1,0:T(8,128)(2,1)}), bf16[8,16,512]{2,1,0:T(8,128)(2,1)S(1)}, u32[]{:S(2)}, u32[]{:S(2)}) async-start(bf16[8,16,512]{2,1,0:T(8,128)(2,1)} %get-tuple-element.37), calls=%async_computation | async-start | bytes 262144 | tf_op jit(solution)/shard_map/all_to_all | solution.py:487
  15.0 14.4 %collective-permute-start.1 = (bf16[128,640]{1,0:T(8,128)(2,1)}, bf16[128,640]{1,0:T(8,128)(2,1)S(1)}, u32[]{:S(2)}, u32[]{:S(2)}) collective-permute-start(bf16[128,640]{1,0:T(8,128)(2,1)} %get-tuple-element.38.pack_any), channel_id=1, source_target_pairs={{324,0},{193,1},{390,2},{200,8},{333,9},{398,10},{388,64},{257,65}... | collective-permute-start | bytes 491528 | tf_op jit(solution)/shard_map/ppermute | solution.py:460
  20.7 10.5 %collective-permute-start = (bf16[128,640]{1,0:T(8,128)(2,1)}, bf16[128,640]{1,0:T(8,128)(2,1)S(1)}, u32[]{:S(2)}, u32[]{:S(2)}) collective-permute-start(bf16[128,640]{1,0:T(8,128)(2,1)} %get-tuple-element.38.pack_any), channel_id=1, source_target_pairs={{64,0},{453,1},{130,2},{259,3},{460,8},{73,9},{138,10},{271,11},{1... | collective-permute-start | bytes 491528 | tf_op jit(solution)/shard_map/ppermute | solution.py:460
  32.4 23.4 %all-to-all-start.1 = ((bf16[4,256,640]{2,1,0:T(8,128)(2,1)}), bf16[4,256,640]{2,1,0:T(8,128)(2,1)S(1)}, u32[]{:S(2)}, u32[]{:S(2)}) async-start(bf16[4,256,640]{2,1,0:T(8,128)(2,1)} %spread_latent.1), calls=%async_computation.1 | async-start | bytes 2621440 | tf_op jit(solution)/shard_map/all_to_all | solution.py:487
  38.3 10.2 %collective-permute-start.4 = (bf16[128,512]{1,0:T(8,128)(2,1)S(1)}, bf16[128,512]{1,0:T(8,128)(2,1)S(1)}, u32[]{:S(2)}, u32[]{:S(2)}) collective-permute-start(bf16[128,512]{1,0:T(8,128)(2,1)S(1)} %order_weight.1.refs_0_), channel_id=1, source_target_pairs={{0,48},{16,32},{32,16},{48,0},{1,49},{17,33},{33,17},{49,1},{2,50}... | collective-permute-start | bytes 393224 | tf_op jit(solution)/shard_map/ppermute | solution.py:465
  40.7 9.1 %collective-permute-start.3 = (bf16[128,512]{1,0:T(8,128)(2,1)S(1)}, bf16[128,512]{1,0:T(8,128)(2,1)S(1)}, u32[]{:S(2)}, u32[]{:S(2)}) collective-permute-start(bf16[128,512]{1,0:T(8,128)(2,1)S(1)} %order_weight.1.refs_0_), channel_id=1, source_target_pairs={{0,32},{16,48},{32,0},{48,16},{1,33},{17,49},{33,1},{49,17},{2,34}... | collective-permute-start | bytes 393224 | tf_op jit(solution)/shard_map/ppermute | solution.py:465
  45.0 6.9 %collective-permute-start.2 = (bf16[128,512]{1,0:T(8,128)(2,1)S(1)}, bf16[128,512]{1,0:T(8,128)(2,1)S(1)}, u32[]{:S(2)}, u32[]{:S(2)}) collective-permute-start(bf16[128,512]{1,0:T(8,128)(2,1)S(1)} %order_weight.1.refs_0_), channel_id=1, source_target_pairs={{0,16},{16,0},{32,48},{48,32},{1,17},{17,1},{33,49},{49,33},{2,18}... | collective-permute-start | bytes 393224 | tf_op jit(solution)/shard_map/ppermute | solution.py:465
  52.0 4.7 %copy-start.2 = (bf16[512,512]{1,0:T(8,128)(2,1)}, bf16[512,512]{1,0:T(8,128)(2,1)S(1)}, u32[]{:S(2)}) copy-start(bf16[512,512]{1,0:T(8,128)(2,1)S(1)} %join.1) | copy-start | bytes 1572868
  52.0 3.8 %collective-permute-start.5 = (bf16[512,512]{1,0:T(8,128)(2,1)S(1)}, bf16[512,512]{1,0:T(8,128)(2,1)S(1)}, u32[]{:S(2)}, u32[]{:S(2)}) collective-permute-start(bf16[512,512]{1,0:T(8,128)(2,1)S(1)} %join.1), channel_id=1, source_target_pairs={{0,8},{8,0},{1,9},{9,1},{2,10},{10,2},{3,11},{11,3},{4,12},{12,4},... | collective-permute-start | bytes 1572872 | tf_op jit(solution)/shard_map/ppermute | solution.py:465
  55.8 0.8 copy-start.5
  55.8 1.3 copy-start.4
  68.6 9.0 %copy-start.3 = (bf16[512,512]{1,0:T(8,128)(2,1)S(1)}, bf16[512,512]{1,0:T(8,128)(2,1)}, u32[]{:S(2)}) copy-start(bf16[512,512]{1,0:T(8,128)(2,1)} %get-tuple-element.49.own_ref) | copy-start | bytes 1572868
  68.6 19.0 %copy-start = (bf16[1024,640]{1,0:T(8,128)(2,1)S(1)}, bf16[1024,640]{1,0:T(8,128)(2,1)}, u32[]{:S(2)}) copy-start(bf16[1024,640]{1,0:T(8,128)(2,1)} %get-tuple-element.45.dq_ref) | copy-start | bytes 3932164
  68.6 23.1 %all-to-all-start.2 = ((bf16[4,256,640]{2,1,0:T(8,128)(2,1)}), bf16[4,256,640]{2,1,0:T(8,128)(2,1)S(1)}, u32[]{:S(2)}, u32[]{:S(2)}) async-start(bf16[4,256,640]{2,1,0:T(8,128)(2,1)} %get-tuple-element.44), calls=%async_computation.2 | async-start | bytes 2621440 | tf_op jit(solution)/shard_map/all_to_all | solution.py:487
  73.5 14.1 %copy-start.1 = (bf16[8,128,512]{2,1,0:T(8,128)(2,1)S(1)}, bf16[8,128,512]{2,1,0:T(8,128)(2,1)}, u32[]{:S(2)}) copy-start(bf16[8,128,512]{2,1,0:T(8,128)(2,1)} %get-tuple-element.46.weight_ref) | copy-start | bytes 3145732
  73.5 4.1 %collective-permute-start.6 = (bf16[512,512]{1,0:T(8,128)(2,1)}, bf16[512,512]{1,0:T(8,128)(2,1)S(1)}, u32[]{:S(2)}, u32[]{:S(2)}) collective-permute-start(bf16[512,512]{1,0:T(8,128)(2,1)} %get-tuple-element.50), channel_id=1, source_target_pairs={{0,8},{8,0},{1,9},{9,1},{2,10},{10,2},{3,11},{11,3},{4,12},{12,4},... | collective-permute-start | bytes 1572872 | tf_op jit(solution)/shard_map/ppermute | solution.py:465
  77.8 12.1 %collective-permute-start.7 = (bf16[128,512]{1,0:T(8,128)(2,1)S(1)}, bf16[128,512]{1,0:T(8,128)(2,1)S(1)}, u32[]{:S(2)}, u32[]{:S(2)}) collective-permute-start(bf16[128,512]{1,0:T(8,128)(2,1)S(1)} %get-tuple-element.51), channel_id=1, source_target_pairs={{0,32},{16,48},{32,0},{48,16},{1,33},{17,49},{33,1},{49,17},{2,34}... | collective-permute-start | bytes 393224 | tf_op jit(solution)/shard_map/ppermute | solution.py:465
  80.8 9.1 %collective-permute-start.8 = (bf16[128,512]{1,0:T(8,128)(2,1)S(1)}, bf16[128,512]{1,0:T(8,128)(2,1)S(1)}, u32[]{:S(2)}, u32[]{:S(2)}) collective-permute-start(bf16[128,512]{1,0:T(8,128)(2,1)S(1)} %get-tuple-element.52), channel_id=1, source_target_pairs={{0,16},{16,0},{32,48},{48,32},{1,17},{17,1},{33,49},{49,33},{2,18}... | collective-permute-start | bytes 393224 | tf_op jit(solution)/shard_map/ppermute | solution.py:465
  83.6 8.1 %collective-permute-start.9 = (bf16[128,512]{1,0:T(8,128)(2,1)S(1)}, bf16[128,512]{1,0:T(8,128)(2,1)S(1)}, u32[]{:S(2)}, u32[]{:S(2)}) collective-permute-start(bf16[128,512]{1,0:T(8,128)(2,1)S(1)} %get-tuple-element.53), channel_id=1, source_target_pairs={{0,48},{16,32},{32,16},{48,0},{1,49},{17,33},{33,17},{49,1},{2,50}... | collective-permute-start | bytes 393224 | tf_op jit(solution)/shard_map/ppermute | solution.py:465
  110.6 13.1 %collective-permute-start.10 = (bf16[80,640]{1,0:T(8,128)(2,1)S(1)}, bf16[80,640]{1,0:T(8,128)(2,1)S(1)}, u32[]{:S(2)}, u32[]{:S(2)}) collective-permute-start(bf16[80,640]{1,0:T(8,128)(2,1)S(1)} %get-tuple-element.61.both_ref), channel_id=1, source_target_pairs={{0,256},{8,268},{64,320},{72,332},{128,384},{136,396},{192,448},{2... | collective-permute-start | bytes 307208 | tf_op jit(solution)/shard_map/ppermute | solution.py:478
  123.7 10.1 %collective-permute-start.11 = (bf16[48,640]{1,0:T(8,128)(2,1)S(1)}, bf16[48,640]{1,0:T(8,128)(2,1)S(1)}, u32[]{:S(2)}, u32[]{:S(2)}) collective-permute-start(bf16[48,640]{1,0:T(8,128)(2,1)S(1)} %get-tuple-element.63), channel_id=1, source_target_pairs={{0,260},{8,264},{64,324},{72,328},{128,388},{136,392},{192,452},{2... | collective-permute-start | bytes 184328 | tf_op jit(solution)/shard_map/ppermute | solution.py:478

commit v6 on v5

--- a/solution.py
+++ b/solution.py
@@ -517,8 +517,8 @@
     far, left, right = [across(w_own, "x", step) for step in (2, 1, 3)]
     (w_own,) = call(join_kernel, (shape(512, DC),), (w_own, left, far, right), name="join")
     w_other = across(w_own, "c", 1)
-    latent_all, w_own, w_other = together((latent_all, w_own, w_other))
     runs = latent_all.reshape(8, TOK, WIDE)[:, 0, DC + DR : DC + DR + 2].astype(jnp.int32).reshape(16)
+    latent_all, w_own, w_other, runs = together((latent_all, w_own, w_other, runs))
     dkey, own, other, dq, weight = call(
         attention_kernel,
         (

time: 147 us -> 147 us (level)
    ppermute x8, waiting for transfers between devices: 9.59 us -> 7.71 us  [across(): return lax.ppermute(block, axis, [(i, i ^ step) for i in range(n)])]
  transfers between devices with their start and end apart: 15 -> 15, of which waited for: 10 -> 10; matrix products, arithmetic and copies ran while one was open for 0% -> 1% of each run, Pallas kernels for 3% -> 3%
where the time goes in v6:
time: 147 us; the launch traced here: 145 us
  starting transfers between devices  65.7 us (45%)
  waiting for transfers between devices  29.1 us (20%)
  blocking collectives  28.9 us (20%)
  Pallas kernels  19 us (13%)
  local copies, waits for them, and re-layouts  1.63 us (1%)
    ppermute x8, starting transfers between devices, across(): return lax.ppermute(block, axis, [(i, i ^ step) for i in range(n)])  23.6 us
    all_to_all x3, starting transfers between devices, everyone(): return lax.all_to_all(blocks, axes, 0, 0, tiled=True)  22.9 us
    pallas_call x12, Pallas kernels, call(): pl.pallas_call(body, out_shape=outs, in_specs=specs, out_specs=[pl.BlockS...  19 us
    all_to_all x1, blocking collectives, quads(): lax.all_to_all(blocks, 'zl', 0, 0, tiled=True, axis_index_groups=groups)  18.5 us
    ppermute x2, waiting for transfers between devices, across_half(): return lax.ppermute(block, ('zl', 'c', 'zh'), pairs)  14.6 us
    ppermute x2, starting transfers between devices, fetch(): return lax.ppermute(block, axes, pairs)  10.7 us
    all_to_all x1, blocking collectives, everyone(): return lax.all_to_all(blocks, axes, 0, 0, tiled=True)  10.5 us
    ppermute x2, starting transfers between devices, across_half(): return lax.ppermute(block, ('zl', 'c', 'zh'), pairs)  8.52 us
  transfers between devices with their start and end apart: 15, of which 10 were waited for; matrix products, arithmetic and copies ran while one was open for 1% of the time, Pallas kernels for 3%

profile of v6, /device:TPU:6, one launch (start us, length us, event | category | flops | bytes accessed | tf_op | source)
XLA Modules:
  0.0 145.1 jit_solution(6716888447690181270)
XLA Ops:
  2.5 12.5 %all-to-all-start = ((bf16[8,16,512]{2,1,0:T(8,128)(2,1)}), bf16[8,16,512]{2,1,0:T(8,128)(2,1)S(1)}, u32[]{:S(2)}, u32[]{:S(2)}) async-start(bf16[8,16,512]{2,1,0:T(8,128)(2,1)} %get-tuple-element.38), calls=%async_computation | async-start | bytes 262144 | tf_op jit(solution)/shard_map/all_to_all | solution.py:487
  15.0 5.7 %collective-permute-start.1 = (bf16[128,640]{1,0:T(8,128)(2,1)}, bf16[128,640]{1,0:T(8,128)(2,1)S(1)}, u32[]{:S(2)}, u32[]{:S(2)}) collective-permute-start(bf16[128,640]{1,0:T(8,128)(2,1)} %get-tuple-element.39.pack_any), channel_id=1, source_target_pairs={{324,0},{193,1},{390,2},{200,8},{333,9},{398,10},{388,64},{257,65}... | collective-permute-start | bytes 491528 | tf_op jit(solution)/shard_map/ppermute | solution.py:460
  20.7 5.0 %collective-permute-start = (bf16[128,640]{1,0:T(8,128)(2,1)}, bf16[128,640]{1,0:T(8,128)(2,1)S(1)}, u32[]{:S(2)}, u32[]{:S(2)}) collective-permute-start(bf16[128,640]{1,0:T(8,128)(2,1)} %get-tuple-element.39.pack_any), channel_id=1, source_target_pairs={{64,0},{453,1},{130,2},{259,3},{460,8},{73,9},{138,10},{271,11},{1... | collective-permute-start | bytes 491528 | tf_op jit(solution)/shard_map/ppermute | solution.py:460
  25.7 3.7 %collective-permute-done.1.second = bf16[128,640]{1,0:T(8,128)(2,1)S(1)} collective-permute-done((bf16[128,640]{1,0:T(8,128)(2,1)}, bf16[128,640]{1,0:T(8,128)(2,1)S(1)}, u32[]{:S(2)}, u32[]{:S(2)}) %collective-permute-start.1) | collective-permute-done | bytes 163872 | tf_op jit(solution)/shard_map/ppermute | solution.py:460
  32.4 5.7 %all-to-all-start.1 = ((bf16[4,256,640]{2,1,0:T(8,128)(2,1)}), bf16[4,256,640]{2,1,0:T(8,128)(2,1)S(1)}, u32[]{:S(2)}, u32[]{:S(2)}) async-start(bf16[4,256,640]{2,1,0:T(8,128)(2,1)} %spread_latent.1), calls=%async_computation.1 | async-start | bytes 2621440 | tf_op jit(solution)/shard_map/all_to_all | solution.py:487
  38.3 2.4 %collective-permute-start.4 = (bf16[128,512]{1,0:T(8,128)(2,1)S(1)}, bf16[128,512]{1,0:T(8,128)(2,1)S(1)}, u32[]{:S(2)}, u32[]{:S(2)}) collective-permute-start(bf16[128,512]{1,0:T(8,128)(2,1)S(1)} %order_weight.1.refs_0_), channel_id=1, source_target_pairs={{0,48},{16,32},{32,16},{48,0},{1,49},{17,33},{33,17},{49,1},{2,50}... | collective-permute-start | bytes 393224 | tf_op jit(solution)/shard_map/ppermute | solution.py:465
  40.7 4.3 %collective-permute-start.3 = (bf16[128,512]{1,0:T(8,128)(2,1)S(1)}, bf16[128,512]{1,0:T(8,128)(2,1)S(1)}, u32[]{:S(2)}, u32[]{:S(2)}) collective-permute-start(bf16[128,512]{1,0:T(8,128)(2,1)S(1)} %order_weight.1.refs_0_), channel_id=1, source_target_pairs={{0,32},{16,48},{32,0},{48,16},{1,33},{17,49},{33,1},{49,17},{2,34}... | collective-permute-start | bytes 393224 | tf_op jit(solution)/shard_map/ppermute | solution.py:465
  45.0 3.1 %collective-permute-start.2 = (bf16[128,512]{1,0:T(8,128)(2,1)S(1)}, bf16[128,512]{1,0:T(8,128)(2,1)S(1)}, u32[]{:S(2)}, u32[]{:S(2)}) collective-permute-start(bf16[128,512]{1,0:T(8,128)(2,1)S(1)} %order_weight.1.refs_0_), channel_id=1, source_target_pairs={{0,16},{16,0},{32,48},{48,32},{1,17},{17,1},{33,49},{49,33},{2,18}... | collective-permute-start | bytes 393224 | tf_op jit(solution)/shard_map/ppermute | solution.py:465
  49.8 2.1 %collective-permute-done.2.refs_1_ = bf16[128,512]{1,0:T(8,128)(2,1)S(1)} collective-permute-done((bf16[128,512]{1,0:T(8,128)(2,1)S(1)}, bf16[128,512]{1,0:T(8,128)(2,1)S(1)}, u32[]{:S(2)}, u32[]{:S(2)}) %collective-permute-start.2) | collective-permute-done | bytes 131104 | tf_op jit(solution)/shard_map/ppermute | solution.py:465
  52.0 1.9 %collective-permute-start.5 = (bf16[512,512]{1,0:T(8,128)(2,1)S(1)}, bf16[512,512]{1,0:T(8,128)(2,1)S(1)}, u32[]{:S(2)}, u32[]{:S(2)}) collective-permute-start(bf16[512,512]{1,0:T(8,128)(2,1)S(1)} %join.1), channel_id=1, source_target_pairs={{0,8},{8,0},{1,9},{9,1},{2,10},{10,2},{3,11},{11,3},{4,12},{12,4},... | collective-permute-start | bytes 1572872 | tf_op jit(solution)/shard_map/ppermute | solution.py:465
  56.9 11.6 %attention.1 = (bf16[4,256,640]{2,1,0:T(8,128)(2,1)}, bf16[512,512]{1,0:T(8,128)(2,1)}, bf16[512,512]{1,0:T(8,128)(2,1)}, bf16[1024,640]{1,0:T(8,128)(2,1)}, bf16[8,128,512]{2,1,0:T(8,128)(2,1)}) custom-call(s32[16]{0:T(128)} %reshape.50.runs_in, s32[128]{0:T(128)} %pos_ref.1, bf16[128,640]{1,0:T(8,128)(2,1)} %get-tuple-element.39.pack_any, ...), custom_call_target="tpu_custom_call" | custom-call | flops 3858759680 | bytes 8684096 | tf_op jit(solution)/shard_map/attention/pallas_call | solution.py:80
  68.4 4.6 %all-to-all-start.2 = ((bf16[4,256,640]{2,1,0:T(8,128)(2,1)}), bf16[4,256,640]{2,1,0:T(8,128)(2,1)S(1)}, u32[]{:S(2)}, u32[]{:S(2)}) async-start(bf16[4,256,640]{2,1,0:T(8,128)(2,1)} %get-tuple-element.46), calls=%async_computation.2 | async-start | bytes 2621440 | tf_op jit(solution)/shard_map/all_to_all | solution.py:487
  73.0 2.0 %collective-permute-start.6 = (bf16[512,512]{1,0:T(8,128)(2,1)}, bf16[512,512]{1,0:T(8,128)(2,1)S(1)}, u32[]{:S(2)}, u32[]{:S(2)}) collective-permute-start(bf16[512,512]{1,0:T(8,128)(2,1)} %get-tuple-element.52), channel_id=1, source_target_pairs={{0,8},{8,0},{1,9},{9,1},{2,10},{10,2},{3,11},{11,3},{4,12},{12,4},... | collective-permute-start | bytes 1572872 | tf_op jit(solution)/shard_map/ppermute | solution.py:465
  75.1 2.1 %collective-permute-done.6.got_ref = bf16[512,512]{1,0:T(8,128)(2,1)S(1)} collective-permute-done((bf16[512,512]{1,0:T(8,128)(2,1)}, bf16[512,512]{1,0:T(8,128)(2,1)S(1)}, u32[]{:S(2)}, u32[]{:S(2)}) %collective-permute-start.6) | collective-permute-done | bytes 524320 | tf_op jit(solution)/shard_map/ppermute | solution.py:465
  77.3 3.0 %collective-permute-start.7 = (bf16[128,512]{1,0:T(8,128)(2,1)S(1)}, bf16[128,512]{1,0:T(8,128)(2,1)S(1)}, u32[]{:S(2)}, u32[]{:S(2)}) collective-permute-start(bf16[128,512]{1,0:T(8,128)(2,1)S(1)} %get-tuple-element.53), channel_id=1, source_target_pairs={{0,32},{16,48},{32,0},{48,16},{1,33},{17,49},{33,1},{49,17},{2,34}... | collective-permute-start | bytes 393224 | tf_op jit(solution)/shard_map/ppermute | solution.py:465
  80.3 2.8 %collective-permute-start.8 = (bf16[128,512]{1,0:T(8,128)(2,1)S(1)}, bf16[128,512]{1,0:T(8,128)(2,1)S(1)}, u32[]{:S(2)}, u32[]{:S(2)}) collective-permute-start(bf16[128,512]{1,0:T(8,128)(2,1)S(1)} %get-tuple-element.54), channel_id=1, source_target_pairs={{0,16},{16,0},{32,48},{48,32},{1,17},{17,1},{33,49},{49,33},{2,18}... | collective-permute-start | bytes 393224 | tf_op jit(solution)/shard_map/ppermute | solution.py:465
  83.1 4.0 %collective-permute-start.9 = (bf16[128,512]{1,0:T(8,128)(2,1)S(1)}, bf16[128,512]{1,0:T(8,128)(2,1)S(1)}, u32[]{:S(2)}, u32[]{:S(2)}) collective-permute-start(bf16[128,512]{1,0:T(8,128)(2,1)S(1)} %get-tuple-element.55), channel_id=1, source_target_pairs={{0,48},{16,32},{32,16},{48,0},{1,49},{17,33},{33,17},{49,1},{2,50}... | collective-permute-start | bytes 393224 | tf_op jit(solution)/shard_map/ppermute | solution.py:465
  87.2 2.2 %query_grads.1 = (bf16[1024,128]{1,0:T(8,128)(2,1)}, bf16[128,512]{1,0:T(8,128)(2,1)}) custom-call(bf16[1024,640]{1,0:T(8,128)(2,1)S(1)} %copy-done, bf16[8,128,512]{2,1,0:T(8,128)(2,1)S(1)} %copy-done.1), custom_call_target="tpu_custom_call" | custom-call | flops 201326592 | bytes 2752512 | tf_op jit(solution)/shard_map/query_grads/pallas_call | solution.py:80
  91.6 18.5 %all_to_all.25.in_ref = bf16[4,96,640]{2,1,0:T(8,128)(2,1)S(1)} all-to-all(bf16[4,96,640]{2,1,0:T(8,128)(2,1)S(1)} %plane.1), channel_id=1, replica_groups={{0,64,128,192},{256,320,384,448},{1,65,129,193},{257,321,385,449},{2,66..., dimensions={0} | all-to-all | bytes 983040 | tf_op jit(solution)/shard_map/all_to_all | solution.py:483
  110.2 4.7 %collective-permute-start.10 = (bf16[80,640]{1,0:T(8,128)(2,1)S(1)}, bf16[80,640]{1,0:T(8,128)(2,1)S(1)}, u32[]{:S(2)}, u32[]{:S(2)}) collective-permute-start(bf16[80,640]{1,0:T(8,128)(2,1)S(1)} %get-tuple-element.63.both_ref), channel_id=1, source_target_pairs={{0,256},{8,268},{64,320},{72,332},{128,384},{136,396},{192,448},{2... | collective-permute-start | bytes 307208 | tf_op jit(solution)/shard_map/ppermute | solution.py:478
  114.8 8.3 %collective-permute-done.10.got_ref.first_ref = bf16[80,640]{1,0:T(8,128)(2,1)S(1)} collective-permute-done((bf16[80,640]{1,0:T(8,128)(2,1)S(1)}, bf16[80,640]{1,0:T(8,128)(2,1)S(1)}, u32[]{:S(2)}, u32[]{:S(2)}) %collective-permute-start.10) | collective-permute-done | bytes 102432 | tf_op jit(solution)/shard_map/ppermute | solution.py:478
  123.2 3.9 %collective-permute-start.11 = (bf16[48,640]{1,0:T(8,128)(2,1)S(1)}, bf16[48,640]{1,0:T(8,128)(2,1)S(1)}, u32[]{:S(2)}, u32[]{:S(2)}) collective-permute-start(bf16[48,640]{1,0:T(8,128)(2,1)S(1)} %get-tuple-element.65), channel_id=1, source_target_pairs={{0,260},{8,264},{64,324},{72,328},{128,388},{136,392},{192,452},{2... | collective-permute-start | bytes 184328 | tf_op jit(solution)/shard_map/ppermute | solution.py:478
  127.0 6.2 %collective-permute-done.11.got_ref = bf16[48,640]{1,0:T(8,128)(2,1)S(1)} collective-permute-done((bf16[48,640]{1,0:T(8,128)(2,1)S(1)}, bf16[48,640]{1,0:T(8,128)(2,1)S(1)}, u32[]{:S(2)}, u32[]{:S(2)}) %collective-permute-start.11) | collective-permute-done | bytes 61472 | tf_op jit(solution)/shard_map/ppermute | solution.py:478
  133.9 10.5 %all_to_all.26.in_ref = bf16[4,32,640]{2,1,0:T(8,128)(2,1)S(1)} all-to-all(bf16[4,32,640]{2,1,0:T(8,128)(2,1)S(1)} %get-tuple-element.67), channel_id=1, replica_groups=mesh['zl'=8,'x'=4,'c'=2,'zh'=2,'y'=4] {'y'}, dimensions={0} | all-to-all | bytes 327680 | tf_op jit(solution)/shard_map/all_to_all | solution.py:487
  (35 shorter events, 13.4 us)
Async XLA Ops:
  2.5 29.9 %all-to-all-start = ((bf16[8,16,512]{2,1,0:T(8,128)(2,1)}), bf16[8,16,512]{2,1,0:T(8,128)(2,1)S(1)}, u32[]{:S(2)}, u32[]{:S(2)}) async-start(bf16[8,16,512]{2,1,0:T(8,128)(2,1)} %get-tuple-element.38), calls=%async_computation | async-start | bytes 262144 | tf_op jit(solution)/shard_map/all_to_all | solution.py:487
  15.0 14.4 %collective-permute-start.1 = (bf16[128,640]{1,0:T(8,128)(2,1)}, bf16[128,640]{1,0:T(8,128)(2,1)S(1)}, u32[]{:S(2)}, u32[]{:S(2)}) collective-permute-start(bf16[128,640]{1,0:T(8,128)(2,1)} %get-tuple-element.39.pack_any), channel_id=1, source_target_pairs={{324,0},{193,1},{390,2},{200,8},{333,9},{398,10},{388,64},{257,65}... | collective-permute-start | bytes 491528 | tf_op jit(solution)/shard_map/ppermute | solution.py:460
  20.7 10.5 %collective-permute-start = (bf16[128,640]{1,0:T(8,128)(2,1)}, bf16[128,640]{1,0:T(8,128)(2,1)S(1)}, u32[]{:S(2)}, u32[]{:S(2)}) collective-permute-start(bf16[128,640]{1,0:T(8,128)(2,1)} %get-tuple-element.39.pack_any), channel_id=1, source_target_pairs={{64,0},{453,1},{130,2},{259,3},{460,8},{73,9},{138,10},{271,11},{1... | collective-permute-start | bytes 491528 | tf_op jit(solution)/shard_map/ppermute | solution.py:460
  32.4 22.8 %all-to-all-start.1 = ((bf16[4,256,640]{2,1,0:T(8,128)(2,1)}), bf16[4,256,640]{2,1,0:T(8,128)(2,1)S(1)}, u32[]{:S(2)}, u32[]{:S(2)}) async-start(bf16[4,256,640]{2,1,0:T(8,128)(2,1)} %spread_latent.1), calls=%async_computation.1 | async-start | bytes 2621440 | tf_op jit(solution)/shard_map/all_to_all | solution.py:487
  38.3 10.2 %collective-permute-start.4 = (bf16[128,512]{1,0:T(8,128)(2,1)S(1)}, bf16[128,512]{1,0:T(8,128)(2,1)S(1)}, u32[]{:S(2)}, u32[]{:S(2)}) collective-permute-start(bf16[128,512]{1,0:T(8,128)(2,1)S(1)} %order_weight.1.refs_0_), channel_id=1, source_target_pairs={{0,48},{16,32},{32,16},{48,0},{1,49},{17,33},{33,17},{49,1},{2,50}... | collective-permute-start | bytes 393224 | tf_op jit(solution)/shard_map/ppermute | solution.py:465
  40.7 9.1 %collective-permute-start.3 = (bf16[128,512]{1,0:T(8,128)(2,1)S(1)}, bf16[128,512]{1,0:T(8,128)(2,1)S(1)}, u32[]{:S(2)}, u32[]{:S(2)}) collective-permute-start(bf16[128,512]{1,0:T(8,128)(2,1)S(1)} %order_weight.1.refs_0_), channel_id=1, source_target_pairs={{0,32},{16,48},{32,0},{48,16},{1,33},{17,49},{33,1},{49,17},{2,34}... | collective-permute-start | bytes 393224 | tf_op jit(solution)/shard_map/ppermute | solution.py:465
  45.0 6.9 %collective-permute-start.2 = (bf16[128,512]{1,0:T(8,128)(2,1)S(1)}, bf16[128,512]{1,0:T(8,128)(2,1)S(1)}, u32[]{:S(2)}, u32[]{:S(2)}) collective-permute-start(bf16[128,512]{1,0:T(8,128)(2,1)S(1)} %order_weight.1.refs_0_), channel_id=1, source_target_pairs={{0,16},{16,0},{32,48},{48,32},{1,17},{17,1},{33,49},{49,33},{2,18}... | collective-permute-start | bytes 393224 | tf_op jit(solution)/shard_map/ppermute | solution.py:465
  52.0 4.1 %copy-start.2 = (bf16[512,512]{1,0:T(8,128)(2,1)}, bf16[512,512]{1,0:T(8,128)(2,1)S(1)}, u32[]{:S(2)}) copy-start(bf16[512,512]{1,0:T(8,128)(2,1)S(1)} %join.1) | copy-start | bytes 1572868
  52.0 4.1 %collective-permute-start.5 = (bf16[512,512]{1,0:T(8,128)(2,1)S(1)}, bf16[512,512]{1,0:T(8,128)(2,1)S(1)}, u32[]{:S(2)}, u32[]{:S(2)}) collective-permute-start(bf16[512,512]{1,0:T(8,128)(2,1)S(1)} %join.1), channel_id=1, source_target_pairs={{0,8},{8,0},{1,9},{9,1},{2,10},{10,2},{3,11},{11,3},{4,12},{12,4},... | collective-permute-start | bytes 1572872 | tf_op jit(solution)/shard_map/ppermute | solution.py:465
  55.2 1.1 copy-start.4
  56.0 0.8 copy-start.5
  68.4 8.8 %copy-start.3 = (bf16[512,512]{1,0:T(8,128)(2,1)S(1)}, bf16[512,512]{1,0:T(8,128)(2,1)}, u32[]{:S(2)}) copy-start(bf16[512,512]{1,0:T(8,128)(2,1)} %get-tuple-element.51.own_ref) | copy-start | bytes 1572868
  68.4 18.7 %copy-start = (bf16[1024,640]{1,0:T(8,128)(2,1)S(1)}, bf16[1024,640]{1,0:T(8,128)(2,1)}, u32[]{:S(2)}) copy-start(bf16[1024,640]{1,0:T(8,128)(2,1)} %get-tuple-element.47.dq_ref) | copy-start | bytes 3932164
  68.4 22.8 %all-to-all-start.2 = ((bf16[4,256,640]{2,1,0:T(8,128)(2,1)}), bf16[4,256,640]{2,1,0:T(8,128)(2,1)S(1)}, u32[]{:S(2)}, u32[]{:S(2)}) async-start(bf16[4,256,640]{2,1,0:T(8,128)(2,1)} %get-tuple-element.46), calls=%async_computation.2 | async-start | bytes 2621440 | tf_op jit(solution)/shard_map/all_to_all | solution.py:487
  73.0 14.1 %copy-start.1 = (bf16[8,128,512]{2,1,0:T(8,128)(2,1)S(1)}, bf16[8,128,512]{2,1,0:T(8,128)(2,1)}, u32[]{:S(2)}) copy-start(bf16[8,128,512]{2,1,0:T(8,128)(2,1)} %get-tuple-element.48.weight_ref) | copy-start | bytes 3145732
  73.0 4.1 %collective-permute-start.6 = (bf16[512,512]{1,0:T(8,128)(2,1)}, bf16[512,512]{1,0:T(8,128)(2,1)S(1)}, u32[]{:S(2)}, u32[]{:S(2)}) collective-permute-start(bf16[512,512]{1,0:T(8,128)(2,1)} %get-tuple-element.52), channel_id=1, source_target_pairs={{0,8},{8,0},{1,9},{9,1},{2,10},{10,2},{3,11},{11,3},{4,12},{12,4},... | collective-permute-start | bytes 1572872 | tf_op jit(solution)/shard_map/ppermute | solution.py:465
  77.3 12.1 %collective-permute-start.7 = (bf16[128,512]{1,0:T(8,128)(2,1)S(1)}, bf16[128,512]{1,0:T(8,128)(2,1)S(1)}, u32[]{:S(2)}, u32[]{:S(2)}) collective-permute-start(bf16[128,512]{1,0:T(8,128)(2,1)S(1)} %get-tuple-element.53), channel_id=1, source_target_pairs={{0,32},{16,48},{32,0},{48,16},{1,33},{17,49},{33,1},{49,17},{2,34}... | collective-permute-start | bytes 393224 | tf_op jit(solution)/shard_map/ppermute | solution.py:465
  80.3 9.1 %collective-permute-start.8 = (bf16[128,512]{1,0:T(8,128)(2,1)S(1)}, bf16[128,512]{1,0:T(8,128)(2,1)S(1)}, u32[]{:S(2)}, u32[]{:S(2)}) collective-permute-start(bf16[128,512]{1,0:T(8,128)(2,1)S(1)} %get-tuple-element.54), channel_id=1, source_target_pairs={{0,16},{16,0},{32,48},{48,32},{1,17},{17,1},{33,49},{49,33},{2,18}... | collective-permute-start | bytes 393224 | tf_op jit(solution)/shard_map/ppermute | solution.py:465
  83.1 8.1 %collective-permute-start.9 = (bf16[128,512]{1,0:T(8,128)(2,1)S(1)}, bf16[128,512]{1,0:T(8,128)(2,1)S(1)}, u32[]{:S(2)}, u32[]{:S(2)}) collective-permute-start(bf16[128,512]{1,0:T(8,128)(2,1)S(1)} %get-tuple-element.55), channel_id=1, source_target_pairs={{0,48},{16,32},{32,16},{48,0},{1,49},{17,33},{33,17},{49,1},{2,50}... | collective-permute-start | bytes 393224 | tf_op jit(solution)/shard_map/ppermute | solution.py:465
  110.2 13.0 %collective-permute-start.10 = (bf16[80,640]{1,0:T(8,128)(2,1)S(1)}, bf16[80,640]{1,0:T(8,128)(2,1)S(1)}, u32[]{:S(2)}, u32[]{:S(2)}) collective-permute-start(bf16[80,640]{1,0:T(8,128)(2,1)S(1)} %get-tuple-element.63.both_ref), channel_id=1, source_target_pairs={{0,256},{8,268},{64,320},{72,332},{128,384},{136,396},{192,448},{2... | collective-permute-start | bytes 307208 | tf_op jit(solution)/shard_map/ppermute | solution.py:478
  123.2 10.1 %collective-permute-start.11 = (bf16[48,640]{1,0:T(8,128)(2,1)S(1)}, bf16[48,640]{1,0:T(8,128)(2,1)S(1)}, u32[]{:S(2)}, u32[]{:S(2)}) collective-permute-start(bf16[48,640]{1,0:T(8,128)(2,1)S(1)} %get-tuple-element.65), channel_id=1, source_target_pairs={{0,260},{8,264},{64,324},{72,328},{128,388},{136,392},{192,452},{2... | collective-permute-start | bytes 184328 | tf_op jit(solution)/shard_map/ppermute | solution.py:478
